TPU v7x, 128 devices: a whole 4x4x4 slice. The times are simulated.
128 devices in a mesh: row: 8 (over z, y_hi), col: 16 (over y_lo, x, core).
Axes of the slice: x: 4, y: 4 (y_hi: 2, y_lo: 2; y = y_hi * 2 + y_lo), z: 4, core: 2. Of those that a mesh axis runs over, the one named last changes fastest.
Arguments:
- object_amplitude: float32 [2048, 4096], P('row', 'col'), may hold values from 0.3 to 3
- object_phase: float32 [2048, 4096], P('row', 'col'), may hold values from -3.140625 to 3.140625
- probe: float32 [4, 2, 256, 256], replicated, may hold values from -6 to 6
- amplitudes: float32 [1024, 256, 256], P(('row', 'col')), may hold values from 0.5 to 3
- positions: int32 [1024, 2], P(('row', 'col')), may hold values from -64 to 64
Outputs:
- new_object: float32 [2, 2048, 4096], P(None, 'row', 'col')
- new_probe: float32 [4, 2, 256, 256], replicated
Inputs may be any that keep to these rules, and one draw needn't show every extreme that they name: `positions`: row and column offsets of each frame's first pixel from the first pixel of its owner tile f // 8, tiles row-major; both ends of the range occur.
All inputs are finite; a program needn't handle non-finite values.
Results may differ from a plain program's by a relative error of at most 0.0014.
The roundings to bfloat16 on the way count: a program that leaves them out, or rounds other values in their place, can miss the bound.
Values sent between devices are 32-bit elements; how exact they have to be, the bound alone decides.
No kernel may reach another device: no remote copies, remote signals or barrier semaphores. Data moves between devices by JAX's collectives and lax.ppermute only.
A program may use at most 192 MiB of HBM per device.

v0:
```python
import math

import jax
import jax.numpy as jnp
from jax import lax
from jax.sharding import PartitionSpec as P

H = 64


def extended_2(block, sides, width):
    for axis, dim in sides:
        count = lax.axis_size(axis)
        forward = [(i, i + 1) for i in range(count - 1)]
        backward = [(target, source) for source, target in forward]
        low = lax.ppermute(
            lax.slice_in_dim(block, block.shape[dim] - width, None, axis=dim), axis, forward
        )
        high = lax.ppermute(lax.slice_in_dim(block, 0, width, axis=dim), axis, backward)
        block = jnp.concatenate([low, block, high], axis=dim)
    return block


def fourier_table(frame_side, exponent_sign):
    counter = jnp.arange(frame_side, dtype=jnp.int32)
    product = counter[:, None] * counter[None, :] % frame_side
    phase_angle = product.astype(jnp.float32) * (2.0 * math.pi / frame_side)
    norming = 1.0 / math.sqrt(frame_side)
    real_part = jnp.cos(phase_angle) * norming
    imaginary = exponent_sign * jnp.sin(phase_angle) * norming
    upper_rows = jnp.stack([real_part, -imaginary], axis=1)
    lower_rows = jnp.stack([imaginary, real_part], axis=1)
    return jnp.stack([upper_rows, lower_rows], axis=0).astype(jnp.bfloat16)


def transform(matrix, values):
    halfway = jnp.einsum("akcy,fmcyx->fmakx", matrix, values, preferred_element_type=jnp.float32)
    return jnp.einsum(
        "fmakx,blax->fmbkl",
        halfway.astype(jnp.bfloat16),
        matrix,
        preferred_element_type=jnp.float32,
    )


def frame_terms(patches, probe, measured, forward, inverse):
    object_real = patches[:, None, 0]
    object_imag = patches[:, None, 1]
    probe_real = probe[None, :, 0]
    probe_imag = probe[None, :, 1]
    exit_wave = jnp.stack(
        [
            probe_real * object_real - probe_imag * object_imag,
            probe_real * object_imag + probe_imag * object_real,
        ],
        axis=2,
    )
    spectrum = transform(forward, exit_wave.astype(jnp.bfloat16))
    intensity = jnp.sum(spectrum * spectrum, axis=(1, 2))
    factor = measured / jnp.maximum(jnp.sqrt(intensity), 1.0)
    corrected = (spectrum * factor[:, None, None]).astype(jnp.bfloat16)
    returned = transform(inverse, corrected)
    change = returned - exit_wave
    change_real = change[:, :, 0]
    change_imag = change[:, :, 1]
    object_gradient = jnp.stack(
        [
            jnp.sum(probe_real * change_real + probe_imag * change_imag, axis=1),
            jnp.sum(probe_real * change_imag - probe_imag * change_real, axis=1),
        ],
        axis=1,
    )
    probe_gradient = jnp.stack(
        [
            jnp.sum(object_real * change_real + object_imag * change_imag, axis=0),
            jnp.sum(object_real * change_imag - object_imag * change_real, axis=0),
        ],
        axis=1,
    )
    weight = jnp.sum(patches * patches, axis=(0, 1))
    return (object_gradient, probe_gradient, weight)


def shards(object_amplitude, object_phase, probe, amplitudes, positions):
    tile_side = object_amplitude.shape[0]
    frame_side = probe.shape[2]
    frame_count = amplitudes.shape[0]
    object_field = jnp.stack(
        [object_amplitude * jnp.cos(object_phase), object_amplitude * jnp.sin(object_phase)]
    )
    extended = extended_2(object_field, (("row", 1), ("col", 2)), H)
    starts = positions + H
    patches = jax.vmap(
        lambda start_pair: lax.dynamic_slice(
            extended, (jnp.int32(0), start_pair[0], start_pair[1]), (2, frame_side, frame_side)
        )
    )(starts)
    forward = fourier_table(frame_side, -1.0)
    inverse = fourier_table(frame_side, 1.0)
    object_gradient, probe_gradient, weight = frame_terms(
        patches, probe, amplitudes, forward, inverse
    )
    canvas_side = tile_side + 2 * H

    def place_frame(counter, canvas):
        corner = starts[counter]
        current = lax.dynamic_slice(
            canvas, (jnp.int32(0), corner[0], corner[1]), (2, frame_side, frame_side)
        )
        return lax.dynamic_update_slice(
            canvas, current + object_gradient[counter], (jnp.int32(0), corner[0], corner[1])
        )

    canvas = lax.fori_loop(
        0, frame_count, place_frame, jnp.zeros((2, canvas_side, canvas_side), jnp.float32)
    )
    row_edges = jnp.concatenate([canvas[:, :H], canvas[:, tile_side + H :]], axis=1)
    from_rows = extended_2(row_edges, (("row", 1),), H)
    canvas = canvas.at[:, H : 2 * H].add(from_rows[:, :H])
    canvas = canvas.at[:, tile_side : tile_side + H].add(from_rows[:, 3 * H :])
    middle = canvas[:, H : tile_side + H]
    col_edges = jnp.concatenate([middle[:, :, :H], middle[:, :, tile_side + H :]], axis=2)
    from_cols = extended_2(col_edges, (("col", 2),), H)
    inner = middle[:, :, H : tile_side + H]
    inner = inner.at[:, :, :H].add(from_cols[:, :, :H])
    inner = inner.at[:, :, tile_side - H :].add(from_cols[:, :, 3 * H :])
    step_size = 1.0 / (jnp.max(jnp.sum(probe * probe, axis=(0, 1))) + 1e-06)
    new_object = object_field + inner * step_size
    total_gradient, total_weight = lax.psum((probe_gradient, weight), ("row", "col"))
    new_probe = probe + total_gradient / (total_weight + 1e-05)
    return (new_object, new_probe)


def solution(mesh):
    in_specs = (
        P("row", "col"),
        P("row", "col"),
        P(),
        P(("row", "col"), None, None),
        P(("row", "col"), None),
    )
    out_specs = (P(None, "row", "col"), P())
    return jax.shard_map(shards, mesh=mesh, in_specs=in_specs, out_specs=out_specs, check_vma=False)
```

profile of v0, /device:TPU:1, one launch (start us, length us, event | category | flops | bytes accessed | tf_op | source)
XLA Modules:
  0.0 442.0 jit_solution(299347514883888756)
XLA Ops:
  7.2 1.9 multiply_bitcast_fusion.1
  9.9 5.6 %collective-permute-start = (f32[2,64,256]{2,1,0:T(8,128)}, f32[2,64,256]{2,1,0:T(8,128)S(1)}, u32[]{:S(2)}, u32[]{:S(2)}) collective-permute-start(f32[2,64,256]{2,1,0:T(8,128)} %get-tuple-element.196), channel_id=1, source_target_pairs={{0,16},{16,32},{32,48},{48,64},{64,80},{80,96},{96,112},{1,17},{17... | collective-permute-start | bytes 393224 | tf_op jit(solution)/shard_map/ppermute | solution.py:16
  18.7 2.7 slice_bitcast_fusion.5
  22.4 2.9 copy.52
  25.3 1.6 copy.46
  29.4 4.0 collective-permute-start.2
  33.4 2.1 collective-permute-start.3
  36.6 1.6 collective-permute-done.2
  38.1 4.4 collective-permute-done.3
  43.0 24.2 %while.19 = (s32[]{:T(128)}, f32[2,384,384]{2,1,0:T(8,128)S(1)}, s32[8,3]{0,1:T(4,128)S(1)}, f32[8,2,256,256]{3,2,1,0:T(8,128)}, s32[]{:T(128)}) while((s32[]{:T(128)}, f32[2,384,384]{2,1,0:T(8,128)S(1)}, s32[8,3]{0,1:T(4,128)S(1)}, f32[8,2,256,256]{3,2,1,0:T(8,128)}, s32[]{:T(128)}) %tuple.90), condition=%wide.while_cond.4, body=%wide.while_body.4.sunk | while | flops 2 | bytes 1049717 | solution.py:94
  43.7 2.4 bitcast_dynamic-update-slice_fusion.2
  46.7 2.4 bitcast_dynamic-update-slice_fusion.2
  49.8 2.4 bitcast_dynamic-update-slice_fusion.2
  52.8 2.3 bitcast_dynamic-update-slice_fusion.2
  55.8 2.4 bitcast_dynamic-update-slice_fusion.2
  58.8 2.3 bitcast_dynamic-update-slice_fusion.2
  61.8 2.3 bitcast_dynamic-update-slice_fusion.2
  64.9 2.3 bitcast_dynamic-update-slice_fusion.2
  67.2 4.7 %slice_bitcast_fusion.3 = (f32[8,256,256]{2,1,0:T(8,128)}, f32[8,256,256]{2,1,0:T(8,128)}) fusion(f32[8,2,256,256]{3,2,1,0:T(8,128)} %get-tuple-element.137), kind=kLoop, calls=%fused_computation.35 | loop fusion | bytes 8388608 | tf_op jit(solution)/shard_map/mul | solution.py:53
  71.9 1.9 copy.48
  73.8 2.9 copy.50
  76.7 8.3 %multiply_subtract_fusion = (f32[8,4,1,256,256]{3,4,2,1,0:T(8,128)}, f32[8,4,1,256,256]{3,4,2,1,0:T(8,128)}) fusion(f32[8,256,256]{1,2,0:T(8,128)} %copy.50, f32[4,256,256]{1,2,0:T(8,128)} %copy.49, f32[8,256,256]{1,2,0:T(8,128)S(1)} %copy.48, f32[4,256,256]{1,2,0:T(8,128)S(1)} %copy.46), kind=kLoop, calls=%fused_computation.27 | loop fusion | flops 12582912 | bytes 23068672 | tf_op jit(solution)/shard_map/sub | solution.py:53
  85.0 19.9 %fusion = (f32[8,256,256]{1,2,0:T(8,128)}, f32[2,256,8,4,256,1]{4,1,5,3,2,0:T(8,128)}) fusion(f32[8,4,1,256,256]{3,4,2,1,0:T(8,128)} %get-tuple-element.185, f32[8,4,1,256,256]{3,4,2,1,0:T(8,128)} %get-tuple-element.184, bf16[1,256,2,256]{3,1,2,0:T(8,128)(2,1)} %get-tuple-element.201, bf16[1,256,2,256]{3,1,2,0:T(8,128)(2,1)} %get-tuple-element.202), kind=kOutput, calls=%fused_computation.10 | convolution fusion | flops 8620867584 | bytes 36175872 | tf_op jit(solution)/shard_map/fmakx,blax->fmbkl/dot_general | solution.py:38
  104.9 4.2 maximum_divide_fusion
  109.1 22.3 %bitcast_subtract_fusion = f32[8,4,2,256,256]{3,4,2,1,0:T(8,128)} fusion(f32[8,4,1,256,256]{3,4,2,1,0:T(8,128)} %get-tuple-element.185, f32[8,4,1,256,256]{3,4,2,1,0:T(8,128)} %get-tuple-element.184, bf16[1,256,2,256]{3,1,2,0:T(8,128)(2,1)} %get-tuple-element.203, bf16[1,256,2,256]{3,1,2,0:T(8,128)(2,1)} %get-tuple-element.200, ...), kind=kOutput, calls=%fused_computation.6 | convolution fusion | flops 8613003264 | bytes 52953088 | tf_op jit(solution)/shard_map/fmakx,blax->fmbkl/dot_general | solution.py:38
  131.4 11.0 %add_reduce_fusion = (f32[4,256,256]{1,2,0:T(8,128)}, f32[4,256,256]{1,2,0:T(8,128)}, f32[8,256,256]{1,2,0:T(8,128)S(1)}, f32[8,256,256]{1,2,0:T(8,128)S(1)}) fusion(f32[8,4,2,256,256]{3,4,2,1,0:T(8,128)} %bitcast_subtract_fusion, f32[8,256,256]{1,2,0:T(8,128)} %copy.50, f32[8,256,256]{1,2,0:T(8,128)S(1)} %copy.48, f32[4,256,256]{1,2,0:T(8,128)} %copy.49, ...), kind=kLoop, calls=%fused_computation.23 | loop fusion | flops 31981568 | bytes 29360128 | tf_op jit(solution)/shard_map/reduce_sum | solution.py:75
  142.4 2.2 pad_maximum_fusion.1
  144.7 109.2 %while.18 = (s32[]{:T(128)}, f32[2,384,384]{2,1,0:T(8,128)S(1)}, s32[8,2]{0,1:T(2,128)S(1)}, f32[8,2,256,256]{2,3,0,1:T(8,128)}, s32[]{:T(128)}, /*index=5*/s32[]{:T(128)}, s32[]{:T(128)}) while((s32[]{:T(128)}, f32[2,384,384]{2,1,0:T(8,128)S(1)}, s32[8,2]{0,1:T(2,128)S(1)}, f32[8,2,256,256]{2,3,0,1:T(8,128)}, s32[]{:T(128)}, ...), condition=%wide.region_4.5_spmd, body=%wide.region_3.4_spmd.sunk | while | flops 131080 | bytes 4718797 | solution.py:114
  150.7 7.3 %dynamic_update_slice.8 = f32[2,384,384]{2,1,0:T(8,128)S(1)} dynamic-update-slice(f32[2,384,384]{2,1,0:T(8,128)S(1)} %get-tuple-element.293, f32[2,256,256]{2,1,0:T(8,128)S(1)} %bitcast_add_fusion.2, s32[]{:T(128)} %constant.166.clone.1..sunk, s32[]{:T(128)S(6)} %select_n.100, s32[]{:T(128)S(6)} %select_n.101) | dynamic-update-slice | bytes 1048580 | tf_op jit(solution)/shard_map/while/body/eval_jaxpr/dynamic_update_slice | solution.py:110
  164.1 8.0 %dynamic_update_slice.8 = f32[2,384,384]{2,1,0:T(8,128)S(1)} dynamic-update-slice(f32[2,384,384]{2,1,0:T(8,128)S(1)} %get-tuple-element.293, f32[2,256,256]{2,1,0:T(8,128)S(1)} %bitcast_add_fusion.2, s32[]{:T(128)} %constant.166.clone.1..sunk, s32[]{:T(128)S(6)} %select_n.100, s32[]{:T(128)S(6)} %select_n.101) | dynamic-update-slice | bytes 1048580 | tf_op jit(solution)/shard_map/while/body/eval_jaxpr/dynamic_update_slice | solution.py:110
  178.1 7.7 %dynamic_update_slice.8 = f32[2,384,384]{2,1,0:T(8,128)S(1)} dynamic-update-slice(f32[2,384,384]{2,1,0:T(8,128)S(1)} %get-tuple-element.293, f32[2,256,256]{2,1,0:T(8,128)S(1)} %bitcast_add_fusion.2, s32[]{:T(128)} %constant.166.clone.1..sunk, s32[]{:T(128)S(6)} %select_n.100, s32[]{:T(128)S(6)} %select_n.101) | dynamic-update-slice | bytes 1048580 | tf_op jit(solution)/shard_map/while/body/eval_jaxpr/dynamic_update_slice | solution.py:110
  191.8 7.1 %dynamic_update_slice.8 = f32[2,384,384]{2,1,0:T(8,128)S(1)} dynamic-update-slice(f32[2,384,384]{2,1,0:T(8,128)S(1)} %get-tuple-element.293, f32[2,256,256]{2,1,0:T(8,128)S(1)} %bitcast_add_fusion.2, s32[]{:T(128)} %constant.166.clone.1..sunk, s32[]{:T(128)S(6)} %select_n.100, s32[]{:T(128)S(6)} %select_n.101) | dynamic-update-slice | bytes 1048580 | tf_op jit(solution)/shard_map/while/body/eval_jaxpr/dynamic_update_slice | solution.py:110
  204.9 7.4 %dynamic_update_slice.8 = f32[2,384,384]{2,1,0:T(8,128)S(1)} dynamic-update-slice(f32[2,384,384]{2,1,0:T(8,128)S(1)} %get-tuple-element.293, f32[2,256,256]{2,1,0:T(8,128)S(1)} %bitcast_add_fusion.2, s32[]{:T(128)} %constant.166.clone.1..sunk, s32[]{:T(128)S(6)} %select_n.100, s32[]{:T(128)S(6)} %select_n.101) | dynamic-update-slice | bytes 1048580 | tf_op jit(solution)/shard_map/while/body/eval_jaxpr/dynamic_update_slice | solution.py:110
  218.4 8.0 %dynamic_update_slice.8 = f32[2,384,384]{2,1,0:T(8,128)S(1)} dynamic-update-slice(f32[2,384,384]{2,1,0:T(8,128)S(1)} %get-tuple-element.293, f32[2,256,256]{2,1,0:T(8,128)S(1)} %bitcast_add_fusion.2, s32[]{:T(128)} %constant.166.clone.1..sunk, s32[]{:T(128)S(6)} %select_n.100, s32[]{:T(128)S(6)} %select_n.101) | dynamic-update-slice | bytes 1048580 | tf_op jit(solution)/shard_map/while/body/eval_jaxpr/dynamic_update_slice | solution.py:110
  232.4 7.5 %dynamic_update_slice.8 = f32[2,384,384]{2,1,0:T(8,128)S(1)} dynamic-update-slice(f32[2,384,384]{2,1,0:T(8,128)S(1)} %get-tuple-element.293, f32[2,256,256]{2,1,0:T(8,128)S(1)} %bitcast_add_fusion.2, s32[]{:T(128)} %constant.166.clone.1..sunk, s32[]{:T(128)S(6)} %select_n.100, s32[]{:T(128)S(6)} %select_n.101) | dynamic-update-slice | bytes 1048580 | tf_op jit(solution)/shard_map/while/body/eval_jaxpr/dynamic_update_slice | solution.py:110
  245.9 8.0 %dynamic_update_slice.8 = f32[2,384,384]{2,1,0:T(8,128)S(1)} dynamic-update-slice(f32[2,384,384]{2,1,0:T(8,128)S(1)} %get-tuple-element.293, f32[2,256,256]{2,1,0:T(8,128)S(1)} %bitcast_add_fusion.2, s32[]{:T(128)} %constant.166.clone.1..sunk, s32[]{:T(128)S(6)} %select_n.100, s32[]{:T(128)S(6)} %select_n.101) | dynamic-update-slice | bytes 1048580 | tf_op jit(solution)/shard_map/while/body/eval_jaxpr/dynamic_update_slice | solution.py:110
  254.0 5.3 %collective-permute-start.4 = (f32[2,64,384]{2,1,0:T(8,128)S(1)}, f32[2,64,384]{2,1,0:T(8,128)S(1)}, u32[]{:S(2)}, u32[]{:S(2)}) collective-permute-start(f32[2,64,384]{2,1,0:T(8,128)S(1)} %slice.183), channel_id=1, source_target_pairs={{0,16},{16,32},{32,48},{48,64},{64,80},{80,96},{96,112},{1,17},{17... | collective-permute-start | bytes 589832 | tf_op jit(solution)/shard_map/ppermute | solution.py:16
  259.2 2.9 copy.61
  264.2 3.2 multiply_reduce_fusion
  267.4 3.2 pad_maximum_fusion.2
  273.1 6.2 %collective-permute-start.6 = (f32[2,256,64]{2,1,0:T(8,128)}, f32[2,256,64]{2,1,0:T(8,128)}, u32[]{:S(2)}, u32[]{:S(2)}) collective-permute-start(f32[2,256,64]{2,1,0:T(8,128)} %get-tuple-element.191), channel_id=1, source_target_pairs={{0,1},{1,2},{2,3},{3,4},{4,5},{5,6},{6,7},{7,8},{8,9},{9,10},{10,1... | collective-permute-start | bytes 393224 | tf_op jit(solution)/shard_map/ppermute | solution.py:16
  280.1 1.7 reduce_max.9
  282.8 1.9 collective-permute-start.7
  286.9 4.3 collective-permute-done.7
  292.6 1.8 fusion.18
  294.4 135.2 %all-reduce.3.cloned.1.call-done = (f32[4,2,256,256]{2,3,0,1:T(8,128)}, f32[256,256]{1,0:T(8,128)}) async-done(((f32[4,2,256,256]{2,3,0,1:T(8,128)}, f32[256,256]{1,0:T(8,128)}), (f32[4,2,256,256]{2,3,0,1:T(8,128)}, f32[256,256]{1,0:T(8,128)})) %all-reduce.3.cloned.1.call-update) | async-done | bytes 2359312 | tf_op jit(solution)/shard_map/psum | solution.py:129
  430.7 2.6 divide_add_fusion
  433.3 1.8 copy.62
  (96 shorter events, 41.4 us)
Async XLA Ops:
  7.2 422.4 %all-reduce.3.cloned.1.call-start = ((), (), s32[]{:S(2)}) async-start(), calls=%async_computation | async-start | bytes 4718592 | tf_op jit(solution)/shard_map/psum | solution.py:129
  9.2 33.3 %copy-start.1 = (f32[1,256,256]{2,1,0:T(8,128)}, f32[1,256,256]{2,1,0:T(8,128)S(1)}, u32[]{:S(2)}) copy-start(f32[1,256,256]{2,1,0:T(8,128)S(1)} %get-tuple-element.199) | copy-start | bytes 786436
  9.9 19.3 %collective-permute-start = (f32[2,64,256]{2,1,0:T(8,128)}, f32[2,64,256]{2,1,0:T(8,128)S(1)}, u32[]{:S(2)}, u32[]{:S(2)}) collective-permute-start(f32[2,64,256]{2,1,0:T(8,128)} %get-tuple-element.196), channel_id=1, source_target_pairs={{0,16},{16,32},{32,48},{48,64},{64,80},{80,96},{96,112},{1,17},{17... | collective-permute-start | bytes 393224 | tf_op jit(solution)/shard_map/ppermute | solution.py:16
  15.6 13.6 %collective-permute-start.1 = (f32[2,64,256]{2,1,0:T(8,128)}, f32[2,64,256]{2,1,0:T(8,128)S(1)}, u32[]{:S(2)}, u32[]{:S(2)}) collective-permute-start(f32[2,64,256]{2,1,0:T(8,128)} %get-tuple-element.197), channel_id=1, source_target_pairs={{16,0},{32,16},{48,32},{64,48},{80,64},{96,80},{112,96},{17,1},{33... | collective-permute-start | bytes 393224 | tf_op jit(solution)/shard_map/ppermute | solution.py:19
  29.4 8.7 %collective-permute-start.2 = (f32[2,384,64]{2,1,0:T(8,128)S(1)}, f32[2,384,64]{2,1,0:T(8,128)S(1)}, u32[]{:S(2)}, u32[]{:S(2)}) collective-permute-start(f32[2,384,64]{2,1,0:T(8,128)S(1)} %get-tuple-element.194), channel_id=1, source_target_pairs={{0,1},{1,2},{2,3},{3,4},{4,5},{5,6},{6,7},{7,8},{8,9},{9,10},{10,1... | collective-permute-start | bytes 589832 | tf_op jit(solution)/shard_map/ppermute | solution.py:16
  33.4 9.1 %collective-permute-start.3 = (f32[2,384,64]{2,1,0:T(8,128)S(1)}, f32[2,384,64]{2,1,0:T(8,128)S(1)}, u32[]{:S(2)}, u32[]{:S(2)}) collective-permute-start(f32[2,384,64]{2,1,0:T(8,128)S(1)} %get-tuple-element.195), channel_id=1, source_target_pairs={{1,0},{2,1},{3,2},{4,3},{5,4},{6,5},{7,6},{8,7},{9,8},{10,9},{11,1... | collective-permute-start | bytes 589832 | tf_op jit(solution)/shard_map/ppermute | solution.py:19
  254.0 8.2 %collective-permute-start.4 = (f32[2,64,384]{2,1,0:T(8,128)S(1)}, f32[2,64,384]{2,1,0:T(8,128)S(1)}, u32[]{:S(2)}, u32[]{:S(2)}) collective-permute-start(f32[2,64,384]{2,1,0:T(8,128)S(1)} %slice.183), channel_id=1, source_target_pairs={{0,16},{16,32},{32,48},{48,64},{64,80},{80,96},{96,112},{1,17},{17... | collective-permute-start | bytes 589832 | tf_op jit(solution)/shard_map/ppermute | solution.py:16
  262.9 8.4 %collective-permute-start.5 = (f32[2,64,384]{2,1,0:T(8,128)}, f32[2,64,384]{2,1,0:T(8,128)}, u32[]{:S(2)}, u32[]{:S(2)}) collective-permute-start(f32[2,64,384]{2,1,0:T(8,128)} %get-tuple-element.192), channel_id=1, source_target_pairs={{16,0},{32,16},{48,32},{64,48},{80,64},{96,80},{112,96},{17,1},{33... | collective-permute-start | bytes 589832 | tf_op jit(solution)/shard_map/ppermute | solution.py:19
  267.4 11.9 %copy-start = (f32[4,2,256,256]{3,2,1,0:T(8,128)S(1)}, f32[4,2,256,256]{3,2,1,0:T(8,128)}, u32[]{:S(2)}) copy-start(f32[4,2,256,256]{3,2,1,0:T(8,128)} %param.17) | copy-start | bytes 6291460
  273.1 11.6 %collective-permute-start.6 = (f32[2,256,64]{2,1,0:T(8,128)}, f32[2,256,64]{2,1,0:T(8,128)}, u32[]{:S(2)}, u32[]{:S(2)}) collective-permute-start(f32[2,256,64]{2,1,0:T(8,128)} %get-tuple-element.191), channel_id=1, source_target_pairs={{0,1},{1,2},{2,3},{3,4},{4,5},{5,6},{6,7},{7,8},{8,9},{9,10},{10,1... | collective-permute-start | bytes 393224 | tf_op jit(solution)/shard_map/ppermute | solution.py:16
  282.8 8.4 %collective-permute-start.7 = (f32[2,256,64]{2,1,0:T(8,128)}, f32[2,256,64]{2,1,0:T(8,128)S(1)}, u32[]{:S(2)}, u32[]{:S(2)}) collective-permute-start(f32[2,256,64]{2,1,0:T(8,128)} %get-tuple-element.190), channel_id=1, source_target_pairs={{1,0},{2,1},{3,2},{4,3},{5,4},{6,5},{7,6},{8,7},{9,8},{10,9},{11,1... | collective-permute-start | bytes 393224 | tf_op jit(solution)/shard_map/ppermute | solution.py:19
Sparse Core Ops, SparseCore 0:
  270.7 158.8 all-reduce.2
where the time goes:
time: 444 us; the launch traced here: 442 us
  waiting for transfers between devices  146 us (33%)
  local copies, waits for them, and re-layouts  127 us (29%)
  other arithmetic  52.8 us (12%)
  matrix products  42.2 us (10%)
  loops' own time  31.4 us (7%)
  starting transfers between devices  27.7 us (6%)
  between operations  15 us (3%)
    psum x1, waiting for transfers between devices, shards(): lax.psum((probe_gradient, weight), ('row', 'col'))  135 us
    dynamic_update_slice x8, local copies, waits for them, and re-layouts, place_frame(): lax.dynamic_update_slice(canvas, current + object_gradient[counter], (jnp...  61.1 us
    dot_general x2, matrix products, transform(): jnp.einsum('fmakx,blax->fmbkl', halfway.astype(jnp.bfloat16), matrix, pre...  42.2 us
    another operation x1, loops' own time, shards(): lax.fori_loop(0, frame_count, place_frame, jnp.zeros((2, canvas_side, can...  31.4 us
    gather x24, local copies, waits for them, and re-layouts  24.2 us
    ppermute x4, starting transfers between devices, extended_2(): lax.ppermute(lax.slice_in_dim(block, block.shape[dim] - width, None, axis...  21.1 us
    reduce_sum x1, other arithmetic, frame_terms(): jnp.sum(object_real * change_real + object_imag * change_imag, axis=0)  11 us
    dynamic_slice x16, local copies, waits for them, and re-layouts, place_frame(): object_gradient[counter]  10.3 us
  transfers between devices with their start and end apart: 9, of which 5 were waited for; matrix products, arithmetic and copies ran while one was open for 7% of the time, Pallas kernels for 0%

commit v1 on v0

v1 whole, which is shorter than its diff:
```python
import functools
import math

import jax
import jax.numpy as jnp
import numpy as np
from jax import lax
from jax.experimental import pallas as pl
from jax.experimental.pallas import tpu as pltpu
from jax.sharding import Mesh, PartitionSpec as P

H = 64
ROW = ("z", "yh")
COL = ("yl", "x", "c")
CHIPS = ("z", "yh", "yl", "x")
ALL = CHIPS + ("c",)
CHUNK = 16


def fourier_matrix(side):
    counter = np.arange(side, dtype=np.int64)
    angle = (counter[:, None] * counter[None, :] % side).astype(np.float64) * (2.0 * math.pi / side)
    norming = 1.0 / math.sqrt(side)
    real = np.cos(angle) * norming
    imag = -np.sin(angle) * norming
    whole = np.concatenate(
        [np.concatenate([real, -imag], axis=1), np.concatenate([imag, real], axis=1)], axis=0
    )
    return whole.astype(np.float32)


def placed(part, slide, shift, wide):
    rows, side = part.shape
    tall = jnp.concatenate([part, jnp.zeros((8, side), jnp.float32)], axis=0)
    tall = pltpu.roll(tall, slide, 0)
    tall = jnp.concatenate([tall, jnp.zeros((rows + 8, wide - side), jnp.float32)], axis=1)
    return pltpu.roll(tall, shift, 1)


def frames_kernel(
    starts_ref,
    step_ref,
    ext_ref,
    probe_ref,
    power_ref,
    amps_ref,
    fwd_ref,
    inv_ref,
    sums_ref,
    canvas_ref,
    field,
    patch,
    psib,
    half,
    spec,
    corr,
    canvas,
    total,
):
    f = pl.program_id(0)
    count = pl.num_programs(0)
    modes = probe_ref.shape[0] // 2
    side = probe_ref.shape[1]
    wide = ext_ref.shape[2]

    @pl.when(f == 0)
    def _():
        @pl.loop(0, wide // CHUNK)
        def _(i):
            rows = pl.ds(pl.multiple_of(i * CHUNK, CHUNK), CHUNK)
            amp = ext_ref[0, rows, :]
            phase = ext_ref[1, rows, :]
            field[0, rows, :] = amp * jnp.cos(phase)
            field[1, rows, :] = amp * jnp.sin(phase)
            canvas[0, rows, :] = jnp.zeros((CHUNK, wide), jnp.float32)
            canvas[1, rows, :] = jnp.zeros((CHUNK, wide), jnp.float32)

        for k in range(2):
            field[k, wide:, :] = jnp.zeros((8, wide), jnp.float32)
            canvas[k, wide:, :] = jnp.zeros((8, wide), jnp.float32)

        @pl.loop(0, side // CHUNK)
        def _(i):
            rows = pl.ds(pl.multiple_of(i * CHUNK, CHUNK), CHUNK)
            for p in range(2 * modes + 1):
                total[p, rows, :] = jnp.zeros((CHUNK, side), jnp.float32)

    r0 = starts_ref[2 * f] + H
    slide = lax.rem(r0, 8)
    base = pl.multiple_of(r0 - slide, 8)
    lift = lax.rem(CHUNK + 8 - slide, CHUNK + 8)
    c0 = starts_ref[2 * f + 1]
    back_shift = jnp.where(c0 > 0, wide - c0, -c0)
    fore_shift = jnp.where(c0 < 0, wide + c0, c0)

    for i in range(side // CHUNK):
        rows = slice(i * CHUNK, (i + 1) * CHUNK)
        o = [
            pltpu.roll(
                pltpu.roll(field[k, pl.ds(base + i * CHUNK, CHUNK + 8), :], back_shift, 1)[:, :side],
                lift,
                0,
            )[:CHUNK]
            for k in range(2)
        ]
        patch[0, rows, :] = o[0]
        patch[1, rows, :] = o[1]
        total[2 * modes, rows, :] += o[0] * o[0] + o[1] * o[1]
        for m in range(modes):
            pr = probe_ref[2 * m, rows, :]
            pi = probe_ref[2 * m + 1, rows, :]
            cols = slice(m * side, (m + 1) * side)
            psib[rows, cols] = (pr * o[0] - pi * o[1]).astype(jnp.bfloat16)
            psib[side + i * CHUNK : side + (i + 1) * CHUNK, cols] = (
                pr * o[1] + pi * o[0]
            ).astype(jnp.bfloat16)

    for m in range(modes):
        cols = slice(m * side, (m + 1) * side)
        h = jnp.dot(fwd_ref[...], psib[:, cols], preferred_element_type=jnp.float32)
        half[cols, :side] = h[:side].astype(jnp.bfloat16)
        half[cols, side:] = h[side:].astype(jnp.bfloat16)
    for m in range(modes):
        rows = slice(m * side, (m + 1) * side)
        spec[rows, :] = jnp.dot(half[rows, :], inv_ref[...], preferred_element_type=jnp.float32)
    for i in range(side // CHUNK):
        rows = slice(i * CHUNK, (i + 1) * CHUNK)
        parts = []
        energy = None
        for m in range(modes):
            row_m = slice(m * side + i * CHUNK, m * side + (i + 1) * CHUNK)
            a = spec[row_m, :side]
            b = spec[row_m, side:]
            e = a * a + b * b
            energy = e if energy is None else energy + e
            parts.append((a, b))
        fac = amps_ref[0, rows, :] * lax.rsqrt(jnp.maximum(energy, 1.0))
        for m in range(modes):
            cols = slice(m * side, (m + 1) * side)
            corr[rows, cols] = (parts[m][0] * fac).astype(jnp.bfloat16)
            corr[side + i * CHUNK : side + (i + 1) * CHUNK, cols] = (parts[m][1] * fac).astype(
                jnp.bfloat16
            )
    for m in range(modes):
        cols = slice(m * side, (m + 1) * side)
        h = jnp.dot(inv_ref[...], corr[:, cols], preferred_element_type=jnp.float32)
        half[cols, :side] = h[:side].astype(jnp.bfloat16)
        half[cols, side:] = h[side:].astype(jnp.bfloat16)
    for m in range(modes):
        rows = slice(m * side, (m + 1) * side)
        spec[rows, :] = jnp.dot(half[rows, :], fwd_ref[...], preferred_element_type=jnp.float32)
    for i in range(side // CHUNK):
        rows = slice(i * CHUNK, (i + 1) * CHUNK)
        o_r = patch[0, rows, :]
        o_i = patch[1, rows, :]
        power = power_ref[rows, :]
        g_r = -(o_r * power)
        g_i = -(o_i * power)
        for m in range(modes):
            row_m = slice(m * side + i * CHUNK, m * side + (i + 1) * CHUNK)
            a = spec[row_m, :side]
            b = spec[row_m, side:]
            pr = probe_ref[2 * m, rows, :]
            pi = probe_ref[2 * m + 1, rows, :]
            g_r += pr * a + pi * b
            g_i += pr * b - pi * a
            total[2 * m, rows, :] += o_r * a + o_i * b
            total[2 * m + 1, rows, :] += o_r * b - o_i * a
        here = pl.ds(base + i * CHUNK, CHUNK + 8)
        canvas[0, here, :] += placed(g_r, slide, fore_shift, wide)
        canvas[1, here, :] += placed(g_i, slide, fore_shift, wide)

    @pl.when(f == count - 1)
    def _():
        step = step_ref[0]

        @pl.loop(0, wide // CHUNK)
        def _(i):
            rows = pl.ds(pl.multiple_of(i * CHUNK, CHUNK), CHUNK)
            inside = jnp.logical_and(i * CHUNK >= H, i * CHUNK < H + side).astype(jnp.float32)
            for k in range(2):
                canvas_ref[k, rows, :side] = (
                    step * canvas[k, rows, :side] + inside * field[k, rows, :side]
                )
                canvas_ref[k, rows, side:] = step * canvas[k, rows, side:]

        planes = modes

        @pl.loop(0, side // 8)
        def _(i):
            rows = pl.ds(pl.multiple_of(i * 8, 8), 8)
            for j in range(side // 128):
                lanes = slice(j * 128, (j + 1) * 128)
                tile = i * (side // 128) + j
                for owner in range(2):
                    for p in range(planes):
                        sums_ref[owner, tile, p] = total[owner * planes + p, rows, lanes]
                    sums_ref[owner, tile, planes] = total[2 * modes, rows, lanes]


def frames(starts, step, ext, probe, power, amps, fwd, inv):
    count, side, _ = amps.shape
    planes = probe.shape[0]
    modes = planes // 2
    wide = ext.shape[2]
    tiles = (side // 8) * (side // 128)

    def whole(shape):
        return pl.BlockSpec(shape, lambda f, *_: (0,) * len(shape))

    return pl.pallas_call(
        frames_kernel,
        out_shape=(
            jax.ShapeDtypeStruct((2, tiles, planes // 2 + 1, 8, 128), jnp.float32),
            jax.ShapeDtypeStruct((2, wide, wide), jnp.float32),
        ),
        grid_spec=pltpu.PrefetchScalarGridSpec(
            num_scalar_prefetch=2,
            grid=(count,),
            in_specs=[
                whole((2, wide, wide)),
                whole((planes, side, side)),
                whole((side, side)),
                pl.BlockSpec((1, side, side), lambda f, *_: (f, 0, 0)),
                whole((2 * side, 2 * side)),
                whole((2 * side, 2 * side)),
            ],
            out_specs=(
                whole((2, tiles, planes // 2 + 1, 8, 128)),
                whole((2, wide, wide)),
            ),
            scratch_shapes=[
                pltpu.VMEM((2, wide + 8, wide), jnp.float32),
                pltpu.VMEM((2, side, side), jnp.float32),
                pltpu.VMEM((2 * side, modes * side), jnp.bfloat16),
                pltpu.VMEM((modes * side, 2 * side), jnp.bfloat16),
                pltpu.VMEM((modes * side, 2 * side), jnp.float32),
                pltpu.VMEM((2 * side, modes * side), jnp.bfloat16),
                pltpu.VMEM((2, wide + 8, wide), jnp.float32),
                pltpu.VMEM((planes + 1, side, side), jnp.float32),
            ],
        ),
        compiler_params=pltpu.CompilerParams(vmem_limit_bytes=48 * 1024 * 1024),
        cost_estimate=pl.CostEstimate(
            flops=count * modes * 4 * 8 * side**3, bytes_accessed=8 * 2**20, transcendentals=0
        ),
    )(starts, step, ext, probe, power, amps, fwd, inv)


def send(block, axes, shift):
    count = math.prod(lax.axis_size(a) for a in axes)
    return lax.ppermute(
        block, axes, [(i, i + shift) for i in range(count) if 0 <= i + shift < count]
    )


def shards(object_amplitude, object_phase, probe, amplitudes, positions):
    tile = object_amplitude.shape[0]
    side = probe.shape[2]
    own = jnp.stack([object_amplitude, object_phase])
    top = send(own[:, tile - H :], ROW, 1)
    bottom = send(own[:, :H], ROW, -1)
    tall = jnp.concatenate([top, own, bottom], axis=1)
    left = send(tall[:, :, tile - H :], COL, 1)
    right = send(tall[:, :, :H], COL, -1)
    ext = jnp.concatenate([tall, right, left], axis=2)

    power = jnp.sum(probe * probe, axis=(0, 1))
    step = 1.0 / (jnp.max(power) + 1e-06)
    table = fourier_matrix(side)
    planes = probe.reshape((-1, side, side))
    sums, canvas = frames(
        positions.reshape((-1,)),
        step.reshape((1,)),
        ext,
        planes,
        power,
        amplitudes,
        jnp.asarray(table, dtype=jnp.bfloat16),
        jnp.asarray(table.T, dtype=jnp.bfloat16),
    )

    core = lax.axis_index("c")
    mine = planes.shape[0] // 2
    other = lax.dynamic_index_in_dim(sums, 1 - core, 0, keepdims=False)
    kept = lax.dynamic_index_in_dim(sums, core, 0, keepdims=False)
    from_above = send(canvas[:, H + tile :, :], ROW, 1)
    from_below = send(canvas[:, :H, :], ROW, -1)
    both = kept + lax.ppermute(other, "c", [(0, 1), (1, 0)])
    spread = lax.all_to_all(both, CHIPS, 0, 0, tiled=True)
    summed = jnp.sum(spread, axis=0)
    chip = lax.axis_index(CHIPS)
    lanes = side // 128
    old = lax.dynamic_slice(
        planes, (core * mine, chip // lanes * 8, chip % lanes * 128), (mine, 8, 128)
    )
    weight = summed[mine]
    new = old + (summed[:mine] - old * weight) / (weight + 1e-05)
    centre = canvas[:, H : H + tile, :]
    centre = centre.at[:, :H].add(from_above)
    centre = centre.at[:, tile - H :].add(from_below)
    from_left = send(centre[:, :, tile : tile + H], COL, 1)
    from_right = send(centre[:, :, tile + H :], COL, -1)
    gathered = lax.all_to_all(
        jnp.broadcast_to(new[None], both.shape[:1] + new.shape), CHIPS, 0, 0, tiled=True
    )
    swapped = lax.ppermute(gathered, "c", [(0, 1), (1, 0)])
    first = jnp.where(core == 0, gathered, swapped)
    second = jnp.where(core == 0, swapped, gathered)
    pair = jnp.stack([first, second])
    pair = pair.reshape((2, side // 8, lanes, mine, 8, 128)).transpose((0, 3, 1, 4, 2, 5))
    new_probe = pair.reshape(probe.shape)
    inner = centre[:, :, :tile]
    inner = inner.at[:, :, :H].add(from_left)
    inner = inner.at[:, :, tile - H :].add(from_right)
    return (inner, new_probe)


def solution(mesh):
    fine = Mesh(mesh.devices.reshape((4, 2, 2, 4, 2)), ALL)
    in_specs = (
        P(ROW, COL),
        P(ROW, COL),
        P(),
        P(ALL, None, None),
        P(ALL, None),
    )
    out_specs = (P(None, ROW, COL), P())
    return jax.shard_map(shards, mesh=fine, in_specs=in_specs, out_specs=out_specs, check_vma=False)
```

time: 444 us -> 156 us (0.35)
  local copies, waits for them, and re-layouts: 127 us -> 8.73 us
  waiting for transfers between devices: 146 us -> 50.5 us
  matrix products: 42.2 us -> 0 us
  other arithmetic: 52.8 us -> 10.6 us
  Pallas kernels: 0 us -> 35 us
  loops' own time: 31.4 us -> 0 us
  starting transfers between devices: 27.7 us -> 48.5 us
  between operations: 15 us -> 1.65 us
    psum x1 -> x0, waiting for transfers between devices: 135 us -> none  [shards(): lax.psum((probe_gradient, weight), ('row', 'col'))]
    dynamic_update_slice x8 -> x0, local copies, waits for them, and re-layouts: 61.1 us -> none  [place_frame(): lax.dynamic_update_slice(canvas, current + object_gradient[counter], (jnp...]
    dot_general x2 -> x0, matrix products: 42.2 us -> none  [transform(): jnp.einsum('fmakx,blax->fmbkl', halfway.astype(jnp.bfloat16), matrix, pre...]
    pallas_call x0 -> x1, Pallas kernels: none -> 35 us  [frames(): pl.pallas_call(frames_kernel, out_shape=(jax.ShapeDtypeStruct((2, tiles,...]
    another operation x2 -> x0, loops' own time: 31.4 us -> none  [the longest x1 31.4 us: shards(): lax.fori_loop(0, frame_count, place_frame, jnp.zeros((2, canvas_side, can...]
    gather x24 -> x0, local copies, waits for them, and re-layouts: 24.2 us -> none
    all_to_all x0 -> x2, waiting for transfers between devices: none -> 22.7 us  [the longest x1 20.9 us: shards(): spread = lax.all_to_all(both, CHIPS, 0, 0, tiled=True)]
    all_to_all x0 -> x2, starting transfers between devices: none -> 19.7 us  [the longest x1 14.5 us: shards(): spread = lax.all_to_all(both, CHIPS, 0, 0, tiled=True)]
  transfers between devices with their start and end apart: 9 -> 12, of which waited for: 5 -> 11; matrix products, arithmetic and copies ran while one was open for 7% -> 2% of each run, Pallas kernels for 0% -> 0%
where the time goes in v1:
time: 156 us; the launch traced here: 155 us
  waiting for transfers between devices  50.5 us (32%)
  starting transfers between devices  48.5 us (31%)
  Pallas kernels  35 us (22%)
  other arithmetic  10.6 us (7%)
  local copies, waits for them, and re-layouts  8.73 us (6%)
  between operations  1.65 us (1%)
    pallas_call x1, Pallas kernels, frames(): pl.pallas_call(frames_kernel, out_shape=(jax.ShapeDtypeStruct((2, tiles,...  35 us
    ppermute x8, starting transfers between devices, send(): lax.ppermute(block, axes, [(i, i + shift) for i in range(count) if 0 <= i...  26 us
    ppermute x8, waiting for transfers between devices, send(): lax.ppermute(block, axes, [(i, i + shift) for i in range(count) if 0 <= i...  24.4 us
    all_to_all x1, waiting for transfers between devices, shards(): spread = lax.all_to_all(both, CHIPS, 0, 0, tiled=True)  20.9 us
    all_to_all x1, starting transfers between devices, shards(): spread = lax.all_to_all(both, CHIPS, 0, 0, tiled=True)  14.5 us
    all_to_all x1, starting transfers between devices, shards(): lax.all_to_all(jnp.broadcast_to(new[None], both.shape[:1] + new.shape), C...  5.23 us
    ppermute x1, waiting for transfers between devices, shards(): both = kept + lax.ppermute(other, 'c', [(0, 1), (1, 0)])  3.37 us
  transfers between devices with their start and end apart: 12, of which 11 were waited for; matrix products, arithmetic and copies ran while one was open for 2% of the time, Pallas kernels for 0%

profile of v1, /device:TPU:1, one launch (start us, length us, event | category | flops | bytes accessed | tf_op | source)
XLA Modules:
  0.0 155.0 jit_solution(16134880476688896557)
XLA Ops:
  0.6 1.0 pad_maximum_fusion.3
  1.6 1.3 collective-permute-start.1
  2.9 0.0 copy-start.6
  2.9 0.0 copy-start
  2.9 6.4 %collective-permute-start = (f32[2,64,256]{2,1,0:T(8,128)S(1)}, f32[2,64,256]{2,1,0:T(8,128)S(1)}, u32[]{:S(2)}, u32[]{:S(2)}) collective-permute-start(f32[2,64,256]{2,1,0:T(8,128)S(1)} %get-tuple-element.62), channel_id=1, source_target_pairs={{0,16},{16,32},{32,48},{48,64},{64,80},{80,96},{96,112},{1,17},{17... | collective-permute-start | bytes 393224 | tf_op jit(solution)/shard_map/ppermute | solution.py:252
  9.3 0.8 collective-permute-done.1
  10.2 1.1 collective-permute-done
  11.3 1.1 pad_maximum_fusion.1
  12.3 0.9 fusion.5
  13.3 4.8 %collective-permute-start.3 = (f32[2,384,64]{2,1,0:T(8,128)}, f32[2,384,64]{2,1,0:T(8,128)}, u32[]{:S(2)}, u32[]{:S(2)}) collective-permute-start(f32[2,384,64]{2,1,0:T(8,128)} %get-tuple-element.61), channel_id=1, source_target_pairs={{0,1},{1,2},{2,3},{3,4},{4,5},{5,6},{6,7},{7,8},{8,9},{9,10},{10,1... | collective-permute-start | bytes 589832 | tf_op jit(solution)/shard_map/ppermute | solution.py:252
  18.1 1.9 %collective-permute-start.2 = (f32[2,384,64]{2,1,0:T(8,128)S(1)}, f32[2,384,64]{2,1,0:T(8,128)}, u32[]{:S(2)}, u32[]{:S(2)}) collective-permute-start(f32[2,384,64]{2,1,0:T(8,128)S(1)} %get-tuple-element.60), channel_id=1, source_target_pairs={{1,0},{2,1},{3,2},{4,3},{5,4},{6,5},{7,6},{8,7},{9,8},{10,9},{11,1... | collective-permute-start | bytes 589832 | tf_op jit(solution)/shard_map/ppermute | solution.py:252
  20.1 0.1 copy.11
  20.1 0.1 reshape.139.starts_ref
  20.2 0.0 copy-start.4
  20.2 0.2 multiply_reduce_fusion.power_ref
  20.4 0.7 reduce_max.9
  21.8 0.0 copy-start.1
  21.8 0.0 copy-start.2
  21.8 1.3 collective-permute-done.3
  23.1 4.2 %collective-permute-done.2 = f32[2,384,64]{2,1,0:T(8,128)} collective-permute-done((f32[2,384,64]{2,1,0:T(8,128)S(1)}, f32[2,384,64]{2,1,0:T(8,128)}, u32[]{:S(2)}, u32[]{:S(2)}) %collective-permute-start.2) | collective-permute-done | bytes 196640 | tf_op jit(solution)/shard_map/ppermute | solution.py:252
  27.3 1.3 pad_maximum_fusion.ext_ref
  28.6 35.0 %shard_map.86 = (f32[2,64,5,8,128]{4,3,2,1,0:T(8,128)}, f32[2,384,384]{2,1,0:T(8,128)S(1)}) custom-call(s32[16]{0:T(128)S(1)} %reshape.139.starts_ref, f32[1]{0:T(128)} %bitcast.step_ref, f32[2,384,384]{2,1,0:T(8,128)S(1)} %pad_maximum_fusion.ext_ref, f32[8,256,256]{2,1,0:T(8,128)S(1)} %bitcast.17, f32[256,256]{1,0:T(8,128)S(1)} %multiply_reduce_fusion.power_ref, ...), custom_call_target="tpu_custom_call" | custom-call | flops 17179869184 | bytes 8388608 | tf_op jit(solution)/shard_map/pallas_call | solution.py:211
  63.7 2.5 %dynamic-slice_bitcast_fusion = f32[64,5,8,128]{3,2,1,0:T(8,128)} fusion(f32[2,64,5,8,128]{4,3,2,1,0:T(8,128)} %get-tuple-element.53, s32[]{:T(128)S(6)} %select_n.46), kind=kLoop, calls=%fused_computation.3 | loop fusion | bytes 2621444 | tf_op jit(solution)/shard_map/jit(dynamic_index_in_dim)/squeeze | solution.py:285
  66.1 3.4 %collective-permute-done.8 = f32[64,5,8,128]{3,2,1,0:T(8,128)} collective-permute-done((f32[64,5,8,128]{3,2,1,0:T(8,128)}, f32[64,5,8,128]{3,2,1,0:T(8,128)}, u32[]{:S(2)}, u32[]{:S(2)}) %collective-permute-start.8) | collective-permute-done | bytes 1310752 | tf_op jit(solution)/shard_map/ppermute | solution.py:289
  69.5 2.9 %bitcast_add_fusion = f32[64,5,8,128]{3,2,1,0:T(8,128)} fusion(f32[64,5,8,128]{3,2,1,0:T(8,128)} %collective-permute-done.8, f32[2,64,5,8,128]{4,3,2,1,0:T(8,128)} %get-tuple-element.53, s32[]{:T(128)S(6)} %select_n.45), kind=kLoop, calls=%fused_computation.2 | loop fusion | flops 327680 | bytes 3932164 | tf_op jit(solution)/shard_map/add | solution.py:289
  72.4 14.5 %all-to-all-start = ((f32[64,5,8,128]{3,2,1,0:T(8,128)}), f32[64,5,8,128]{3,2,1,0:T(8,128)}, u32[]{:S(2)}, u32[]{:S(2)}) async-start(f32[64,5,8,128]{3,2,1,0:T(8,128)} %bitcast_add_fusion), calls=%async_computation | async-start | bytes 2621440 | tf_op jit(solution)/shard_map/all_to_all | solution.py:290
  87.0 20.9 %all-to-all-done = f32[64,5,8,128]{3,2,1,0:T(8,128)} async-done(((f32[64,5,8,128]{3,2,1,0:T(8,128)}), f32[64,5,8,128]{3,2,1,0:T(8,128)}, u32[]{:S(2)}, u32[]{:S(2)}) %all-to-all-start) | async-done | bytes 1310752 | tf_op jit(solution)/shard_map/all_to_all | solution.py:290
  107.8 1.4 reduce_sum.19
  109.3 1.1 broadcast_in_dim.2
  110.4 5.2 %all-to-all-start.1 = ((f32[64,4,8,128]{3,2,1,0:T(8,128)}), f32[64,4,8,128]{3,2,1,0:T(8,128)S(1)}, u32[]{:S(2)}, u32[]{:S(2)}) async-start(f32[64,4,8,128]{3,2,1,0:T(8,128)} %broadcast_in_dim.2), calls=%async_computation.1 | async-start | bytes 2097152 | tf_op jit(solution)/shard_map/all_to_all | solution.py:304
  115.7 4.4 %collective-permute-start.4 = (f32[2,64,384]{2,1,0:T(8,128)S(1)}, f32[2,64,384]{2,1,0:T(8,128)S(1)}, u32[]{:S(2)}, u32[]{:S(2)}) collective-permute-start(f32[2,64,384]{2,1,0:T(8,128)S(1)} %get-tuple-element.57), channel_id=1, source_target_pairs={{0,16},{16,32},{32,48},{48,64},{64,80},{80,96},{96,112},{1,17},{17... | collective-permute-start | bytes 589832 | tf_op jit(solution)/shard_map/ppermute | solution.py:252
  120.1 0.1 slice.138
  120.2 1.3 collective-permute-start.5
  121.5 9.5 %collective-permute-done.4 = f32[2,64,384]{2,1,0:T(8,128)S(1)} collective-permute-done((f32[2,64,384]{2,1,0:T(8,128)S(1)}, f32[2,64,384]{2,1,0:T(8,128)S(1)}, u32[]{:S(2)}, u32[]{:S(2)}) %collective-permute-start.4) | collective-permute-done | bytes 196640 | tf_op jit(solution)/shard_map/ppermute | solution.py:252
  131.0 1.8 %all-to-all-done.1 = f32[64,4,8,128]{3,2,1,0:T(8,128)S(1)} async-done(((f32[64,4,8,128]{3,2,1,0:T(8,128)}), f32[64,4,8,128]{3,2,1,0:T(8,128)S(1)}, u32[]{:S(2)}, u32[]{:S(2)}) %all-to-all-start.1) | async-done | bytes 1048608 | tf_op jit(solution)/shard_map/all_to_all | solution.py:304
  132.8 2.7 %collective-permute-start.9 = (f32[64,4,8,128]{3,2,1,0:T(8,128)S(1)}, f32[64,4,8,128]{3,2,1,0:T(8,128)}, u32[]{:S(2)}, u32[]{:S(2)}) collective-permute-start(f32[64,4,8,128]{3,2,1,0:T(8,128)S(1)} %all-to-all-done.1), channel_id=1, source_target_pairs={{0,1},{1,0},{2,3},{3,2},{4,5},{5,4},{6,7},{7,6},{8,9},{9,8},{10,11... | collective-permute-start | bytes 3145736 | tf_op jit(solution)/shard_map/ppermute | solution.py:307
  135.6 2.8 %collective-permute-done.5 = f32[2,64,384]{2,1,0:T(8,128)S(1)} collective-permute-done((f32[2,64,384]{2,1,0:T(8,128)S(1)}, f32[2,64,384]{2,1,0:T(8,128)S(1)}, u32[]{:S(2)}, u32[]{:S(2)}) %collective-permute-start.5) | collective-permute-done | bytes 196640 | tf_op jit(solution)/shard_map/ppermute | solution.py:252
  138.4 0.1 fusion.4
  138.5 3.9 %collective-permute-start.6 = (f32[2,256,64]{2,1,0:T(8,128)S(1)}, f32[2,256,64]{2,1,0:T(8,128)S(1)}, u32[]{:S(2)}, u32[]{:S(2)}) collective-permute-start(f32[2,256,64]{2,1,0:T(8,128)S(1)} %get-tuple-element.59), channel_id=1, source_target_pairs={{0,1},{1,2},{2,3},{3,4},{4,5},{5,6},{6,7},{7,8},{8,9},{9,10},{10,1... | collective-permute-start | bytes 393224 | tf_op jit(solution)/shard_map/ppermute | solution.py:252
  142.5 1.9 %collective-permute-start.7 = (f32[2,256,64]{2,1,0:T(8,128)S(1)}, f32[2,256,64]{2,1,0:T(8,128)S(1)}, u32[]{:S(2)}, u32[]{:S(2)}) collective-permute-start(f32[2,256,64]{2,1,0:T(8,128)S(1)} %get-tuple-element.58), channel_id=1, source_target_pairs={{1,0},{2,1},{3,2},{4,3},{5,4},{6,5},{7,6},{8,7},{9,8},{10,9},{11,1... | collective-permute-start | bytes 393224 | tf_op jit(solution)/shard_map/ppermute | solution.py:252
  144.4 1.3 collective-permute-done.6
  145.8 1.1 scatter-add.16
  146.9 3.3 %collective-permute-done.7 = f32[2,256,64]{2,1,0:T(8,128)S(1)} collective-permute-done((f32[2,256,64]{2,1,0:T(8,128)S(1)}, f32[2,256,64]{2,1,0:T(8,128)S(1)}, u32[]{:S(2)}, u32[]{:S(2)}) %collective-permute-start.7) | collective-permute-done | bytes 131104 | tf_op jit(solution)/shard_map/ppermute | solution.py:252
  150.2 0.1 slice_add_fusion
  150.3 1.2 scatter-add.19
  151.6 1.6 %broadcast_select_fusion.1 = (f32[64,4,8,128]{3,2,1,0:T(8,128)S(1)}, f32[64,4,8,128]{3,2,1,0:T(8,128)S(1)}) fusion(f32[64,4,8,128]{3,2,1,0:T(8,128)S(1)} %all-to-all-done.1, f32[64,4,8,128]{3,2,1,0:T(8,128)} %collective-permute-done.9, pred[]{:T(512)S(6)} %eq.6), kind=kLoop, calls=%fused_computation.7 | loop fusion | flops 524288 | bytes 4194305 | tf_op jit(solution)/shard_map/jit(_where)/select_n | solution.py:308
  153.2 0.3 maximum_bitcast_fusion
  153.5 1.5 copy.12
  (18 shorter events, 0.2 us)
Async XLA Ops:
  1.6 8.6 %collective-permute-start.1 = (f32[2,64,256]{2,1,0:T(8,128)S(1)}, f32[2,64,256]{2,1,0:T(8,128)S(1)}, u32[]{:S(2)}, u32[]{:S(2)}) collective-permute-start(f32[2,64,256]{2,1,0:T(8,128)S(1)} %get-tuple-element.63), channel_id=1, source_target_pairs={{16,0},{32,16},{48,32},{64,48},{80,64},{96,80},{112,96},{17,1},{33... | collective-permute-start | bytes 393224 | tf_op jit(solution)/shard_map/ppermute | solution.py:252
  2.9 17.2 %copy-start.6 = (s32[8,2]{0,1:T(2,128)S(1)}, s32[8,2]{0,1:T(2,128)}, u32[]{:S(2)}) copy-start(s32[8,2]{0,1:T(2,128)} %param.19) | copy-start | bytes 196
  2.9 17.3 %copy-start = (f32[4,2,256,256]{3,2,1,0:T(8,128)S(1)}, f32[4,2,256,256]{3,2,1,0:T(8,128)}, u32[]{:S(2)}) copy-start(f32[4,2,256,256]{3,2,1,0:T(8,128)} %param.17) | copy-start | bytes 6291460
  2.9 8.3 %collective-permute-start = (f32[2,64,256]{2,1,0:T(8,128)S(1)}, f32[2,64,256]{2,1,0:T(8,128)S(1)}, u32[]{:S(2)}, u32[]{:S(2)}) collective-permute-start(f32[2,64,256]{2,1,0:T(8,128)S(1)} %get-tuple-element.62), channel_id=1, source_target_pairs={{0,16},{16,32},{32,48},{48,64},{64,80},{80,96},{96,112},{1,17},{17... | collective-permute-start | bytes 393224 | tf_op jit(solution)/shard_map/ppermute | solution.py:252
  13.3 9.9 %collective-permute-start.3 = (f32[2,384,64]{2,1,0:T(8,128)}, f32[2,384,64]{2,1,0:T(8,128)}, u32[]{:S(2)}, u32[]{:S(2)}) collective-permute-start(f32[2,384,64]{2,1,0:T(8,128)} %get-tuple-element.61), channel_id=1, source_target_pairs={{0,1},{1,2},{2,3},{3,4},{4,5},{5,6},{6,7},{7,8},{8,9},{9,10},{10,1... | collective-permute-start | bytes 589832 | tf_op jit(solution)/shard_map/ppermute | solution.py:252
  18.1 9.2 %collective-permute-start.2 = (f32[2,384,64]{2,1,0:T(8,128)S(1)}, f32[2,384,64]{2,1,0:T(8,128)}, u32[]{:S(2)}, u32[]{:S(2)}) collective-permute-start(f32[2,384,64]{2,1,0:T(8,128)S(1)} %get-tuple-element.60), channel_id=1, source_target_pairs={{1,0},{2,1},{3,2},{4,3},{5,4},{6,5},{7,6},{8,7},{9,8},{10,9},{11,1... | collective-permute-start | bytes 589832 | tf_op jit(solution)/shard_map/ppermute | solution.py:252
  20.2 7.1 %copy-start.3 = (f32[256,256]{1,0:T(8,128)S(1)}, f32[256,256]{1,0:T(8,128)}, u32[]{:S(2)}) copy-start(f32[256,256]{1,0:T(8,128)} %param.16) | copy-start | bytes 786436
  20.2 7.1 %copy-start.4 = (f32[256,256]{1,0:T(8,128)S(1)}, f32[256,256]{1,0:T(8,128)}, u32[]{:S(2)}) copy-start(f32[256,256]{1,0:T(8,128)} %param.15) | copy-start | bytes 786436
  21.8 6.9 %copy-start.1 = (bf16[512,512]{1,0:T(8,128)(2,1)S(1)}, bf16[512,512]{1,0:T(8,128)(2,1)}, u32[]{:S(2)}) copy-start(bf16[512,512]{1,0:T(8,128)(2,1)} %constant.182.clone.fwd_ref) | copy-start | bytes 1572868
  21.8 6.9 %copy-start.2 = (bf16[512,512]{1,0:T(8,128)(2,1)S(1)}, bf16[512,512]{1,0:T(8,128)(2,1)}, u32[]{:S(2)}) copy-start(bf16[512,512]{1,0:T(8,128)(2,1)} %constant.183.clone.inv_ref) | copy-start | bytes 1572868
  66.1 3.4 %collective-permute-start.8 = (f32[64,5,8,128]{3,2,1,0:T(8,128)}, f32[64,5,8,128]{3,2,1,0:T(8,128)}, u32[]{:S(2)}, u32[]{:S(2)}) collective-permute-start(f32[64,5,8,128]{3,2,1,0:T(8,128)} %dynamic-slice_bitcast_fusion), channel_id=1, source_target_pairs={{0,1},{1,0},{2,3},{3,2},{4,5},{5,4},{6,7},{7,6},{8,9},{9,8},{10,11... | collective-permute-start | bytes 3932168 | tf_op jit(solution)/shard_map/ppermute | solution.py:289
  72.4 35.4 %all-to-all-start = ((f32[64,5,8,128]{3,2,1,0:T(8,128)}), f32[64,5,8,128]{3,2,1,0:T(8,128)}, u32[]{:S(2)}, u32[]{:S(2)}) async-start(f32[64,5,8,128]{3,2,1,0:T(8,128)} %bitcast_add_fusion), calls=%async_computation | async-start | bytes 2621440 | tf_op jit(solution)/shard_map/all_to_all | solution.py:290
  110.4 22.4 %all-to-all-start.1 = ((f32[64,4,8,128]{3,2,1,0:T(8,128)}), f32[64,4,8,128]{3,2,1,0:T(8,128)S(1)}, u32[]{:S(2)}, u32[]{:S(2)}) async-start(f32[64,4,8,128]{3,2,1,0:T(8,128)} %broadcast_in_dim.2), calls=%async_computation.1 | async-start | bytes 2097152 | tf_op jit(solution)/shard_map/all_to_all | solution.py:304
  115.7 15.3 %collective-permute-start.4 = (f32[2,64,384]{2,1,0:T(8,128)S(1)}, f32[2,64,384]{2,1,0:T(8,128)S(1)}, u32[]{:S(2)}, u32[]{:S(2)}) collective-permute-start(f32[2,64,384]{2,1,0:T(8,128)S(1)} %get-tuple-element.57), channel_id=1, source_target_pairs={{0,16},{16,32},{32,48},{48,64},{64,80},{80,96},{96,112},{1,17},{17... | collective-permute-start | bytes 589832 | tf_op jit(solution)/shard_map/ppermute | solution.py:252
  120.2 18.2 %collective-permute-start.5 = (f32[2,64,384]{2,1,0:T(8,128)S(1)}, f32[2,64,384]{2,1,0:T(8,128)S(1)}, u32[]{:S(2)}, u32[]{:S(2)}) collective-permute-start(f32[2,64,384]{2,1,0:T(8,128)S(1)} %get-tuple-element.56), channel_id=1, source_target_pairs={{16,0},{32,16},{48,32},{64,48},{80,64},{96,80},{112,96},{17,1},{33... | collective-permute-start | bytes 589832 | tf_op jit(solution)/shard_map/ppermute | solution.py:252
  132.8 18.7 %collective-permute-start.9 = (f32[64,4,8,128]{3,2,1,0:T(8,128)S(1)}, f32[64,4,8,128]{3,2,1,0:T(8,128)}, u32[]{:S(2)}, u32[]{:S(2)}) collective-permute-start(f32[64,4,8,128]{3,2,1,0:T(8,128)S(1)} %all-to-all-done.1), channel_id=1, source_target_pairs={{0,1},{1,0},{2,3},{3,2},{4,5},{5,4},{6,7},{7,6},{8,9},{9,8},{10,11... | collective-permute-start | bytes 3145736 | tf_op jit(solution)/shard_map/ppermute | solution.py:307
  138.5 7.2 %collective-permute-start.6 = (f32[2,256,64]{2,1,0:T(8,128)S(1)}, f32[2,256,64]{2,1,0:T(8,128)S(1)}, u32[]{:S(2)}, u32[]{:S(2)}) collective-permute-start(f32[2,256,64]{2,1,0:T(8,128)S(1)} %get-tuple-element.59), channel_id=1, source_target_pairs={{0,1},{1,2},{2,3},{3,4},{4,5},{5,6},{6,7},{7,8},{8,9},{9,10},{10,1... | collective-permute-start | bytes 393224 | tf_op jit(solution)/shard_map/ppermute | solution.py:252
  142.5 7.7 %collective-permute-start.7 = (f32[2,256,64]{2,1,0:T(8,128)S(1)}, f32[2,256,64]{2,1,0:T(8,128)S(1)}, u32[]{:S(2)}, u32[]{:S(2)}) collective-permute-start(f32[2,256,64]{2,1,0:T(8,128)S(1)} %get-tuple-element.58), channel_id=1, source_target_pairs={{1,0},{2,1},{3,2},{4,3},{5,4},{6,5},{7,6},{8,7},{9,8},{10,9},{11,1... | collective-permute-start | bytes 393224 | tf_op jit(solution)/shard_map/ppermute | solution.py:252
  151.5 1.7 %copy-start.5 = (f32[2,256,256]{2,1,0:T(8,128)}, f32[2,256,256]{2,1,0:T(8,128)S(1)}, u32[]{:S(2)}) copy-start(f32[2,256,256]{2,1,0:T(8,128)S(1)} %scatter-add.19) | copy-start | bytes 1572868

commit v2 on v1

v2 whole, which is shorter than its diff:
```python
import functools
import math

import jax
import jax.numpy as jnp
import numpy as np
from jax import lax
from jax.experimental import pallas as pl
from jax.experimental.pallas import tpu as pltpu
from jax.sharding import Mesh, PartitionSpec as P

H = 64
ROW = ("z", "yh")
COL = ("yl", "x", "c")
CHIPS = ("z", "yh", "yl", "x")
ALL = CHIPS + ("c",)
CHUNK = 16
PATCH = 64


def real_form(table):
    return np.concatenate(
        [
            np.concatenate([table.real, -table.imag], axis=1),
            np.concatenate([table.imag, table.real], axis=1),
        ],
        axis=0,
    )


def fourier_tables(side):
    counter = np.arange(side, dtype=np.int64)
    angle = (counter[:, None] * counter[None, :] % side).astype(np.float64) * (2.0 * math.pi / side)
    table = (np.cos(angle) - 1j * np.sin(angle)) / math.sqrt(side)
    sorted_half = np.concatenate([counter[: side // 2 : 2], counter[1 : side // 2 : 2]])
    halves = table[sorted_half]
    row_fwd = np.stack([real_form(halves[:, p::2]) for p in range(2)])
    row_inv = np.stack([real_form(halves.conj()[:, p::2]) for p in range(2)])
    col_fwd = real_form(table).T
    col_inv = real_form(table.conj()).T
    return [jnp.asarray(t, dtype=jnp.bfloat16) for t in (row_fwd, col_fwd, row_inv, col_inv)]


def cosine_sine(angle):
    turns = jnp.floor(angle * (2.0 / math.pi) + 0.5)
    rest = ((angle - turns * 1.5703125) - turns * 4.837512969970703125e-4) - turns * 7.549789954e-8
    z = rest * rest
    s = ((-1.9515295891e-4 * z + 8.3321608736e-3) * z - 1.6666654611e-1) * z * rest + rest
    c = (
        ((2.443315711809948e-5 * z - 1.388731625493765e-3) * z + 4.166664568298827e-2) * z * z
        - 0.5 * z
        + 1.0
    )
    size = jnp.abs(turns)
    odd = size == 1.0
    sign = 1.0 - size
    return jnp.where(odd, -turns * s, sign * c), jnp.where(odd, turns * c, sign * s)


def frames_kernel(
    starts_ref,
    core_ref,
    step_ref,
    ext_ref,
    probe_ref,
    power_ref,
    amps_ref,
    row_fwd_ref,
    col_fwd_ref,
    row_inv_ref,
    col_inv_ref,
    kept_ref,
    other_ref,
    canvas_ref,
    field,
    patch,
    psib,
    half,
    spec,
    corr,
    canvas,
    total,
    lined,
    level,
):
    f = pl.program_id(0)
    count = pl.num_programs(0)
    modes = probe_ref.shape[0] // 2
    side = probe_ref.shape[1]
    wide = ext_ref.shape[2]
    hside = side // 2
    quarter = side // 4
    strips = wide // 128
    lines = wide // 2

    def strip_lanes(c):
        return slice(c * 128, (c + 1) * 128)

    @pl.when(f == 0)
    def _():
        zero = jnp.zeros((CHUNK, 128), jnp.float32)

        @pl.loop(0, wide // CHUNK)
        def _(i):
            rows = pl.ds(pl.multiple_of(i * CHUNK, CHUNK), CHUNK)
            for k in range(2):
                for c in range(strips):
                    lined[k, c, rows, :] = ext_ref[k, rows, strip_lanes(c)]

        @pl.loop(0, lines // CHUNK)
        def _(i):
            rows = pl.ds(pl.multiple_of(i * CHUNK, CHUNK), CHUNK)
            for p in range(2):
                source = pl.ds(2 * i * CHUNK + p, CHUNK, stride=2)
                for c in range(strips):
                    amp = lined[0, c, source, :]
                    cosine, sine = cosine_sine(lined[1, c, source, :])
                    for k, value in enumerate((amp * cosine, amp * sine)):
                        field[p, k, c + 1, rows, :] = value
                        if c == strips - 1:
                            field[p, k, 0, rows, :] = value
                for k in range(2):
                    for c in range(strips + 1):
                        canvas[p, k, c, rows, :] = zero

        for p in range(2):
            for k in range(2):
                for c in range(strips + 1):
                    field[p, k, c, lines:, :] = jnp.zeros((8, 128), jnp.float32)
                    canvas[p, k, c, lines:, :] = jnp.zeros((8, 128), jnp.float32)

        @pl.loop(0, side // CHUNK)
        def _(i):
            rows = pl.ds(pl.multiple_of(i * CHUNK, CHUNK), CHUNK)
            for p in range(2 * modes + 1):
                total[p, rows, :] = jnp.zeros((CHUNK, side), jnp.float32)

    r0 = starts_ref[2 * f] + H
    c0 = starts_ref[2 * f + 1]
    shift = jnp.where(c0 < 0, 128 + c0, c0)
    unshift = jnp.where(shift > 0, 128 - shift, 0)
    first = jnp.where(c0 < 0, 0, 1)
    lane_tall = lax.broadcasted_iota(jnp.int32, (PATCH + 8, 128), 1)

    for i in range(side // CHUNK):
        rows = slice(i * CHUNK, (i + 1) * CHUNK)
        for c in range(side // 128):
            level[c, rows, :] = amps_ref[0, rows, strip_lanes(c)]

    def cols(m):
        return slice(m * side, (m + 1) * side)

    def line_start(w):
        q = r0 + w
        index = q // 2
        slide = lax.rem(index, 8)
        return lax.rem(q, 2), pl.multiple_of(index - slide, 8), slide

    for w in range(2):
        p, base, slide = line_start(w)
        lift = lax.rem(PATCH + 8 - slide, PATCH + 8)
        for i in range(hside // PATCH):
            rows = slice(w * hside + i * PATCH, w * hside + (i + 1) * PATCH)
            o = []
            for k in range(2):
                turned = [
                    pltpu.roll(field[p, k, first + c, pl.ds(base + i * PATCH, PATCH + 8), :], unshift, 1)
                    for c in range(3)
                ]
                near = lane_tall < 128 - shift
                joined = [jnp.where(near, turned[c], turned[c + 1]) for c in range(2)]
                o.append(
                    jnp.concatenate([pltpu.roll(x, lift, 0)[:PATCH] for x in joined], axis=1)
                )
            patch[0, rows, :] = o[0]
            patch[1, rows, :] = o[1]
            total[2 * modes, rows, :] += o[0] * o[0] + o[1] * o[1]
            for m in range(modes):
                pr = probe_ref[2 * m, rows, :]
                pi = probe_ref[2 * m + 1, rows, :]
                psib[w, i * PATCH : (i + 1) * PATCH, cols(m)] = (pr * o[0] - pi * o[1]).astype(
                    jnp.bfloat16
                )
                psib[w, hside + i * PATCH : hside + (i + 1) * PATCH, cols(m)] = (
                    pr * o[1] + pi * o[0]
                ).astype(jnp.bfloat16)

    def butterfly(table, source, m):
        a = jnp.dot(table[0], source[0, :, cols(m)], preferred_element_type=jnp.float32)
        b = jnp.dot(table[1], source[1, :, cols(m)], preferred_element_type=jnp.float32)
        return (a + b).astype(jnp.bfloat16), (a - b).astype(jnp.bfloat16)

    for m in range(modes):
        for n, value in enumerate(butterfly(row_fwd_ref, psib, m)):
            rows = slice(m * side + n * hside, m * side + (n + 1) * hside)
            half[rows, :side] = value[:hside]
            half[rows, side:] = value[hside:]
    for m in range(modes):
        spec[cols(m), :] = jnp.dot(
            half[cols(m), :], col_fwd_ref[...], preferred_element_type=jnp.float32
        )
    for i in range(side // CHUNK):
        parts = []
        energy = None
        for m in range(modes):
            here = slice(m * side + i * CHUNK, m * side + (i + 1) * CHUNK)
            a = spec[here, :side]
            b = spec[here, side:]
            e = a * a + b * b
            energy = e if energy is None else energy + e
            parts.append((a, b))
        group, offset = divmod(i * CHUNK, quarter)
        parity = group % 2
        place = group // 2 * quarter + offset
        measured = jnp.concatenate(
            [level[c, pl.ds(parity + 2 * place, CHUNK, stride=2), :] for c in range(side // 128)],
            axis=1,
        )
        fac = measured * lax.rsqrt(jnp.maximum(energy, 1.0))
        for m in range(modes):
            corr[parity, place : place + CHUNK, cols(m)] = (parts[m][0] * fac).astype(jnp.bfloat16)
            corr[parity, hside + place : hside + place + CHUNK, cols(m)] = (
                parts[m][1] * fac
            ).astype(jnp.bfloat16)
    for m in range(modes):
        for n, value in enumerate(butterfly(row_inv_ref, corr, m)):
            for w in range(2):
                start = m * side + w * hside + n * quarter
                rows = slice(start, start + quarter)
                half[rows, :side] = value[w * quarter : (w + 1) * quarter]
                half[rows, side:] = value[hside + w * quarter : hside + (w + 1) * quarter]
    for m in range(modes):
        spec[cols(m), :] = jnp.dot(
            half[cols(m), :], col_inv_ref[...], preferred_element_type=jnp.float32
        )
    for w in range(2):
        p, base, slide = line_start(w)
        for i in range(hside // PATCH):
            rows = slice(w * hside + i * PATCH, w * hside + (i + 1) * PATCH)
            o_r = patch[0, rows, :]
            o_i = patch[1, rows, :]
            power = power_ref[rows, :]
            g_r = -(o_r * power)
            g_i = -(o_i * power)
            for m in range(modes):
                row_m = slice(
                    m * side + w * hside + i * PATCH, m * side + w * hside + (i + 1) * PATCH
                )
                a = spec[row_m, :side]
                b = spec[row_m, side:]
                pr = probe_ref[2 * m, rows, :]
                pi = probe_ref[2 * m + 1, rows, :]
                g_r += pr * a + pi * b
                g_i += pr * b - pi * a
                total[2 * m, rows, :] += o_r * a + o_i * b
                total[2 * m + 1, rows, :] += o_r * b - o_i * a
            here = pl.ds(base + i * PATCH, PATCH + 8)
            far = lane_tall >= shift
            none = jnp.zeros((8, 128), jnp.float32)
            for k, g in enumerate((g_r, g_i)):
                a, b = (
                    pltpu.roll(
                        pltpu.roll(jnp.concatenate([g[:, strip_lanes(c)], none], axis=0), slide, 0),
                        shift,
                        1,
                    )
                    for c in range(2)
                )
                canvas[p, k, first, here, :] += jnp.where(far, a, 0.0)
                canvas[p, k, first + 1, here, :] += jnp.where(far, b, a)
                canvas[p, k, first + 2, here, :] += jnp.where(far, 0.0, b)

    @pl.when(f == count - 1)
    def _():
        step = step_ref[0]

        @pl.loop(0, lines // CHUNK)
        def _(i):
            rows = pl.ds(pl.multiple_of(i * CHUNK, CHUNK), CHUNK)
            inside = jnp.logical_and(i * CHUNK >= H // 2, i * CHUNK < (H + side) // 2)
            inside = inside.astype(jnp.float32)
            for p in range(2):
                target = pl.ds(2 * i * CHUNK + p, CHUNK, stride=2)
                for k in range(2):
                    for c in range(strips):
                        value = canvas[p, k, c + 1, rows, :]
                        if c == strips - 1:
                            value = step * (value + canvas[p, k, 0, rows, :])
                        else:
                            value = step * value + inside * field[p, k, c + 1, rows, :]
                        lined[k, c, target, :] = value

        @pl.loop(0, wide // CHUNK)
        def _(i):
            rows = pl.ds(pl.multiple_of(i * CHUNK, CHUNK), CHUNK)
            for k in range(2):
                for c in range(strips):
                    canvas_ref[k, rows, strip_lanes(c)] = lined[k, c, rows, :]

        planes = modes
        mine = core_ref[0] * planes
        theirs = planes - mine

        @pl.loop(0, side // 8)
        def _(i):
            rows = pl.ds(pl.multiple_of(i * 8, 8), 8)
            for j in range(side // 128):
                lanes = slice(j * 128, (j + 1) * 128)
                tile = i * (side // 128) + j
                for p in range(planes):
                    kept_ref[tile, p] = total[mine + p, rows, lanes]
                    other_ref[tile, p] = total[theirs + p, rows, lanes]
                kept_ref[tile, planes] = total[2 * modes, rows, lanes]
                other_ref[tile, planes] = total[2 * modes, rows, lanes]


def assemble_kernel(core_ref, mine_ref, theirs_ref, out_ref, lined):
    p = pl.program_id(0)
    half = pl.num_programs(0) // 2
    side = out_ref.shape[1]
    lanes = side // 128
    plane = lax.rem(p, half)

    def place(source):
        for i in range(side // 8):
            parity, line = divmod(i * 8, side // 2)
            rows = pl.ds(2 * line + parity, 8, stride=2)
            for j in range(lanes):
                lined[j, rows, :] = source[i * lanes + j, plane]
        for i in range(side // 8):
            rows = slice(i * 8, (i + 1) * 8)
            for j in range(lanes):
                out_ref[0, rows, j * 128 : (j + 1) * 128] = lined[j, rows, :]

    is_mine = p // half == core_ref[0]

    @pl.when(is_mine)
    def _():
        place(mine_ref)

    @pl.when(jnp.logical_not(is_mine))
    def _():
        place(theirs_ref)


def assemble(core, mine, theirs, side):
    tiles, planes = mine.shape[:2]

    def whole(shape):
        return pl.BlockSpec(shape, lambda p, *_: (0,) * len(shape))

    return pl.pallas_call(
        assemble_kernel,
        out_shape=jax.ShapeDtypeStruct((2 * planes, side, side), jnp.float32),
        grid_spec=pltpu.PrefetchScalarGridSpec(
            num_scalar_prefetch=1,
            grid=(2 * planes,),
            in_specs=[whole(mine.shape), whole(theirs.shape)],
            out_specs=pl.BlockSpec((1, side, side), lambda p, *_: (p, 0, 0)),
            scratch_shapes=[pltpu.VMEM((side // 128, side, 128), jnp.float32)],
        ),
        compiler_params=pltpu.CompilerParams(vmem_limit_bytes=16 * 1024 * 1024),
        cost_estimate=pl.CostEstimate(flops=0, bytes_accessed=4 * 2**20, transcendentals=0),
    )(core, mine, theirs)


def frames(starts, core, step, ext, probe, power, amps, *tables):
    count, side, _ = amps.shape
    planes = probe.shape[0]
    modes = planes // 2
    wide = ext.shape[2]
    tiles = (side // 8) * (side // 128)

    def whole(shape):
        return pl.BlockSpec(shape, lambda f, *_: (0,) * len(shape))

    return pl.pallas_call(
        frames_kernel,
        out_shape=(
            jax.ShapeDtypeStruct((tiles, planes // 2 + 1, 8, 128), jnp.float32),
            jax.ShapeDtypeStruct((tiles, planes // 2 + 1, 8, 128), jnp.float32),
            jax.ShapeDtypeStruct((2, wide, wide), jnp.float32),
        ),
        grid_spec=pltpu.PrefetchScalarGridSpec(
            num_scalar_prefetch=3,
            grid=(count,),
            in_specs=[
                whole((2, wide, wide)),
                whole((planes, side, side)),
                whole((side, side)),
                pl.BlockSpec((1, side, side), lambda f, *_: (f, 0, 0)),
                *[whole(t.shape) for t in tables],
            ],
            out_specs=(
                whole((tiles, planes // 2 + 1, 8, 128)),
                whole((tiles, planes // 2 + 1, 8, 128)),
                whole((2, wide, wide)),
            ),
            scratch_shapes=[
                pltpu.VMEM((2, 2, wide // 128 + 1, wide // 2 + 8, 128), jnp.float32),
                pltpu.VMEM((2, side, side), jnp.float32),
                pltpu.VMEM((2, side, modes * side), jnp.bfloat16),
                pltpu.VMEM((modes * side, 2 * side), jnp.bfloat16),
                pltpu.VMEM((modes * side, 2 * side), jnp.float32),
                pltpu.VMEM((2, side, modes * side), jnp.bfloat16),
                pltpu.VMEM((2, 2, wide // 128 + 1, wide // 2 + 8, 128), jnp.float32),
                pltpu.VMEM((planes + 1, side, side), jnp.float32),
                pltpu.VMEM((2, wide // 128, wide, 128), jnp.float32),
                pltpu.VMEM((side // 128, side, 128), jnp.float32),
            ],
        ),
        compiler_params=pltpu.CompilerParams(vmem_limit_bytes=34 * 1024 * 1024),
        cost_estimate=pl.CostEstimate(
            flops=count * modes * 4 * 8 * side**3, bytes_accessed=8 * 2**20, transcendentals=0
        ),
    )(starts, core, step, ext, probe, power, amps, *tables)


def exchange(low, high, axes):
    count = math.prod(lax.axis_size(a) for a in axes)
    even = lax.axis_index(axes) % 2 == 0
    pairs = [(i, i + 1) for i in range(0, count - 1, 2)]
    gaps = [(i, i + 1) for i in range(1, count - 1, 2)]
    inner = lax.ppermute(
        jnp.where(even, high, low), axes, pairs + [(j, i) for i, j in pairs]
    )
    outer = lax.ppermute(jnp.where(even, low, high), axes, gaps + [(j, i) for i, j in gaps])
    return jnp.where(even, outer, inner), jnp.where(even, inner, outer)


def shards(object_amplitude, object_phase, probe, amplitudes, positions):
    tile = object_amplitude.shape[0]
    side = probe.shape[2]
    own = jnp.stack([object_amplitude, object_phase])
    top, bottom = exchange(own[:, :H], own[:, tile - H :], ROW)
    tall = jnp.concatenate([top, own, bottom], axis=1)
    left, right = exchange(tall[:, :, :H], tall[:, :, tile - H :], COL)
    ext = jnp.concatenate([tall, right, left], axis=2)

    planes = probe.reshape((-1, side // 2, 2, side)).swapaxes(1, 2).reshape((-1, side, side))
    power = jnp.sum(planes * planes, axis=0)
    step = 1.0 / (jnp.max(power) + 1e-06)
    core = lax.axis_index("c").astype(jnp.int32)
    kept, other, canvas = frames(
        positions.reshape((-1,)),
        core.reshape((1,)),
        step.reshape((1,)),
        ext,
        planes,
        power,
        amplitudes,
        *fourier_tables(side),
    )

    mine = planes.shape[0] // 2
    swap = [(0, 1), (1, 0)]
    both = kept + lax.ppermute(other, "c", swap)
    spread = lax.all_to_all(both, CHIPS, 0, 0, tiled=True)
    from_above, from_below = exchange(canvas[:, :H, :], canvas[:, H + tile :, :], ROW)
    spread, from_above, from_below = lax.optimization_barrier((spread, from_above, from_below))
    summed = jnp.sum(spread, axis=0)
    chip = lax.axis_index(CHIPS)
    lanes = side // 128
    old = lax.dynamic_slice(
        planes, (core * mine, chip // lanes * 8, chip % lanes * 128), (mine, 8, 128)
    )
    weight = summed[mine]
    new = old + (summed[:mine] - old * weight) / (weight + 1e-05)
    gathered = lax.all_to_all(
        jnp.broadcast_to(new[None], both.shape[:1] + new.shape), CHIPS, 0, 0, tiled=True
    )
    centre = canvas[:, H : H + tile, :]
    centre = centre.at[:, :H].add(from_above)
    centre = centre.at[:, tile - H :].add(from_below)
    from_left, from_right = exchange(centre[:, :, tile + H :], centre[:, :, tile : tile + H], COL)
    inner = centre[:, :, :tile]
    inner = inner.at[:, :, :H].add(from_left)
    inner = inner.at[:, :, tile - H :].add(from_right)
    gathered, inner = lax.optimization_barrier((gathered, inner))
    swapped = lax.ppermute(gathered, "c", swap)
    new_probe = assemble(core.reshape((1,)), gathered, swapped, side)
    return (inner, new_probe.reshape(probe.shape))


def solution(mesh):
    fine = Mesh(mesh.devices.reshape((4, 2, 2, 4, 2)), ALL)
    in_specs = (
        P(ROW, COL),
        P(ROW, COL),
        P(),
        P(ALL, None, None),
        P(ALL, None),
    )
    out_specs = (P(None, ROW, COL), P())
    return jax.shard_map(shards, mesh=fine, in_specs=in_specs, out_specs=out_specs, check_vma=False)
```

time: 156 us -> 140 us (0.90)
  waiting for transfers between devices: 50.5 us -> 36.7 us
  local copies, waits for them, and re-layouts: 8.73 us -> 12.8 us
  Pallas kernels: 35 us -> 31.1 us
  starting transfers between devices: 48.5 us -> 46.8 us
    all_to_all x1, waiting for transfers between devices: 20.9 us -> 0.01 us  [shards(): spread = lax.all_to_all(both, CHIPS, 0, 0, tiled=True)]
    ppermute x10, waiting for transfers between devices: 27.8 us -> 36.7 us  [the longest x4 15.9 us: exchange(): lax.ppermute(jnp.where(even, low, high), axes, gaps + [(j, i) for i, j in...]
    all_to_all x1, starting transfers between devices: 5.23 us -> 13.2 us  [shards(): lax.all_to_all(jnp.broadcast_to(new[None], both.shape[:1] + new.shape), C...]
    ppermute x10, starting transfers between devices: 28.8 us -> 21.9 us  [the longest x4 10.6 us: exchange(): lax.ppermute(jnp.where(even, high, low), axes, pairs + [(j, i) for i, j i...]
    reshape x0 -> x2, local copies, waits for them, and re-layouts: none -> 5.33 us  [shards(): probe.reshape((-1, side // 2, 2, side)).swapaxes(1, 2)]
    select_n x1 -> x8, other arithmetic: 1.64 us -> 5.95 us  [the longest x3 3 us: exchange(): return (jnp.where(even, outer, inner), jnp.where(even, inner, outer))]
    pallas_call x1 -> x2, Pallas kernels: 35 us -> 31.1 us  [the longest x1 28 us: frames(): pl.pallas_call(frames_kernel, out_shape=(jax.ShapeDtypeStruct((tiles, pla...]
    unnamed x15 -> x35, local copies, waits for them, and re-layouts: 0.12 us -> 3.03 us
  transfers between devices with their start and end apart: 12 -> 12, of which waited for: 11 -> 6; matrix products, arithmetic and copies ran while one was open for 2% -> 9% of each run, Pallas kernels for 0% -> 0%
where the time goes in v2:
time: 140 us; the launch traced here: 139 us
  starting transfers between devices  46.8 us (33%)
  waiting for transfers between devices  36.7 us (26%)
  Pallas kernels  31.1 us (22%)
  local copies, waits for them, and re-layouts  12.8 us (9%)
  other arithmetic  9.87 us (7%)
  between operations  1.72 us (1%)
    pallas_call x1, Pallas kernels, frames(): pl.pallas_call(frames_kernel, out_shape=(jax.ShapeDtypeStruct((tiles, pla...  28 us
    ppermute x4, waiting for transfers between devices, exchange(): lax.ppermute(jnp.where(even, low, high), axes, gaps + [(j, i) for i, j in...  15.9 us
    ppermute x4, waiting for transfers between devices, exchange(): lax.ppermute(jnp.where(even, high, low), axes, pairs + [(j, i) for i, j i...  15.4 us
    all_to_all x1, starting transfers between devices, shards(): lax.all_to_all(jnp.broadcast_to(new[None], both.shape[:1] + new.shape), C...  13.2 us
    all_to_all x1, starting transfers between devices, shards(): spread = lax.all_to_all(both, CHIPS, 0, 0, tiled=True)  11.7 us
    ppermute x4, starting transfers between devices, exchange(): lax.ppermute(jnp.where(even, high, low), axes, pairs + [(j, i) for i, j i...  10.6 us
    ppermute x4, starting transfers between devices, exchange(): lax.ppermute(jnp.where(even, low, high), axes, gaps + [(j, i) for i, j in...  8.93 us
    reshape x2, local copies, waits for them, and re-layouts, shards(): probe.reshape((-1, side // 2, 2, side)).swapaxes(1, 2)  5.33 us
  transfers between devices with their start and end apart: 12, of which 6 were waited for; matrix products, arithmetic and copies ran while one was open for 9% of the time, Pallas kernels for 0%

profile of v2, /device:TPU:1, one launch (start us, length us, event | category | flops | bytes accessed | tf_op | source)
XLA Modules:
  0.0 139.0 jit_solution(413448889689059460)
XLA Ops:
  0.7 1.0 broadcast_select_fusion.7
  1.6 0.7 collective-permute-start
  2.3 6.5 %collective-permute-start.1 = (f32[2,64,256]{2,1,0:T(8,128)S(1)}, f32[2,64,256]{2,1,0:T(8,128)S(1)}, u32[]{:S(2)}, u32[]{:S(2)}) collective-permute-start(f32[2,64,256]{2,1,0:T(8,128)S(1)} %broadcast_select_fusion.6), channel_id=1, source_target_pairs={{0,16},{32,48},{64,80},{96,112},{16,0},{48,32},{80,64},{112,96},{1... | collective-permute-start | bytes 393224 | tf_op jit(solution)/shard_map/ppermute | solution.py:424
  8.8 0.1 copy.14
  8.9 0.1 reshape.144.starts_ref
  9.0 3.4 %reshape.142 = f32[8,128,2,256]{3,2,1,0:T(2,128)} reshape(f32[4,2,256,256]{3,2,1,0:T(8,128)} %param.19) | data formatting | bytes 4194304 | tf_op jit(solution)/shard_map/reshape | solution.py:440
  12.4 1.9 %copy.13 = f32[8,128,2,256]{3,1,2,0:T(8,128)S(1)} copy(f32[8,128,2,256]{3,2,1,0:T(2,128)} %reshape.142) | data formatting | bytes 4194304 | tf_op jit(solution)/shard_map/reshape | solution.py:440
  14.3 0.1 collective-permute-done.1
  14.4 0.0 copy-start.5
  14.5 0.1 pad_maximum_fusion.1
  14.5 1.1 slice_select_fusion.1
  15.6 1.5 %collective-permute-start.2 = (f32[2,384,64]{2,1,0:T(8,128)}, f32[2,384,64]{2,1,0:T(8,128)S(1)}, u32[]{:S(2)}, u32[]{:S(2)}) collective-permute-start(f32[2,384,64]{2,1,0:T(8,128)} %get-tuple-element.75), channel_id=1, source_target_pairs={{0,1},{2,3},{4,5},{6,7},{8,9},{10,11},{12,13},{14,15},{1,0},{3,2},... | collective-permute-start | bytes 589832 | tf_op jit(solution)/shard_map/ppermute | solution.py:424
  17.1 3.0 %collective-permute-start.3 = (f32[2,384,64]{2,1,0:T(8,128)}, f32[2,384,64]{2,1,0:T(8,128)}, u32[]{:S(2)}, u32[]{:S(2)}) collective-permute-start(f32[2,384,64]{2,1,0:T(8,128)} %get-tuple-element.76), channel_id=1, source_target_pairs={{1,2},{3,4},{5,6},{7,8},{9,10},{11,12},{13,14},{2,1},{4,3},{6,5},{... | collective-permute-start | bytes 589832 | tf_op jit(solution)/shard_map/ppermute | solution.py:427
  20.1 0.1 fusion
  20.3 0.7 reduce_max.9
  21.7 0.7 copy-done.14
  22.4 4.1 %collective-permute-done.3 = f32[2,384,64]{2,1,0:T(8,128)} collective-permute-done((f32[2,384,64]{2,1,0:T(8,128)}, f32[2,384,64]{2,1,0:T(8,128)}, u32[]{:S(2)}, u32[]{:S(2)}) %collective-permute-start.3) | collective-permute-done | bytes 196640 | tf_op jit(solution)/shard_map/ppermute | solution.py:427
  26.5 1.3 broadcast_select_fusion.1
  27.8 0.0 copy-start
  27.8 0.0 copy-start.1
  27.8 0.2 pad_maximum_fusion.ext_ref
  28.0 1.4 copy-done
  29.4 0.1 copy-done.1
  29.5 28.0 %shard_map.104 = (f32[64,5,8,128]{3,2,1,0:T(8,128)S(1)}, f32[64,5,8,128]{3,2,1,0:T(8,128)S(1)}, f32[2,384,384]{2,1,0:T(8,128)S(1)}) custom-call(s32[16]{0:T(128)S(1)} %reshape.144.starts_ref, s32[1]{0:T(128)} %bitcast.2.core_ref, f32[1]{0:T(128)} %bitcast.3.step_ref, f32[2,384,384]{2,1,0:T(8,128)S(1)} %pad_maximum_fusion.ext_ref, ...), custom_call_target="tpu_custom_call" | custom-call | flops 17179869184 | bytes 8388608 | tf_op jit(solution)/shard_map/pallas_call | solution.py:377
  57.5 0.1 collective-permute-start.4
  57.6 3.0 %collective-permute-done.4 = f32[64,5,8,128]{3,2,1,0:T(8,128)S(1)} collective-permute-done((f32[64,5,8,128]{3,2,1,0:T(8,128)S(1)}, f32[64,5,8,128]{3,2,1,0:T(8,128)S(1)}, u32[]{:S(2)}, u32[]{:S(2)}) %collective-permute-start.4) | collective-permute-done | bytes 1310752 | tf_op jit(solution)/shard_map/ppermute | solution.py:457
  60.7 1.2 add.100
  61.9 11.7 %all-to-all-start = ((f32[64,5,8,128]{3,2,1,0:T(8,128)}), f32[64,5,8,128]{3,2,1,0:T(8,128)}, u32[]{:S(2)}, u32[]{:S(2)}) async-start(f32[64,5,8,128]{3,2,1,0:T(8,128)} %add.100), calls=%async_computation | async-start | bytes 2621440 | tf_op jit(solution)/shard_map/all_to_all | solution.py:458
  73.6 0.8 slice_select_fusion.4
  74.3 2.5 %collective-permute-start.6 = (f32[2,64,384]{2,1,0:T(8,128)}, f32[2,64,384]{2,1,0:T(8,128)S(1)}, u32[]{:S(2)}, u32[]{:S(2)}) collective-permute-start(f32[2,64,384]{2,1,0:T(8,128)} %get-tuple-element.69), channel_id=1, source_target_pairs={{0,16},{32,48},{64,80},{96,112},{16,0},{48,32},{80,64},{112,96},{1... | collective-permute-start | bytes 589832 | tf_op jit(solution)/shard_map/ppermute | solution.py:424
  76.8 1.3 collective-permute-start.5
  78.1 0.9 slice.142
  79.0 15.4 %collective-permute-done.6 = f32[2,64,384]{2,1,0:T(8,128)S(1)} collective-permute-done((f32[2,64,384]{2,1,0:T(8,128)}, f32[2,64,384]{2,1,0:T(8,128)S(1)}, u32[]{:S(2)}, u32[]{:S(2)}) %collective-permute-start.6) | collective-permute-done | bytes 196640 | tf_op jit(solution)/shard_map/ppermute | solution.py:424
  94.4 0.7 copy-done.15
  95.1 1.7 %broadcast_select_fusion.2 = (f32[2,64,384]{2,1,0:T(8,128)S(1)}, f32[2,64,384]{2,1,0:T(8,128)}) fusion(f32[2,64,384]{2,1,0:T(8,128)} %copy-done.15, f32[2,64,384]{2,1,0:T(8,128)} %collective-permute-done.5, pred[]{:T(512)S(6)} %eq.14), kind=kLoop, calls=%fused_computation.19 | loop fusion | flops 98304 | bytes 786433 | tf_op jit(solution)/shard_map/jit(_where)/select_n | solution.py:428
  96.8 1.4 %reduce_sum.22 = f32[5,8,128]{2,1,0:T(8,128)S(1)} reduce(f32[64,5,8,128]{3,2,1,0:T(8,128)} %all-to-all-done, f32[]{:T(128)} %constant.184.clone.1), dimensions={0}, to_apply=%region_2.3 | reduce | flops 322560 | bytes 1331204 | tf_op jit(solution)/shard_map/reduce_sum | solution.py:461
  98.3 1.1 broadcast_in_dim.2
  99.4 13.2 %all-to-all-start.1 = ((f32[64,4,8,128]{3,2,1,0:T(8,128)}), f32[64,4,8,128]{3,2,1,0:T(8,128)S(1)}, u32[]{:S(2)}, u32[]{:S(2)}) async-start(f32[64,4,8,128]{3,2,1,0:T(8,128)} %broadcast_in_dim.2), calls=%async_computation.1 | async-start | bytes 2097152 | tf_op jit(solution)/shard_map/all_to_all | solution.py:469
  112.7 0.1 slice_select_fusion.2
  112.8 3.9 %collective-permute-start.7 = (f32[2,256,64]{2,1,0:T(8,128)S(1)}, f32[2,256,64]{2,1,0:T(8,128)S(1)}, u32[]{:S(2)}, u32[]{:S(2)}) collective-permute-start(f32[2,256,64]{2,1,0:T(8,128)S(1)} %get-tuple-element.72), channel_id=1, source_target_pairs={{1,2},{3,4},{5,6},{7,8},{9,10},{11,12},{13,14},{2,1},{4,3},{6,5},{... | collective-permute-start | bytes 393224 | tf_op jit(solution)/shard_map/ppermute | solution.py:427
  116.8 0.1 collective-permute-start.8
  116.9 11.8 %collective-permute-done.7 = f32[2,256,64]{2,1,0:T(8,128)S(1)} collective-permute-done((f32[2,256,64]{2,1,0:T(8,128)S(1)}, f32[2,256,64]{2,1,0:T(8,128)S(1)}, u32[]{:S(2)}, u32[]{:S(2)}) %collective-permute-start.7) | collective-permute-done | bytes 131104 | tf_op jit(solution)/shard_map/ppermute | solution.py:427
  128.8 1.1 scatter-add.16
  129.9 0.1 slice_add_fusion
  130.0 1.2 scatter-add.19
  131.3 2.4 %collective-permute-start.9 = (f32[64,4,8,128]{3,2,1,0:T(8,128)S(1)}, f32[64,4,8,128]{3,2,1,0:T(8,128)S(1)}, u32[]{:S(2)}, u32[]{:S(2)}) collective-permute-start(f32[64,4,8,128]{3,2,1,0:T(8,128)S(1)} %all-to-all-done.1.mine_ref), channel_id=1, source_target_pairs={{0,1},{1,0},{2,3},{3,2},{4,5},{5,4},{6,7},{7,6},{8,9},{9,8},{10,11... | collective-permute-start | bytes 3145736 | tf_op jit(solution)/shard_map/ppermute | solution.py:480
  133.6 2.3 %collective-permute-done.9.theirs_ref = f32[64,4,8,128]{3,2,1,0:T(8,128)S(1)} collective-permute-done((f32[64,4,8,128]{3,2,1,0:T(8,128)S(1)}, f32[64,4,8,128]{3,2,1,0:T(8,128)S(1)}, u32[]{:S(2)}, u32[]{:S(2)}) %collective-permute-start.9) | collective-permute-done | bytes 1048608 | tf_op jit(solution)/shard_map/ppermute | solution.py:480
  135.9 3.1 %shard_map.105 = f32[8,256,256]{2,1,0:T(8,128)} custom-call(s32[1]{0:T(128)} %bitcast.2.core_ref, f32[64,4,8,128]{3,2,1,0:T(8,128)S(1)} %all-to-all-done.1.mine_ref, f32[64,4,8,128]{3,2,1,0:T(8,128)S(1)} %collective-permute-done.9.theirs_ref), custom_call_target="tpu_custom_call" | custom-call | bytes 4194304 | tf_op jit(solution)/shard_map/pallas_call | solution.py:352
  (41 shorter events, 0.3 us)
Async XLA Ops:
  0.6 8.2 %copy-start.16 = (s32[8,2]{0,1:T(2,128)S(1)}, s32[8,2]{0,1:T(2,128)}, u32[]{:S(2)}) copy-start(s32[8,2]{0,1:T(2,128)} %param.21) | copy-start | bytes 196
  1.6 12.7 %collective-permute-start = (f32[2,64,256]{2,1,0:T(8,128)S(1)}, f32[2,64,256]{2,1,0:T(8,128)S(1)}, u32[]{:S(2)}, u32[]{:S(2)}) collective-permute-start(f32[2,64,256]{2,1,0:T(8,128)S(1)} %get-tuple-element.66), channel_id=1, source_target_pairs={{16,32},{48,64},{80,96},{32,16},{64,48},{96,80},{17,33},{49,65},{8... | collective-permute-start | bytes 393224 | tf_op jit(solution)/shard_map/ppermute | solution.py:427
  2.3 12.1 %collective-permute-start.1 = (f32[2,64,256]{2,1,0:T(8,128)S(1)}, f32[2,64,256]{2,1,0:T(8,128)S(1)}, u32[]{:S(2)}, u32[]{:S(2)}) collective-permute-start(f32[2,64,256]{2,1,0:T(8,128)S(1)} %broadcast_select_fusion.6), channel_id=1, source_target_pairs={{0,16},{32,48},{64,80},{96,112},{16,0},{48,32},{80,64},{112,96},{1... | collective-permute-start | bytes 393224 | tf_op jit(solution)/shard_map/ppermute | solution.py:424
  12.4 2.0 %copy-start.7 = (f32[256,256]{1,0:T(8,128)S(1)}, f32[256,256]{1,0:T(8,128)}, u32[]{:S(2)}) copy-start(f32[256,256]{1,0:T(8,128)} %param.18) | copy-start | bytes 786436
  12.4 2.0 %copy-start.8 = (f32[256,256]{1,0:T(8,128)S(1)}, f32[256,256]{1,0:T(8,128)}, u32[]{:S(2)}) copy-start(f32[256,256]{1,0:T(8,128)} %param.17) | copy-start | bytes 786436
  14.4 1.2 copy-start.11
  14.4 5.7 %copy-start.5 = (f32[8,128,2,256]{3,2,1,0:T(2,128)S(1)}, f32[8,128,2,256]{3,2,1,0:T(2,128)}, u32[]{:S(2)}) copy-start(f32[8,128,2,256]{3,2,1,0:T(2,128)} %reshape.142) | copy-start | bytes 6291460
  15.6 6.1 %collective-permute-start.2 = (f32[2,384,64]{2,1,0:T(8,128)}, f32[2,384,64]{2,1,0:T(8,128)S(1)}, u32[]{:S(2)}, u32[]{:S(2)}) collective-permute-start(f32[2,384,64]{2,1,0:T(8,128)} %get-tuple-element.75), channel_id=1, source_target_pairs={{0,1},{2,3},{4,5},{6,7},{8,9},{10,11},{12,13},{14,15},{1,0},{3,2},... | collective-permute-start | bytes 589832 | tf_op jit(solution)/shard_map/ppermute | solution.py:424
  17.1 9.4 %collective-permute-start.3 = (f32[2,384,64]{2,1,0:T(8,128)}, f32[2,384,64]{2,1,0:T(8,128)}, u32[]{:S(2)}, u32[]{:S(2)}) collective-permute-start(f32[2,384,64]{2,1,0:T(8,128)} %get-tuple-element.76), channel_id=1, source_target_pairs={{1,2},{3,4},{5,6},{7,8},{9,10},{11,12},{13,14},{2,1},{4,3},{6,5},{... | collective-permute-start | bytes 589832 | tf_op jit(solution)/shard_map/ppermute | solution.py:427
  20.3 7.5 %copy-start.9 = (f32[256,256]{1,0:T(8,128)S(1)}, f32[256,256]{1,0:T(8,128)}, u32[]{:S(2)}) copy-start(f32[256,256]{1,0:T(8,128)} %param.17) | copy-start | bytes 786436
  20.3 7.5 %copy-start.12 = (f32[2,64,256]{2,1,0:T(8,128)S(1)}, f32[2,64,256]{2,1,0:T(8,128)}, u32[]{:S(2)}) copy-start(f32[2,64,256]{2,1,0:T(8,128)} %copy-done.11) | copy-start | bytes 393220
  21.7 0.7 copy-start.14
  26.5 1.5 %copy-start.2 = (bf16[512,512]{1,0:T(8,128)(2,1)S(1)}, bf16[512,512]{1,0:T(8,128)(2,1)}, u32[]{:S(2)}) copy-start(bf16[512,512]{1,0:T(8,128)(2,1)} %constant.192.clone.col_inv_ref) | copy-start | bytes 1572868
  26.5 1.5 %copy-start.3 = (bf16[2,256,256]{2,1,0:T(8,128)(2,1)S(1)}, bf16[2,256,256]{2,1,0:T(8,128)(2,1)}, u32[]{:S(2)}) copy-start(bf16[2,256,256]{2,1,0:T(8,128)(2,1)} %constant.189.clone.row_fwd_ref) | copy-start | bytes 786436
  26.5 1.5 %copy-start.4 = (bf16[2,256,256]{2,1,0:T(8,128)(2,1)S(1)}, bf16[2,256,256]{2,1,0:T(8,128)(2,1)}, u32[]{:S(2)}) copy-start(bf16[2,256,256]{2,1,0:T(8,128)(2,1)} %constant.191.clone.row_inv_ref) | copy-start | bytes 786436
  27.8 1.6 %copy-start = (f32[8,256,256]{2,1,0:T(8,128)S(1)}, f32[8,256,256]{2,1,0:T(8,128)}, u32[]{:S(2)}) copy-start(f32[8,256,256]{2,1,0:T(8,128)} %amps_ref.1) | copy-start | bytes 6291460
  27.8 1.7 %copy-start.1 = (bf16[512,512]{1,0:T(8,128)(2,1)S(1)}, bf16[512,512]{1,0:T(8,128)(2,1)}, u32[]{:S(2)}) copy-start(bf16[512,512]{1,0:T(8,128)(2,1)} %constant.190.clone.col_fwd_ref) | copy-start | bytes 1572868
  57.5 3.1 %collective-permute-start.4 = (f32[64,5,8,128]{3,2,1,0:T(8,128)S(1)}, f32[64,5,8,128]{3,2,1,0:T(8,128)S(1)}, u32[]{:S(2)}, u32[]{:S(2)}) collective-permute-start(f32[64,5,8,128]{3,2,1,0:T(8,128)S(1)} %get-tuple-element.59), channel_id=1, source_target_pairs={{0,1},{1,0},{2,3},{3,2},{4,5},{5,4},{6,7},{7,6},{8,9},{9,8},{10,11... | collective-permute-start | bytes 3932168 | tf_op jit(solution)/shard_map/ppermute | solution.py:457
  61.9 35.0 %all-to-all-start = ((f32[64,5,8,128]{3,2,1,0:T(8,128)}), f32[64,5,8,128]{3,2,1,0:T(8,128)}, u32[]{:S(2)}, u32[]{:S(2)}) async-start(f32[64,5,8,128]{3,2,1,0:T(8,128)} %add.100), calls=%async_computation | async-start | bytes 2621440 | tf_op jit(solution)/shard_map/all_to_all | solution.py:458
  74.3 20.1 %collective-permute-start.6 = (f32[2,64,384]{2,1,0:T(8,128)}, f32[2,64,384]{2,1,0:T(8,128)S(1)}, u32[]{:S(2)}, u32[]{:S(2)}) collective-permute-start(f32[2,64,384]{2,1,0:T(8,128)} %get-tuple-element.69), channel_id=1, source_target_pairs={{0,16},{32,48},{64,80},{96,112},{16,0},{48,32},{80,64},{112,96},{1... | collective-permute-start | bytes 589832 | tf_op jit(solution)/shard_map/ppermute | solution.py:424
  76.8 18.3 %collective-permute-start.5 = (f32[2,64,384]{2,1,0:T(8,128)}, f32[2,64,384]{2,1,0:T(8,128)}, u32[]{:S(2)}, u32[]{:S(2)}) collective-permute-start(f32[2,64,384]{2,1,0:T(8,128)} %get-tuple-element.70), channel_id=1, source_target_pairs={{16,32},{48,64},{80,96},{32,16},{64,48},{96,80},{17,33},{49,65},{8... | collective-permute-start | bytes 589832 | tf_op jit(solution)/shard_map/ppermute | solution.py:427
  94.4 0.7 copy-start.15
  99.4 13.2 %copy-start.6 = (f32[2,256,384]{2,1,0:T(8,128)S(1)}, f32[2,256,384]{2,1,0:T(8,128)}, u32[]{:S(2)}) copy-start(f32[2,256,384]{2,1,0:T(8,128)} %slice.142) | copy-start | bytes 2359300
  99.4 13.2 %copy-start.13 = (f32[2,64,384]{2,1,0:T(8,128)S(1)}, f32[2,64,384]{2,1,0:T(8,128)}, u32[]{:S(2)}) copy-start(f32[2,64,384]{2,1,0:T(8,128)} %get-tuple-element.62) | copy-start | bytes 589828
  99.4 31.9 %all-to-all-start.1 = ((f32[64,4,8,128]{3,2,1,0:T(8,128)}), f32[64,4,8,128]{3,2,1,0:T(8,128)S(1)}, u32[]{:S(2)}, u32[]{:S(2)}) async-start(f32[64,4,8,128]{3,2,1,0:T(8,128)} %broadcast_in_dim.2), calls=%async_computation.1 | async-start | bytes 2097152 | tf_op jit(solution)/shard_map/all_to_all | solution.py:469
  112.8 15.9 %collective-permute-start.7 = (f32[2,256,64]{2,1,0:T(8,128)S(1)}, f32[2,256,64]{2,1,0:T(8,128)S(1)}, u32[]{:S(2)}, u32[]{:S(2)}) collective-permute-start(f32[2,256,64]{2,1,0:T(8,128)S(1)} %get-tuple-element.72), channel_id=1, source_target_pairs={{1,2},{3,4},{5,6},{7,8},{9,10},{11,12},{13,14},{2,1},{4,3},{6,5},{... | collective-permute-start | bytes 393224 | tf_op jit(solution)/shard_map/ppermute | solution.py:427
  116.8 12.0 %collective-permute-start.8 = (f32[2,256,64]{2,1,0:T(8,128)S(1)}, f32[2,256,64]{2,1,0:T(8,128)S(1)}, u32[]{:S(2)}, u32[]{:S(2)}) collective-permute-start(f32[2,256,64]{2,1,0:T(8,128)S(1)} %get-tuple-element.71), channel_id=1, source_target_pairs={{0,1},{2,3},{4,5},{6,7},{8,9},{10,11},{12,13},{14,15},{1,0},{3,2},... | collective-permute-start | bytes 393224 | tf_op jit(solution)/shard_map/ppermute | solution.py:424
  131.2 7.8 %copy-start.10 = (f32[2,256,256]{2,1,0:T(8,128)}, f32[2,256,256]{2,1,0:T(8,128)S(1)}, u32[]{:S(2)}) copy-start(f32[2,256,256]{2,1,0:T(8,128)S(1)} %scatter-add.19) | copy-start | bytes 1572868
  131.3 4.6 %collective-permute-start.9 = (f32[64,4,8,128]{3,2,1,0:T(8,128)S(1)}, f32[64,4,8,128]{3,2,1,0:T(8,128)S(1)}, u32[]{:S(2)}, u32[]{:S(2)}) collective-permute-start(f32[64,4,8,128]{3,2,1,0:T(8,128)S(1)} %all-to-all-done.1.mine_ref), channel_id=1, source_target_pairs={{0,1},{1,0},{2,3},{3,2},{4,5},{5,4},{6,7},{7,6},{8,9},{9,8},{10,11... | collective-permute-start | bytes 3145736 | tf_op jit(solution)/shard_map/ppermute | solution.py:480

commit v3 on v2

--- a/solution.py
+++ b/solution.py
@@ -16,6 +16,7 @@
 ALL = CHIPS + ("c",)
 CHUNK = 16
 PATCH = 64
+GROUP = 64
 
 
 def real_form(table):
@@ -76,7 +77,7 @@
     patch,
     psib,
     half,
-    spec,
+    grad,
     corr,
     canvas,
     total,
@@ -190,77 +191,92 @@
         b = jnp.dot(table[1], source[1, :, cols(m)], preferred_element_type=jnp.float32)
         return (a + b).astype(jnp.bfloat16), (a - b).astype(jnp.bfloat16)
 
+    def spread_rows(m, row, lanes, value):
+        size = min(GROUP, value.shape[0])
+        for t in range(value.shape[0] // size):
+            group, offset = divmod(row + t * size, GROUP)
+            start = (group * modes + m) * GROUP + offset
+            half[start : start + size, lanes] = value[t * size : (t + 1) * size]
+
+    def columns(t, table):
+        rows = slice(t * modes * GROUP, (t + 1) * modes * GROUP)
+        return jnp.dot(half[rows, :], table[...], preferred_element_type=jnp.float32)
+
+    first_lanes, last_lanes = slice(0, side), slice(side, 2 * side)
     for m in range(modes):
         for n, value in enumerate(butterfly(row_fwd_ref, psib, m)):
-            rows = slice(m * side + n * hside, m * side + (n + 1) * hside)
-            half[rows, :side] = value[:hside]
-            half[rows, side:] = value[hside:]
-    for m in range(modes):
-        spec[cols(m), :] = jnp.dot(
-            half[cols(m), :], col_fwd_ref[...], preferred_element_type=jnp.float32
-        )
-    for i in range(side // CHUNK):
-        parts = []
-        energy = None
-        for m in range(modes):
-            here = slice(m * side + i * CHUNK, m * side + (i + 1) * CHUNK)
-            a = spec[here, :side]
-            b = spec[here, side:]
-            e = a * a + b * b
-            energy = e if energy is None else energy + e
-            parts.append((a, b))
-        group, offset = divmod(i * CHUNK, quarter)
-        parity = group % 2
-        place = group // 2 * quarter + offset
-        measured = jnp.concatenate(
-            [level[c, pl.ds(parity + 2 * place, CHUNK, stride=2), :] for c in range(side // 128)],
-            axis=1,
-        )
-        fac = measured * lax.rsqrt(jnp.maximum(energy, 1.0))
-        for m in range(modes):
-            corr[parity, place : place + CHUNK, cols(m)] = (parts[m][0] * fac).astype(jnp.bfloat16)
-            corr[parity, hside + place : hside + place + CHUNK, cols(m)] = (
-                parts[m][1] * fac
-            ).astype(jnp.bfloat16)
+            spread_rows(m, n * hside, first_lanes, value[:hside])
+            spread_rows(m, n * hside, last_lanes, value[hside:])
+    for t in range(side // GROUP):
+        product = columns(t, col_fwd_ref)
+        for u in range(GROUP // CHUNK):
+            i = t * (GROUP // CHUNK) + u
+            parts = []
+            energy = None
+            for m in range(modes):
+                here = slice(m * GROUP + u * CHUNK, m * GROUP + (u + 1) * CHUNK)
+                a = product[here, :side]
+                b = product[here, side:]
+                e = a * a + b * b
+                energy = e if energy is None else energy + e
+                parts.append((a, b))
+            group, offset = divmod(i * CHUNK, quarter)
+            parity = group % 2
+            place = group // 2 * quarter + offset
+            measured = jnp.concatenate(
+                [level[c, pl.ds(parity + 2 * place, CHUNK, stride=2), :] for c in range(side // 128)],
+                axis=1,
+            )
+            fac = measured * lax.rsqrt(jnp.maximum(energy, 1.0))
+            for m in range(modes):
+                corr[parity, place : place + CHUNK, cols(m)] = (parts[m][0] * fac).astype(
+                    jnp.bfloat16
+                )
+                corr[parity, hside + place : hside + place + CHUNK, cols(m)] = (
+                    parts[m][1] * fac
+                ).astype(jnp.bfloat16)
     for m in range(modes):
         for n, value in enumerate(butterfly(row_inv_ref, corr, m)):
             for w in range(2):
-                start = m * side + w * hside + n * quarter
-                rows = slice(start, start + quarter)
-                half[rows, :side] = value[w * quarter : (w + 1) * quarter]
-                half[rows, side:] = value[hside + w * quarter : hside + (w + 1) * quarter]
-    for m in range(modes):
-        spec[cols(m), :] = jnp.dot(
-            half[cols(m), :], col_inv_ref[...], preferred_element_type=jnp.float32
-        )
-    for w in range(2):
-        p, base, slide = line_start(w)
-        for i in range(hside // PATCH):
-            rows = slice(w * hside + i * PATCH, w * hside + (i + 1) * PATCH)
+                row = w * hside + n * quarter
+                spread_rows(m, row, first_lanes, value[w * quarter : (w + 1) * quarter])
+                spread_rows(
+                    m, row, last_lanes, value[hside + w * quarter : hside + (w + 1) * quarter]
+                )
+    for t in range(side // GROUP):
+        product = columns(t, col_inv_ref)
+        for u in range(GROUP // CHUNK):
+            rows = slice(t * GROUP + u * CHUNK, t * GROUP + (u + 1) * CHUNK)
             o_r = patch[0, rows, :]
             o_i = patch[1, rows, :]
             power = power_ref[rows, :]
             g_r = -(o_r * power)
             g_i = -(o_i * power)
             for m in range(modes):
-                row_m = slice(
-                    m * side + w * hside + i * PATCH, m * side + w * hside + (i + 1) * PATCH
-                )
-                a = spec[row_m, :side]
-                b = spec[row_m, side:]
+                here = slice(m * GROUP + u * CHUNK, m * GROUP + (u + 1) * CHUNK)
+                a = product[here, :side]
+                b = product[here, side:]
                 pr = probe_ref[2 * m, rows, :]
                 pi = probe_ref[2 * m + 1, rows, :]
                 g_r += pr * a + pi * b
                 g_i += pr * b - pi * a
                 total[2 * m, rows, :] += o_r * a + o_i * b
                 total[2 * m + 1, rows, :] += o_r * b - o_i * a
+            grad[0, rows, :] = g_r
+            grad[1, rows, :] = g_i
+    for w in range(2):
+        p, base, slide = line_start(w)
+        for i in range(hside // PATCH):
+            rows = slice(w * hside + i * PATCH, w * hside + (i + 1) * PATCH)
             here = pl.ds(base + i * PATCH, PATCH + 8)
             far = lane_tall >= shift
             none = jnp.zeros((8, 128), jnp.float32)
-            for k, g in enumerate((g_r, g_i)):
+            for k in range(2):
                 a, b = (
                     pltpu.roll(
-                        pltpu.roll(jnp.concatenate([g[:, strip_lanes(c)], none], axis=0), slide, 0),
+                        pltpu.roll(
+                            jnp.concatenate([grad[k, rows, strip_lanes(c)], none], axis=0), slide, 0
+                        ),
                         shift,
                         1,
                     )
@@ -314,54 +330,69 @@
                 other_ref[tile, planes] = total[2 * modes, rows, lanes]
 
 
-def assemble_kernel(core_ref, mine_ref, theirs_ref, out_ref, lined):
-    p = pl.program_id(0)
-    half = pl.num_programs(0) // 2
+def renew_kernel(spread_ref, old_ref, out_ref):
+    modes = old_ref.shape[0]
+    sums = [jnp.zeros((8, 128), jnp.float32) for _ in range(modes + 1)]
+    for i in range(spread_ref.shape[0]):
+        for p in range(modes + 1):
+            sums[p] += spread_ref[i, p]
+    weight = sums[modes]
+    for p in range(modes):
+        old = old_ref[p]
+        new = old + (sums[p] - old * weight) / (weight + 1e-05)
+        for i in range(out_ref.shape[0]):
+            out_ref[i, p] = new
+
+
+def renew(spread, old):
+    return pl.pallas_call(
+        renew_kernel,
+        out_shape=jax.ShapeDtypeStruct(spread.shape[:1] + old.shape, jnp.float32),
+        in_specs=[pl.BlockSpec(memory_space=pltpu.VMEM)] * 2,
+        out_specs=pl.BlockSpec(memory_space=pltpu.VMEM),
+        compiler_params=pltpu.CompilerParams(vmem_limit_bytes=8 * 1024 * 1024),
+        cost_estimate=pl.CostEstimate(flops=0, bytes_accessed=2 * 2**20, transcendentals=0),
+    )(spread, old)
+
+
+def assemble_kernel(first_ref, source_ref, *refs):
+    out_ref, lined = refs[-2:]
+    plane = pl.program_id(0)
     side = out_ref.shape[1]
     lanes = side // 128
-    plane = lax.rem(p, half)
-
-    def place(source):
-        for i in range(side // 8):
-            parity, line = divmod(i * 8, side // 2)
-            rows = pl.ds(2 * line + parity, 8, stride=2)
-            for j in range(lanes):
-                lined[j, rows, :] = source[i * lanes + j, plane]
-        for i in range(side // 8):
-            rows = slice(i * 8, (i + 1) * 8)
-            for j in range(lanes):
-                out_ref[0, rows, j * 128 : (j + 1) * 128] = lined[j, rows, :]
-
-    is_mine = p // half == core_ref[0]
-
-    @pl.when(is_mine)
-    def _():
-        place(mine_ref)
-
-    @pl.when(jnp.logical_not(is_mine))
-    def _():
-        place(theirs_ref)
-
-
-def assemble(core, mine, theirs, side):
-    tiles, planes = mine.shape[:2]
-
-    def whole(shape):
-        return pl.BlockSpec(shape, lambda p, *_: (0,) * len(shape))
-
+    for i in range(side // 8):
+        parity, line = divmod(i * 8, side // 2)
+        rows = pl.ds(2 * line + parity, 8, stride=2)
+        for j in range(lanes):
+            lined[j, rows, :] = source_ref[i * lanes + j, plane]
+    for i in range(side // 8):
+        rows = slice(i * 8, (i + 1) * 8)
+        for j in range(lanes):
+            out_ref[0, rows, j * 128 : (j + 1) * 128] = lined[j, rows, :]
+
+
+def assemble(first, source, side, started=None):
+    planes = source.shape[1]
+    more = () if started is None else (started,)
     return pl.pallas_call(
         assemble_kernel,
         out_shape=jax.ShapeDtypeStruct((2 * planes, side, side), jnp.float32),
         grid_spec=pltpu.PrefetchScalarGridSpec(
             num_scalar_prefetch=1,
-            grid=(2 * planes,),
-            in_specs=[whole(mine.shape), whole(theirs.shape)],
-            out_specs=pl.BlockSpec((1, side, side), lambda p, *_: (p, 0, 0)),
+            grid=(planes,),
+            in_specs=[
+                pl.BlockSpec(source.shape, lambda p, *_: (0,) * source.ndim),
+                *[pl.BlockSpec(memory_space=pl.ANY) for _ in more],
+            ],
+            out_specs=pl.BlockSpec(
+                (1, side, side), lambda p, first_ref: (first_ref[0] + p, 0, 0)
+            ),
             scratch_shapes=[pltpu.VMEM((side // 128, side, 128), jnp.float32)],
         ),
+        input_output_aliases={2: 0} if more else {},
         compiler_params=pltpu.CompilerParams(vmem_limit_bytes=16 * 1024 * 1024),
-        cost_estimate=pl.CostEstimate(flops=0, bytes_accessed=4 * 2**20, transcendentals=0),
-    )(core, mine, theirs)
+        cost_estimate=pl.CostEstimate(flops=0, bytes_accessed=2 * 2**20, transcendentals=0),
+    )(first, source, *more)
 
 
 def frames(starts, core, step, ext, probe, power, amps, *tables):
@@ -401,7 +432,7 @@
                 pltpu.VMEM((2, side, side), jnp.float32),
                 pltpu.VMEM((2, side, modes * side), jnp.bfloat16),
                 pltpu.VMEM((modes * side, 2 * side), jnp.bfloat16),
-                pltpu.VMEM((modes * side, 2 * side), jnp.float32),
+                pltpu.VMEM((2, side, side), jnp.float32),
                 pltpu.VMEM((2, side, modes * side), jnp.bfloat16),
                 pltpu.VMEM((2, 2, wide // 128 + 1, wide // 2 + 8, 128), jnp.float32),
                 pltpu.VMEM((planes + 1, side, side), jnp.float32),
@@ -455,20 +486,15 @@
     mine = planes.shape[0] // 2
     swap = [(0, 1), (1, 0)]
     both = kept + lax.ppermute(other, "c", swap)
+    from_above, from_below = exchange(canvas[:, :H, :], canvas[:, H + tile :, :], ROW)
+    both, from_above, from_below = lax.optimization_barrier((both, from_above, from_below))
     spread = lax.all_to_all(both, CHIPS, 0, 0, tiled=True)
-    from_above, from_below = exchange(canvas[:, :H, :], canvas[:, H + tile :, :], ROW)
-    spread, from_above, from_below = lax.optimization_barrier((spread, from_above, from_below))
-    summed = jnp.sum(spread, axis=0)
     chip = lax.axis_index(CHIPS)
     lanes = side // 128
     old = lax.dynamic_slice(
         planes, (core * mine, chip // lanes * 8, chip % lanes * 128), (mine, 8, 128)
     )
-    weight = summed[mine]
-    new = old + (summed[:mine] - old * weight) / (weight + 1e-05)
-    gathered = lax.all_to_all(
-        jnp.broadcast_to(new[None], both.shape[:1] + new.shape), CHIPS, 0, 0, tiled=True
-    )
+    gathered = lax.all_to_all(renew(spread, old), CHIPS, 0, 0, tiled=True)
     centre = canvas[:, H : H + tile, :]
     centre = centre.at[:, :H].add(from_above)
     centre = centre.at[:, tile - H :].add(from_below)
@@ -478,7 +504,9 @@
     inner = inner.at[:, :, tile - H :].add(from_right)
     gathered, inner = lax.optimization_barrier((gathered, inner))
     swapped = lax.ppermute(gathered, "c", swap)
-    new_probe = assemble(core.reshape((1,)), gathered, swapped, side)
+    first = (core * mine).reshape((1,))
+    new_probe = assemble(first, gathered, side)
+    new_probe = assemble(mine - first, swapped, side, new_probe)
     return (inner, new_probe.reshape(probe.shape))
 
 

time: 140 us -> 135 us (0.964)
  waiting for transfers between devices: 36.7 us -> 39.7 us
  other arithmetic: 9.87 us -> 7.55 us
  starting transfers between devices: 46.8 us -> 44.5 us
  local copies, waits for them, and re-layouts: 12.8 us -> 10.6 us
    all_to_all x1, waiting for transfers between devices: 0.01 us -> 17.5 us  [shards(): spread = lax.all_to_all(both, CHIPS, 0, 0, tiled=True)]
    ppermute x4, waiting for transfers between devices: 15.4 us -> 6.39 us  [exchange(): lax.ppermute(jnp.where(even, high, low), axes, pairs + [(j, i) for i, j i...]
    all_to_all x1, starting transfers between devices: 13.2 us -> 5.3 us  [shards(): gathered = lax.all_to_all(renew(spread, old), CHIPS, 0, 0, tiled=True)]
    all_to_all x1, starting transfers between devices: 11.7 us -> 16.6 us  [shards(): spread = lax.all_to_all(both, CHIPS, 0, 0, tiled=True)]
    ppermute x1, waiting for transfers between devices: 3.02 us -> 0.01 us  [shards(): both = kept + lax.ppermute(other, 'c', swap)]
    ppermute x4, starting transfers between devices: 10.6 us -> 8.67 us  [exchange(): lax.ppermute(jnp.where(even, high, low), axes, pairs + [(j, i) for i, j i...]
    pallas_call x1, Pallas kernels: 28 us -> 26.4 us  [frames(): pl.pallas_call(frames_kernel, out_shape=(jax.ShapeDtypeStruct((tiles, pla...]
    ppermute x1, starting transfers between devices: 2.36 us -> 3.99 us  [shards(): swapped = lax.ppermute(gathered, 'c', swap)]
  transfers between devices with their start and end apart: 12 -> 12, of which waited for: 6 -> 6; matrix products, arithmetic and copies ran while one was open for 9% -> 9% of each run, Pallas kernels for 0% -> 1%
where the time goes in v3:
time: 135 us
  starting transfers between devices  44.5 us (33%)
  waiting for transfers between devices  39.7 us (29%)
  Pallas kernels  30.7 us (23%)
  local copies, waits for them, and re-layouts  10.6 us (8%)
  other arithmetic  7.55 us (6%)
  between operations  1.74 us (1%)
    pallas_call x1, Pallas kernels, frames(): pl.pallas_call(frames_kernel, out_shape=(jax.ShapeDtypeStruct((tiles, pla...  26.4 us
    all_to_all x1, waiting for transfers between devices, shards(): spread = lax.all_to_all(both, CHIPS, 0, 0, tiled=True)  17.5 us
    all_to_all x1, starting transfers between devices, shards(): spread = lax.all_to_all(both, CHIPS, 0, 0, tiled=True)  16.6 us
    ppermute x4, waiting for transfers between devices, exchange(): lax.ppermute(jnp.where(even, low, high), axes, gaps + [(j, i) for i, j in...  15.1 us
    ppermute x4, starting transfers between devices, exchange(): lax.ppermute(jnp.where(even, low, high), axes, gaps + [(j, i) for i, j in...  9.89 us
    ppermute x4, starting transfers between devices, exchange(): lax.ppermute(jnp.where(even, high, low), axes, pairs + [(j, i) for i, j i...  8.67 us
    ppermute x4, waiting for transfers between devices, exchange(): lax.ppermute(jnp.where(even, high, low), axes, pairs + [(j, i) for i, j i...  6.39 us
    reshape x2, local copies, waits for them, and re-layouts, shards(): probe.reshape((-1, side // 2, 2, side)).swapaxes(1, 2)  5.33 us
  transfers between devices with their start and end apart: 12, of which 6 were waited for; matrix products, arithmetic and copies ran while one was open for 9% of the time, Pallas kernels for 1%

profile of v3, /device:TPU:1, one launch (start us, length us, event | category | flops | bytes accessed | tf_op | source)
XLA Modules:
  0.0 134.9 jit_solution(8568317863850950939)
XLA Ops:
  0.7 1.0 broadcast_select_fusion.7
  1.6 0.7 collective-permute-start
  2.3 6.5 %collective-permute-start.1 = (f32[2,64,256]{2,1,0:T(8,128)S(1)}, f32[2,64,256]{2,1,0:T(8,128)S(1)}, u32[]{:S(2)}, u32[]{:S(2)}) collective-permute-start(f32[2,64,256]{2,1,0:T(8,128)S(1)} %broadcast_select_fusion.6), channel_id=1, source_target_pairs={{0,16},{32,48},{64,80},{96,112},{16,0},{48,32},{80,64},{112,96},{1... | collective-permute-start | bytes 393224 | tf_op jit(solution)/shard_map/ppermute | solution.py:455
  8.8 0.1 copy.14
  8.9 0.1 reshape.143.starts_ref
  9.0 3.4 %reshape.145 = f32[8,128,2,256]{3,2,1,0:T(2,128)} reshape(f32[4,2,256,256]{3,2,1,0:T(8,128)} %param.19) | data formatting | bytes 4194304 | tf_op jit(solution)/shard_map/reshape | solution.py:471
  12.4 1.9 %copy.15 = f32[8,128,2,256]{3,1,2,0:T(8,128)S(1)} copy(f32[8,128,2,256]{3,2,1,0:T(2,128)} %reshape.145) | data formatting | bytes 4194304 | tf_op jit(solution)/shard_map/reshape | solution.py:471
  14.3 0.1 collective-permute-done.1
  14.4 0.0 copy-start.6
  14.4 0.1 pad_maximum_fusion.1
  14.5 1.1 slice_select_fusion.1
  15.6 1.5 %collective-permute-start.2 = (f32[2,384,64]{2,1,0:T(8,128)}, f32[2,384,64]{2,1,0:T(8,128)S(1)}, u32[]{:S(2)}, u32[]{:S(2)}) collective-permute-start(f32[2,384,64]{2,1,0:T(8,128)} %get-tuple-element.75), channel_id=1, source_target_pairs={{0,1},{2,3},{4,5},{6,7},{8,9},{10,11},{12,13},{14,15},{1,0},{3,2},... | collective-permute-start | bytes 589832 | tf_op jit(solution)/shard_map/ppermute | solution.py:455
  17.1 3.0 %collective-permute-start.3 = (f32[2,384,64]{2,1,0:T(8,128)}, f32[2,384,64]{2,1,0:T(8,128)}, u32[]{:S(2)}, u32[]{:S(2)}) collective-permute-start(f32[2,384,64]{2,1,0:T(8,128)} %get-tuple-element.76), channel_id=1, source_target_pairs={{1,2},{3,4},{5,6},{7,8},{9,10},{11,12},{13,14},{2,1},{4,3},{6,5},{... | collective-permute-start | bytes 589832 | tf_op jit(solution)/shard_map/ppermute | solution.py:458
  20.1 0.1 fusion
  20.3 0.7 reduce_max.9
  21.6 0.0 collective-permute-done.2
  21.6 4.9 %collective-permute-done.3 = f32[2,384,64]{2,1,0:T(8,128)} collective-permute-done((f32[2,384,64]{2,1,0:T(8,128)}, f32[2,384,64]{2,1,0:T(8,128)}, u32[]{:S(2)}, u32[]{:S(2)}) %collective-permute-start.3) | collective-permute-done | bytes 196640 | tf_op jit(solution)/shard_map/ppermute | solution.py:458
  26.5 1.1 broadcast_select_fusion.1
  27.7 0.0 copy-start.1
  27.7 0.0 copy-start.2
  27.7 0.2 pad_maximum_fusion.ext_ref
  27.9 1.4 %copy-done.1 = f32[8,256,256]{2,1,0:T(8,128)S(1)} copy-done((f32[8,256,256]{2,1,0:T(8,128)S(1)}, f32[8,256,256]{2,1,0:T(8,128)}, u32[]{:S(2)}) %copy-start.1) | copy-done | bytes 2097176
  29.3 0.1 copy-done.2
  29.4 26.4 %shard_map.104 = (f32[64,5,8,128]{3,2,1,0:T(8,128)S(1)}, f32[64,5,8,128]{3,2,1,0:T(8,128)S(1)}, f32[2,384,384]{2,1,0:T(8,128)S(1)}) custom-call(s32[16]{0:T(128)S(1)} %reshape.143.starts_ref, s32[1]{0:T(128)} %bitcast.core_ref, f32[1]{0:T(128)} %bitcast.2.step_ref, f32[2,384,384]{2,1,0:T(8,128)S(1)} %pad_maximum_fusion.ext_ref, f32[8,256,256]{2,1,0:T(8,128)S(1)} %bitcast.15, ...), custom_call_target="tpu_custom_call" | custom-call | flops 17179869184 | bytes 8388608 | tf_op jit(solution)/shard_map/pallas_call | solution.py:408
  55.8 0.1 collective-permute-start.4
  55.9 0.6 collective-permute-start.6
  56.5 0.7 collective-permute-start.5
  57.1 6.3 %collective-permute-done.6 = f32[2,64,384]{2,1,0:T(8,128)S(1)} collective-permute-done((f32[2,64,384]{2,1,0:T(8,128)S(1)}, f32[2,64,384]{2,1,0:T(8,128)S(1)}, u32[]{:S(2)}, u32[]{:S(2)}) %collective-permute-start.6) | collective-permute-done | bytes 196640 | tf_op jit(solution)/shard_map/ppermute | solution.py:455
  63.5 0.8 broadcast_select_fusion.2
  64.3 1.2 add.83
  65.4 16.6 %all-to-all-start = ((f32[64,5,8,128]{3,2,1,0:T(8,128)}), f32[64,5,8,128]{3,2,1,0:T(8,128)S(1)}, u32[]{:S(2)}, u32[]{:S(2)}) async-start(f32[64,5,8,128]{3,2,1,0:T(8,128)} %add.83), calls=%async_computation | async-start | bytes 2621440 | tf_op jit(solution)/shard_map/all_to_all | solution.py:491
  82.1 1.2 slice.134
  83.4 1.0 add_dynamic-update-slice_fusion
  84.4 17.5 %all-to-all-done.spread_ref = f32[64,5,8,128]{3,2,1,0:T(8,128)S(1)} async-done(((f32[64,5,8,128]{3,2,1,0:T(8,128)}), f32[64,5,8,128]{3,2,1,0:T(8,128)S(1)}, u32[]{:S(2)}, u32[]{:S(2)}) %all-to-all-start) | async-done | bytes 1310752 | tf_op jit(solution)/shard_map/all_to_all | solution.py:491
  101.8 1.2 shard_map.105
  103.0 5.3 %all-to-all-start.1 = ((f32[64,4,8,128]{3,2,1,0:T(8,128)}), f32[64,4,8,128]{3,2,1,0:T(8,128)S(1)}, u32[]{:S(2)}, u32[]{:S(2)}) async-start(f32[64,4,8,128]{3,2,1,0:T(8,128)} %shard_map.105), calls=%async_computation.1 | async-start | bytes 2097152 | tf_op jit(solution)/shard_map/all_to_all | solution.py:497
  108.4 0.1 slice_select_fusion.2
  108.5 5.6 %collective-permute-start.7 = (f32[2,256,64]{2,1,0:T(8,128)S(1)}, f32[2,256,64]{2,1,0:T(8,128)S(1)}, u32[]{:S(2)}, u32[]{:S(2)}) collective-permute-start(f32[2,256,64]{2,1,0:T(8,128)S(1)} %get-tuple-element.72), channel_id=1, source_target_pairs={{1,2},{3,4},{5,6},{7,8},{9,10},{11,12},{13,14},{2,1},{4,3},{6,5},{... | collective-permute-start | bytes 393224 | tf_op jit(solution)/shard_map/ppermute | solution.py:458
  114.1 0.1 collective-permute-start.8
  114.2 10.2 %collective-permute-done.7 = f32[2,256,64]{2,1,0:T(8,128)S(1)} collective-permute-done((f32[2,256,64]{2,1,0:T(8,128)S(1)}, f32[2,256,64]{2,1,0:T(8,128)S(1)}, u32[]{:S(2)}, u32[]{:S(2)}) %collective-permute-start.7) | collective-permute-done | bytes 131104 | tf_op jit(solution)/shard_map/ppermute | solution.py:458
  124.5 1.1 scatter-add.16
  125.6 0.1 slice_add_fusion
  125.8 1.2 scatter-add.19
  127.0 0.0 copy-start.9
  127.0 4.0 %collective-permute-start.9 = (f32[64,4,8,128]{3,2,1,0:T(8,128)S(1)}, f32[64,4,8,128]{3,2,1,0:T(8,128)S(1)}, u32[]{:S(2)}, u32[]{:S(2)}) collective-permute-start(f32[64,4,8,128]{3,2,1,0:T(8,128)S(1)} %all-to-all-done.1.source_ref), channel_id=1, source_target_pairs={{0,1},{1,0},{2,3},{3,2},{4,5},{5,4},{6,7},{7,6},{8,9},{9,8},{10,11... | collective-permute-start | bytes 3145736 | tf_op jit(solution)/shard_map/ppermute | solution.py:506
  131.0 1.6 %shard_map.106.refs_0_ = f32[8,256,256]{2,1,0:T(8,128)} custom-call(s32[1]{0:T(128)} %bitcast.8.first_ref, f32[64,4,8,128]{3,2,1,0:T(8,128)S(1)} %all-to-all-done.1.source_ref), custom_call_target="tpu_custom_call" | custom-call | bytes 2097152 | tf_op jit(solution)/shard_map/pallas_call | solution.py:377
  132.6 0.7 collective-permute-done.9.source_ref
  133.3 1.6 %shard_map.107 = f32[8,256,256]{2,1,0:T(8,128)} custom-call(s32[1]{0:T(128)S(6)} %sub.8.first_ref, f32[64,4,8,128]{3,2,1,0:T(8,128)S(1)} %collective-permute-done.9.source_ref, f32[8,256,256]{2,1,0:T(8,128)} %shard_map.106.refs_0_), custom_call_target="tpu_custom_call", output_to_operand_aliasing={{}: (2, {})} | custom-call | bytes 2097152 | tf_op jit(solution)/shard_map/pallas_call | solution.py:377
  (32 shorter events, 0.3 us)
Async XLA Ops:
  0.6 8.2 %copy-start.12 = (s32[8,2]{0,1:T(2,128)S(1)}, s32[8,2]{0,1:T(2,128)}, u32[]{:S(2)}) copy-start(s32[8,2]{0,1:T(2,128)} %param.21) | copy-start | bytes 196
  1.6 12.7 %collective-permute-start = (f32[2,64,256]{2,1,0:T(8,128)S(1)}, f32[2,64,256]{2,1,0:T(8,128)S(1)}, u32[]{:S(2)}, u32[]{:S(2)}) collective-permute-start(f32[2,64,256]{2,1,0:T(8,128)S(1)} %get-tuple-element.66), channel_id=1, source_target_pairs={{16,32},{48,64},{80,96},{32,16},{64,48},{96,80},{17,33},{49,65},{8... | collective-permute-start | bytes 393224 | tf_op jit(solution)/shard_map/ppermute | solution.py:458
  2.3 12.1 %collective-permute-start.1 = (f32[2,64,256]{2,1,0:T(8,128)S(1)}, f32[2,64,256]{2,1,0:T(8,128)S(1)}, u32[]{:S(2)}, u32[]{:S(2)}) collective-permute-start(f32[2,64,256]{2,1,0:T(8,128)S(1)} %broadcast_select_fusion.6), channel_id=1, source_target_pairs={{0,16},{32,48},{64,80},{96,112},{16,0},{48,32},{80,64},{112,96},{1... | collective-permute-start | bytes 393224 | tf_op jit(solution)/shard_map/ppermute | solution.py:455
  12.4 2.0 %copy-start.7 = (f32[256,256]{1,0:T(8,128)S(1)}, f32[256,256]{1,0:T(8,128)}, u32[]{:S(2)}) copy-start(f32[256,256]{1,0:T(8,128)} %param.18) | copy-start | bytes 786436
  12.4 2.0 %copy-start.8 = (f32[256,256]{1,0:T(8,128)S(1)}, f32[256,256]{1,0:T(8,128)}, u32[]{:S(2)}) copy-start(f32[256,256]{1,0:T(8,128)} %param.17) | copy-start | bytes 786436
  14.4 5.7 %copy-start.6 = (f32[8,128,2,256]{3,2,1,0:T(2,128)S(1)}, f32[8,128,2,256]{3,2,1,0:T(2,128)}, u32[]{:S(2)}) copy-start(f32[8,128,2,256]{3,2,1,0:T(2,128)} %reshape.145) | copy-start | bytes 6291460
  15.6 6.1 %collective-permute-start.2 = (f32[2,384,64]{2,1,0:T(8,128)}, f32[2,384,64]{2,1,0:T(8,128)S(1)}, u32[]{:S(2)}, u32[]{:S(2)}) collective-permute-start(f32[2,384,64]{2,1,0:T(8,128)} %get-tuple-element.75), channel_id=1, source_target_pairs={{0,1},{2,3},{4,5},{6,7},{8,9},{10,11},{12,13},{14,15},{1,0},{3,2},... | collective-permute-start | bytes 589832 | tf_op jit(solution)/shard_map/ppermute | solution.py:455
  17.1 9.4 %collective-permute-start.3 = (f32[2,384,64]{2,1,0:T(8,128)}, f32[2,384,64]{2,1,0:T(8,128)}, u32[]{:S(2)}, u32[]{:S(2)}) collective-permute-start(f32[2,384,64]{2,1,0:T(8,128)} %get-tuple-element.76), channel_id=1, source_target_pairs={{1,2},{3,4},{5,6},{7,8},{9,10},{11,12},{13,14},{2,1},{4,3},{6,5},{... | collective-permute-start | bytes 589832 | tf_op jit(solution)/shard_map/ppermute | solution.py:458
  26.5 1.4 %copy-start.3 = (bf16[512,512]{1,0:T(8,128)(2,1)S(1)}, bf16[512,512]{1,0:T(8,128)(2,1)}, u32[]{:S(2)}) copy-start(bf16[512,512]{1,0:T(8,128)(2,1)} %constant.192.clone.col_inv_ref) | copy-start | bytes 1572868
  26.5 1.4 %copy-start.4 = (bf16[2,256,256]{2,1,0:T(8,128)(2,1)S(1)}, bf16[2,256,256]{2,1,0:T(8,128)(2,1)}, u32[]{:S(2)}) copy-start(bf16[2,256,256]{2,1,0:T(8,128)(2,1)} %constant.189.clone.row_fwd_ref) | copy-start | bytes 786436
  26.5 1.4 %copy-start.5 = (bf16[2,256,256]{2,1,0:T(8,128)(2,1)S(1)}, bf16[2,256,256]{2,1,0:T(8,128)(2,1)}, u32[]{:S(2)}) copy-start(bf16[2,256,256]{2,1,0:T(8,128)(2,1)} %constant.191.clone.row_inv_ref) | copy-start | bytes 786436
  27.7 1.6 %copy-start.1 = (f32[8,256,256]{2,1,0:T(8,128)S(1)}, f32[8,256,256]{2,1,0:T(8,128)}, u32[]{:S(2)}) copy-start(f32[8,256,256]{2,1,0:T(8,128)} %amps_ref.1) | copy-start | bytes 6291460
  27.7 1.7 %copy-start.2 = (bf16[512,512]{1,0:T(8,128)(2,1)S(1)}, bf16[512,512]{1,0:T(8,128)(2,1)}, u32[]{:S(2)}) copy-start(bf16[512,512]{1,0:T(8,128)(2,1)} %constant.190.clone.col_fwd_ref) | copy-start | bytes 1572868
  55.8 9.7 %copy-start = (f32[2,384,384]{2,1,0:T(8,128)}, f32[2,384,384]{2,1,0:T(8,128)S(1)}, u32[]{:S(2)}) copy-start(f32[2,384,384]{2,1,0:T(8,128)S(1)} %get-tuple-element.60) | copy-start | bytes 3538948
  55.8 8.5 %collective-permute-start.4 = (f32[64,5,8,128]{3,2,1,0:T(8,128)S(1)}, f32[64,5,8,128]{3,2,1,0:T(8,128)S(1)}, u32[]{:S(2)}, u32[]{:S(2)}) collective-permute-start(f32[64,5,8,128]{3,2,1,0:T(8,128)S(1)} %get-tuple-element.59), channel_id=1, source_target_pairs={{0,1},{1,0},{2,3},{3,2},{4,5},{5,4},{6,7},{7,6},{8,9},{9,8},{10,11... | collective-permute-start | bytes 3932168 | tf_op jit(solution)/shard_map/ppermute | solution.py:488
  55.9 7.6 %collective-permute-start.6 = (f32[2,64,384]{2,1,0:T(8,128)S(1)}, f32[2,64,384]{2,1,0:T(8,128)S(1)}, u32[]{:S(2)}, u32[]{:S(2)}) collective-permute-start(f32[2,64,384]{2,1,0:T(8,128)S(1)} %get-tuple-element.69), channel_id=1, source_target_pairs={{0,16},{32,48},{64,80},{96,112},{16,0},{48,32},{80,64},{112,96},{1... | collective-permute-start | bytes 589832 | tf_op jit(solution)/shard_map/ppermute | solution.py:455
  56.5 7.0 %collective-permute-start.5 = (f32[2,64,384]{2,1,0:T(8,128)S(1)}, f32[2,64,384]{2,1,0:T(8,128)S(1)}, u32[]{:S(2)}, u32[]{:S(2)}) collective-permute-start(f32[2,64,384]{2,1,0:T(8,128)S(1)} %get-tuple-element.70), channel_id=1, source_target_pairs={{16,32},{48,64},{80,96},{32,16},{64,48},{96,80},{17,33},{49,65},{8... | collective-permute-start | bytes 589832 | tf_op jit(solution)/shard_map/ppermute | solution.py:458
  65.4 36.4 %all-to-all-start = ((f32[64,5,8,128]{3,2,1,0:T(8,128)}), f32[64,5,8,128]{3,2,1,0:T(8,128)S(1)}, u32[]{:S(2)}, u32[]{:S(2)}) async-start(f32[64,5,8,128]{3,2,1,0:T(8,128)} %add.83), calls=%async_computation | async-start | bytes 2621440 | tf_op jit(solution)/shard_map/all_to_all | solution.py:491
  82.1 1.3 copy-start.11
  103.0 5.3 %copy-start.10 = (f32[2,64,384]{2,1,0:T(8,128)S(1)}, f32[2,64,384]{2,1,0:T(8,128)}, u32[]{:S(2)}) copy-start(f32[2,64,384]{2,1,0:T(8,128)} %get-tuple-element.63) | copy-start | bytes 589828
  103.0 24.0 %all-to-all-start.1 = ((f32[64,4,8,128]{3,2,1,0:T(8,128)}), f32[64,4,8,128]{3,2,1,0:T(8,128)S(1)}, u32[]{:S(2)}, u32[]{:S(2)}) async-start(f32[64,4,8,128]{3,2,1,0:T(8,128)} %shard_map.105), calls=%async_computation.1 | async-start | bytes 2097152 | tf_op jit(solution)/shard_map/all_to_all | solution.py:497
  108.5 15.9 %collective-permute-start.7 = (f32[2,256,64]{2,1,0:T(8,128)S(1)}, f32[2,256,64]{2,1,0:T(8,128)S(1)}, u32[]{:S(2)}, u32[]{:S(2)}) collective-permute-start(f32[2,256,64]{2,1,0:T(8,128)S(1)} %get-tuple-element.72), channel_id=1, source_target_pairs={{1,2},{3,4},{5,6},{7,8},{9,10},{11,12},{13,14},{2,1},{4,3},{6,5},{... | collective-permute-start | bytes 393224 | tf_op jit(solution)/shard_map/ppermute | solution.py:458
  114.1 10.4 %collective-permute-start.8 = (f32[2,256,64]{2,1,0:T(8,128)S(1)}, f32[2,256,64]{2,1,0:T(8,128)S(1)}, u32[]{:S(2)}, u32[]{:S(2)}) collective-permute-start(f32[2,256,64]{2,1,0:T(8,128)S(1)} %get-tuple-element.71), channel_id=1, source_target_pairs={{0,1},{2,3},{4,5},{6,7},{8,9},{10,11},{12,13},{14,15},{1,0},{3,2},... | collective-permute-start | bytes 393224 | tf_op jit(solution)/shard_map/ppermute | solution.py:455
  127.0 5.6 %copy-start.9 = (f32[2,256,256]{2,1,0:T(8,128)}, f32[2,256,256]{2,1,0:T(8,128)S(1)}, u32[]{:S(2)}) copy-start(f32[2,256,256]{2,1,0:T(8,128)S(1)} %scatter-add.19) | copy-start | bytes 1572868
  127.0 6.3 %collective-permute-start.9 = (f32[64,4,8,128]{3,2,1,0:T(8,128)S(1)}, f32[64,4,8,128]{3,2,1,0:T(8,128)S(1)}, u32[]{:S(2)}, u32[]{:S(2)}) collective-permute-start(f32[64,4,8,128]{3,2,1,0:T(8,128)S(1)} %all-to-all-done.1.source_ref), channel_id=1, source_target_pairs={{0,1},{1,0},{2,3},{3,2},{4,5},{5,4},{6,7},{7,6},{8,9},{9,8},{10,11... | collective-permute-start | bytes 3145736 | tf_op jit(solution)/shard_map/ppermute | solution.py:506

commit v4 on v3

--- a/solution.py
+++ b/solution.py
@@ -459,14 +459,23 @@
     return jnp.where(even, outer, inner), jnp.where(even, inner, outer)
 
 
+def packed(strip):
+    return jnp.concatenate([strip[0], strip[1]], axis=1)
+
+
+def unpacked(pack):
+    width = pack.shape[1] // 2
+    return jnp.stack([pack[:, :width], pack[:, width:]])
+
+
 def shards(object_amplitude, object_phase, probe, amplitudes, positions):
     tile = object_amplitude.shape[0]
     side = probe.shape[2]
     own = jnp.stack([object_amplitude, object_phase])
     top, bottom = exchange(own[:, :H], own[:, tile - H :], ROW)
     tall = jnp.concatenate([top, own, bottom], axis=1)
-    left, right = exchange(tall[:, :, :H], tall[:, :, tile - H :], COL)
-    ext = jnp.concatenate([tall, right, left], axis=2)
+    left, right = exchange(packed(tall[:, :, :H]), packed(tall[:, :, tile - H :]), COL)
+    ext = jnp.concatenate([tall, unpacked(right), unpacked(left)], axis=2)
 
     planes = probe.reshape((-1, side // 2, 2, side)).swapaxes(1, 2).reshape((-1, side, side))
     power = jnp.sum(planes * planes, axis=0)
@@ -498,7 +507,10 @@
     centre = canvas[:, H : H + tile, :]
     centre = centre.at[:, :H].add(from_above)
     centre = centre.at[:, tile - H :].add(from_below)
-    from_left, from_right = exchange(centre[:, :, tile + H :], centre[:, :, tile : tile + H], COL)
+    from_left, from_right = exchange(
+        packed(centre[:, :, tile + H :]), packed(centre[:, :, tile : tile + H]), COL
+    )
+    from_left, from_right = unpacked(from_left), unpacked(from_right)
     inner = centre[:, :, :tile]
     inner = inner.at[:, :, :H].add(from_left)
     inner = inner.at[:, :, tile - H :].add(from_right)

time: 135 us -> 129 us (0.956)
  waiting for transfers between devices: 39.7 us -> 29.7 us
  local copies, waits for them, and re-layouts: 10.6 us -> 13.3 us
    ppermute x4, waiting for transfers between devices: 15.1 us -> 2.66 us  [exchange(): lax.ppermute(jnp.where(even, low, high), axes, gaps + [(j, i) for i, j in...]
    all_to_all x1, waiting for transfers between devices: 0.01 us -> 10.2 us  [shards(): gathered = lax.all_to_all(renew(spread, old), CHIPS, 0, 0, tiled=True)]
    all_to_all x1, waiting for transfers between devices: 17.5 us -> 9.76 us  [shards(): spread = lax.all_to_all(both, CHIPS, 0, 0, tiled=True)]
    ppermute x4, starting transfers between devices: 9.89 us -> 7.4 us  [exchange(): lax.ppermute(jnp.where(even, low, high), axes, gaps + [(j, i) for i, j in...]
    ppermute x4, starting transfers between devices: 8.67 us -> 10.2 us  [exchange(): lax.ppermute(jnp.where(even, high, low), axes, pairs + [(j, i) for i, j i...]
  transfers between devices with their start and end apart: 12 -> 12, of which waited for: 6 -> 6; matrix products, arithmetic and copies ran while one was open for 9% -> 12% of each run, Pallas kernels for 1% -> 2%
where the time goes in v4:
time: 129 us
  starting transfers between devices  44.1 us (34%)
  Pallas kernels  30.8 us (24%)
  waiting for transfers between devices  29.7 us (23%)
  local copies, waits for them, and re-layouts  13.3 us (10%)
  other arithmetic  8.89 us (7%)
  between operations  1.77 us (1%)
    pallas_call x1, Pallas kernels, frames(): pl.pallas_call(frames_kernel, out_shape=(jax.ShapeDtypeStruct((tiles, pla...  26.4 us
    all_to_all x1, starting transfers between devices, shards(): spread = lax.all_to_all(both, CHIPS, 0, 0, tiled=True)  16.5 us
    all_to_all x1, waiting for transfers between devices, shards(): gathered = lax.all_to_all(renew(spread, old), CHIPS, 0, 0, tiled=True)  10.2 us
    ppermute x4, starting transfers between devices, exchange(): lax.ppermute(jnp.where(even, high, low), axes, pairs + [(j, i) for i, j i...  10.2 us
    all_to_all x1, waiting for transfers between devices, shards(): spread = lax.all_to_all(both, CHIPS, 0, 0, tiled=True)  9.76 us
    ppermute x4, starting transfers between devices, exchange(): lax.ppermute(jnp.where(even, low, high), axes, gaps + [(j, i) for i, j in...  7.4 us
    ppermute x4, waiting for transfers between devices, exchange(): lax.ppermute(jnp.where(even, high, low), axes, pairs + [(j, i) for i, j i...  6.43 us
    reshape x2, local copies, waits for them, and re-layouts, shards(): probe.reshape((-1, side // 2, 2, side)).swapaxes(1, 2)  5.33 us
  transfers between devices with their start and end apart: 12, of which 6 were waited for; matrix products, arithmetic and copies ran while one was open for 12% of the time, Pallas kernels for 2%

profile of v4, /device:TPU:1, one launch (start us, length us, event | category | flops | bytes accessed | tf_op | source)
XLA Modules:
  0.0 128.6 jit_solution(17179187553396404553)
XLA Ops:
  0.7 1.0 broadcast_select_fusion.13
  1.6 0.7 collective-permute-start
  2.3 6.5 %collective-permute-start.1 = (f32[2,64,256]{2,1,0:T(8,128)S(1)}, f32[2,64,256]{2,1,0:T(8,128)S(1)}, u32[]{:S(2)}, u32[]{:S(2)}) collective-permute-start(f32[2,64,256]{2,1,0:T(8,128)S(1)} %broadcast_select_fusion.12), channel_id=1, source_target_pairs={{0,16},{32,48},{64,80},{96,112},{16,0},{48,32},{80,64},{112,96},{1... | collective-permute-start | bytes 393224 | tf_op jit(solution)/shard_map/ppermute | solution.py:455
  8.9 0.1 reshape.143.starts_ref
  9.0 3.4 %reshape.145 = f32[8,128,2,256]{3,2,1,0:T(2,128)} reshape(f32[4,2,256,256]{3,2,1,0:T(8,128)} %param.19) | data formatting | bytes 4194304 | tf_op jit(solution)/shard_map/reshape | solution.py:480
  12.4 1.9 %copy.15 = f32[8,128,2,256]{3,1,2,0:T(8,128)S(1)} copy(f32[8,128,2,256]{3,2,1,0:T(2,128)} %reshape.145) | data formatting | bytes 4194304 | tf_op jit(solution)/shard_map/reshape | solution.py:480
  14.5 0.2 slice_bitcast_fusion.7
  14.7 0.9 broadcast_select_fusion.5
  15.6 1.5 %collective-permute-start.2 = (f32[384,128]{1,0:T(8,128)}, f32[384,128]{1,0:T(8,128)S(1)}, u32[]{:S(2)}, u32[]{:S(2)}) collective-permute-start(f32[384,128]{1,0:T(8,128)} %get-tuple-element.75), channel_id=1, source_target_pairs={{0,1},{2,3},{4,5},{6,7},{8,9},{10,11},{12,13},{14,15},{1,0},{3,2},... | collective-permute-start | bytes 589832 | tf_op jit(solution)/shard_map/ppermute | solution.py:455
  17.1 3.0 %collective-permute-start.3 = (f32[384,128]{1,0:T(8,128)}, f32[384,128]{1,0:T(8,128)S(1)}, u32[]{:S(2)}, u32[]{:S(2)}) collective-permute-start(f32[384,128]{1,0:T(8,128)} %get-tuple-element.76), channel_id=1, source_target_pairs={{1,2},{3,4},{5,6},{7,8},{9,10},{11,12},{13,14},{2,1},{4,3},{6,5},{... | collective-permute-start | bytes 589832 | tf_op jit(solution)/shard_map/ppermute | solution.py:458
  20.1 0.1 fusion
  20.3 0.7 reduce_max.9
  21.7 2.7 %collective-permute-done.3 = f32[384,128]{1,0:T(8,128)S(1)} collective-permute-done((f32[384,128]{1,0:T(8,128)}, f32[384,128]{1,0:T(8,128)S(1)}, u32[]{:S(2)}, u32[]{:S(2)}) %collective-permute-start.3) | collective-permute-done | bytes 196640 | tf_op jit(solution)/shard_map/ppermute | solution.py:458
  24.4 0.2 slice_bitcast_fusion.1
  24.6 0.2 maximum_maximum_fusion.ext_ref
  24.8 0.6 copy-done.3
  25.5 0.8 copy-done.1
  26.4 26.4 %shard_map.104 = (f32[64,5,8,128]{3,2,1,0:T(8,128)S(1)}, f32[64,5,8,128]{3,2,1,0:T(8,128)S(1)}, f32[2,384,384]{2,1,0:T(8,128)S(1)}) custom-call(s32[16]{0:T(128)S(1)} %reshape.143.starts_ref, s32[1]{0:T(128)} %bitcast.core_ref, f32[1]{0:T(128)} %bitcast.2.step_ref, f32[2,384,384]{2,1,0:T(8,128)S(1)} %maximum_maximum_fusion.ext_ref, ...), custom_call_target="tpu_custom_call" | custom-call | flops 17179869184 | bytes 8388608 | tf_op jit(solution)/shard_map/pallas_call | solution.py:408
  52.8 0.1 collective-permute-start.4
  53.0 0.5 collective-permute-start.6
  53.5 0.7 collective-permute-start.5
  54.2 6.4 %collective-permute-done.6 = f32[2,64,384]{2,1,0:T(8,128)S(1)} collective-permute-done((f32[2,64,384]{2,1,0:T(8,128)S(1)}, f32[2,64,384]{2,1,0:T(8,128)S(1)}, u32[]{:S(2)}, u32[]{:S(2)}) %collective-permute-start.6) | collective-permute-done | bytes 196640 | tf_op jit(solution)/shard_map/ppermute | solution.py:455
  60.5 0.8 broadcast_select_fusion
  61.3 1.2 add.83
  62.5 16.5 %all-to-all-start = ((f32[64,5,8,128]{3,2,1,0:T(8,128)}), f32[64,5,8,128]{3,2,1,0:T(8,128)S(1)}, u32[]{:S(2)}, u32[]{:S(2)}) async-start(f32[64,5,8,128]{3,2,1,0:T(8,128)} %add.83), calls=%async_computation | async-start | bytes 2621440 | tf_op jit(solution)/shard_map/all_to_all | solution.py:500
  79.0 1.2 slice.188
  80.3 1.0 add_dynamic-update-slice_fusion
  81.3 0.9 copy-done.7
  82.2 0.1 slice_bitcast_fusion.15
  82.3 0.8 broadcast_select_fusion.8
  83.2 1.6 %collective-permute-start.8 = (f32[256,128]{1,0:T(8,128)}, f32[256,128]{1,0:T(8,128)S(1)}, u32[]{:S(2)}, u32[]{:S(2)}) collective-permute-start(f32[256,128]{1,0:T(8,128)} %get-tuple-element.81), channel_id=1, source_target_pairs={{0,1},{2,3},{4,5},{6,7},{8,9},{10,11},{12,13},{14,15},{1,0},{3,2},... | collective-permute-start | bytes 393224 | tf_op jit(solution)/shard_map/ppermute | solution.py:455
  84.8 3.1 %collective-permute-start.7 = (f32[256,128]{1,0:T(8,128)}, f32[256,128]{1,0:T(8,128)}, u32[]{:S(2)}, u32[]{:S(2)}) collective-permute-start(f32[256,128]{1,0:T(8,128)} %get-tuple-element.82), channel_id=1, source_target_pairs={{1,2},{3,4},{5,6},{7,8},{9,10},{11,12},{13,14},{2,1},{4,3},{6,5},{... | collective-permute-start | bytes 393224 | tf_op jit(solution)/shard_map/ppermute | solution.py:458
  88.0 1.1 slice.211
  89.0 9.8 %all-to-all-done.spread_ref = f32[64,5,8,128]{3,2,1,0:T(8,128)S(1)} async-done(((f32[64,5,8,128]{3,2,1,0:T(8,128)}), f32[64,5,8,128]{3,2,1,0:T(8,128)S(1)}, u32[]{:S(2)}, u32[]{:S(2)}) %all-to-all-start) | async-done | bytes 1310752 | tf_op jit(solution)/shard_map/all_to_all | solution.py:500
  98.8 1.2 shard_map.105
  100.0 4.9 %all-to-all-start.1 = ((f32[64,4,8,128]{3,2,1,0:T(8,128)}), f32[64,4,8,128]{3,2,1,0:T(8,128)S(1)}, u32[]{:S(2)}, u32[]{:S(2)}) async-start(f32[64,4,8,128]{3,2,1,0:T(8,128)} %shard_map.105), calls=%async_computation.1 | async-start | bytes 2097152 | tf_op jit(solution)/shard_map/all_to_all | solution.py:506
  104.9 0.9 broadcast_select_fusion.6
  105.9 0.1 slice_bitcast_fusion.11
  106.0 1.0 slice_add_fusion.1
  106.9 1.1 scatter-add.16
  108.1 0.1 slice_bitcast_fusion.9
  108.2 0.1 slice_add_fusion
  108.3 1.2 scatter-add.19
  109.5 10.2 %all-to-all-done.1.source_ref = f32[64,4,8,128]{3,2,1,0:T(8,128)S(1)} async-done(((f32[64,4,8,128]{3,2,1,0:T(8,128)}), f32[64,4,8,128]{3,2,1,0:T(8,128)S(1)}, u32[]{:S(2)}, u32[]{:S(2)}) %all-to-all-start.1) | async-done | bytes 1048608 | tf_op jit(solution)/shard_map/all_to_all | solution.py:506
  119.7 5.0 %collective-permute-start.9 = (f32[64,4,8,128]{3,2,1,0:T(8,128)S(1)}, f32[64,4,8,128]{3,2,1,0:T(8,128)S(1)}, u32[]{:S(2)}, u32[]{:S(2)}) collective-permute-start(f32[64,4,8,128]{3,2,1,0:T(8,128)S(1)} %all-to-all-done.1.source_ref), channel_id=1, source_target_pairs={{0,1},{1,0},{2,3},{3,2},{4,5},{5,4},{6,7},{7,6},{8,9},{9,8},{10,11... | collective-permute-start | bytes 3145736 | tf_op jit(solution)/shard_map/ppermute | solution.py:518
  124.7 1.6 %shard_map.106.refs_0_ = f32[8,256,256]{2,1,0:T(8,128)} custom-call(s32[1]{0:T(128)} %bitcast.24.first_ref, f32[64,4,8,128]{3,2,1,0:T(8,128)S(1)} %all-to-all-done.1.source_ref), custom_call_target="tpu_custom_call" | custom-call | bytes 2097152 | tf_op jit(solution)/shard_map/pallas_call | solution.py:377
  126.3 0.7 collective-permute-done.9.source_ref
  127.0 1.6 %shard_map.107 = f32[8,256,256]{2,1,0:T(8,128)} custom-call(s32[1]{0:T(128)S(6)} %sub.8.first_ref, f32[64,4,8,128]{3,2,1,0:T(8,128)S(1)} %collective-permute-done.9.source_ref, f32[8,256,256]{2,1,0:T(8,128)} %shard_map.106.refs_0_), custom_call_target="tpu_custom_call", output_to_operand_aliasing={{}: (2, {})} | custom-call | bytes 2097152 | tf_op jit(solution)/shard_map/pallas_call | solution.py:377
  (40 shorter events, 0.6 us)
Async XLA Ops:
  0.6 8.2 %copy-start.13 = (s32[8,2]{0,1:T(2,128)S(1)}, s32[8,2]{0,1:T(2,128)}, u32[]{:S(2)}) copy-start(s32[8,2]{0,1:T(2,128)} %param.21) | copy-start | bytes 196
  1.6 12.7 %collective-permute-start = (f32[2,64,256]{2,1,0:T(8,128)S(1)}, f32[2,64,256]{2,1,0:T(8,128)S(1)}, u32[]{:S(2)}, u32[]{:S(2)}) collective-permute-start(f32[2,64,256]{2,1,0:T(8,128)S(1)} %get-tuple-element.66), channel_id=1, source_target_pairs={{16,32},{48,64},{80,96},{32,16},{64,48},{96,80},{17,33},{49,65},{8... | collective-permute-start | bytes 393224 | tf_op jit(solution)/shard_map/ppermute | solution.py:458
  2.3 12.1 %collective-permute-start.1 = (f32[2,64,256]{2,1,0:T(8,128)S(1)}, f32[2,64,256]{2,1,0:T(8,128)S(1)}, u32[]{:S(2)}, u32[]{:S(2)}) collective-permute-start(f32[2,64,256]{2,1,0:T(8,128)S(1)} %broadcast_select_fusion.12), channel_id=1, source_target_pairs={{0,16},{32,48},{64,80},{96,112},{16,0},{48,32},{80,64},{112,96},{1... | collective-permute-start | bytes 393224 | tf_op jit(solution)/shard_map/ppermute | solution.py:455
  12.4 2.0 %copy-start.8 = (f32[256,256]{1,0:T(8,128)S(1)}, f32[256,256]{1,0:T(8,128)}, u32[]{:S(2)}) copy-start(f32[256,256]{1,0:T(8,128)} %param.18) | copy-start | bytes 786436
  12.4 2.0 %copy-start.9 = (f32[256,256]{1,0:T(8,128)S(1)}, f32[256,256]{1,0:T(8,128)}, u32[]{:S(2)}) copy-start(f32[256,256]{1,0:T(8,128)} %param.17) | copy-start | bytes 786436
  14.5 5.6 %copy-start.6 = (f32[8,128,2,256]{3,2,1,0:T(2,128)S(1)}, f32[8,128,2,256]{3,2,1,0:T(2,128)}, u32[]{:S(2)}) copy-start(f32[8,128,2,256]{3,2,1,0:T(2,128)} %reshape.145) | copy-start | bytes 6291460
  15.6 6.1 %collective-permute-start.2 = (f32[384,128]{1,0:T(8,128)}, f32[384,128]{1,0:T(8,128)S(1)}, u32[]{:S(2)}, u32[]{:S(2)}) collective-permute-start(f32[384,128]{1,0:T(8,128)} %get-tuple-element.75), channel_id=1, source_target_pairs={{0,1},{2,3},{4,5},{6,7},{8,9},{10,11},{12,13},{14,15},{1,0},{3,2},... | collective-permute-start | bytes 589832 | tf_op jit(solution)/shard_map/ppermute | solution.py:455
  17.1 7.2 %collective-permute-start.3 = (f32[384,128]{1,0:T(8,128)}, f32[384,128]{1,0:T(8,128)S(1)}, u32[]{:S(2)}, u32[]{:S(2)}) collective-permute-start(f32[384,128]{1,0:T(8,128)} %get-tuple-element.76), channel_id=1, source_target_pairs={{1,2},{3,4},{5,6},{7,8},{9,10},{11,12},{13,14},{2,1},{4,3},{6,5},{... | collective-permute-start | bytes 589832 | tf_op jit(solution)/shard_map/ppermute | solution.py:458
  24.4 1.0 copy-start.3
  24.4 1.1 copy-start.4
  24.4 1.2 copy-start.5
  24.6 1.8 %copy-start.1 = (f32[8,256,256]{2,1,0:T(8,128)S(1)}, f32[8,256,256]{2,1,0:T(8,128)}, u32[]{:S(2)}) copy-start(f32[8,256,256]{2,1,0:T(8,128)} %amps_ref.1) | copy-start | bytes 6291460
  24.6 1.8 %copy-start.2 = (bf16[512,512]{1,0:T(8,128)(2,1)S(1)}, bf16[512,512]{1,0:T(8,128)(2,1)}, u32[]{:S(2)}) copy-start(bf16[512,512]{1,0:T(8,128)(2,1)} %constant.190.clone.col_fwd_ref) | copy-start | bytes 1572868
  52.8 9.7 %copy-start = (f32[2,384,384]{2,1,0:T(8,128)}, f32[2,384,384]{2,1,0:T(8,128)S(1)}, u32[]{:S(2)}) copy-start(f32[2,384,384]{2,1,0:T(8,128)S(1)} %get-tuple-element.60) | copy-start | bytes 3538948
  52.8 8.5 %collective-permute-start.4 = (f32[64,5,8,128]{3,2,1,0:T(8,128)S(1)}, f32[64,5,8,128]{3,2,1,0:T(8,128)S(1)}, u32[]{:S(2)}, u32[]{:S(2)}) collective-permute-start(f32[64,5,8,128]{3,2,1,0:T(8,128)S(1)} %get-tuple-element.59), channel_id=1, source_target_pairs={{0,1},{1,0},{2,3},{3,2},{4,5},{5,4},{6,7},{7,6},{8,9},{9,8},{10,11... | collective-permute-start | bytes 3932168 | tf_op jit(solution)/shard_map/ppermute | solution.py:497
  53.0 7.6 %collective-permute-start.6 = (f32[2,64,384]{2,1,0:T(8,128)S(1)}, f32[2,64,384]{2,1,0:T(8,128)S(1)}, u32[]{:S(2)}, u32[]{:S(2)}) collective-permute-start(f32[2,64,384]{2,1,0:T(8,128)S(1)} %get-tuple-element.69), channel_id=1, source_target_pairs={{0,16},{32,48},{64,80},{96,112},{16,0},{48,32},{80,64},{112,96},{1... | collective-permute-start | bytes 589832 | tf_op jit(solution)/shard_map/ppermute | solution.py:455
  53.5 7.0 %collective-permute-start.5 = (f32[2,64,384]{2,1,0:T(8,128)S(1)}, f32[2,64,384]{2,1,0:T(8,128)S(1)}, u32[]{:S(2)}, u32[]{:S(2)}) collective-permute-start(f32[2,64,384]{2,1,0:T(8,128)S(1)} %get-tuple-element.70), channel_id=1, source_target_pairs={{16,32},{48,64},{80,96},{32,16},{64,48},{96,80},{17,33},{49,65},{8... | collective-permute-start | bytes 589832 | tf_op jit(solution)/shard_map/ppermute | solution.py:458
  62.5 36.3 %all-to-all-start = ((f32[64,5,8,128]{3,2,1,0:T(8,128)}), f32[64,5,8,128]{3,2,1,0:T(8,128)S(1)}, u32[]{:S(2)}, u32[]{:S(2)}) async-start(f32[64,5,8,128]{3,2,1,0:T(8,128)} %add.83), calls=%async_computation | async-start | bytes 2621440 | tf_op jit(solution)/shard_map/all_to_all | solution.py:500
  79.0 1.3 copy-start.12
  79.0 2.2 %copy-start.11 = (f32[2,64,384]{2,1,0:T(8,128)S(1)}, f32[2,64,384]{2,1,0:T(8,128)}, u32[]{:S(2)}) copy-start(f32[2,64,384]{2,1,0:T(8,128)} %get-tuple-element.63) | copy-start | bytes 589828
  81.3 0.9 copy-start.7
  83.2 21.7 %collective-permute-start.8 = (f32[256,128]{1,0:T(8,128)}, f32[256,128]{1,0:T(8,128)S(1)}, u32[]{:S(2)}, u32[]{:S(2)}) collective-permute-start(f32[256,128]{1,0:T(8,128)} %get-tuple-element.81), channel_id=1, source_target_pairs={{0,1},{2,3},{4,5},{6,7},{8,9},{10,11},{12,13},{14,15},{1,0},{3,2},... | collective-permute-start | bytes 393224 | tf_op jit(solution)/shard_map/ppermute | solution.py:455
  84.8 20.1 %collective-permute-start.7 = (f32[256,128]{1,0:T(8,128)}, f32[256,128]{1,0:T(8,128)}, u32[]{:S(2)}, u32[]{:S(2)}) collective-permute-start(f32[256,128]{1,0:T(8,128)} %get-tuple-element.82), channel_id=1, source_target_pairs={{1,2},{3,4},{5,6},{7,8},{9,10},{11,12},{13,14},{2,1},{4,3},{6,5},{... | collective-permute-start | bytes 393224 | tf_op jit(solution)/shard_map/ppermute | solution.py:458
  100.0 19.7 %all-to-all-start.1 = ((f32[64,4,8,128]{3,2,1,0:T(8,128)}), f32[64,4,8,128]{3,2,1,0:T(8,128)S(1)}, u32[]{:S(2)}, u32[]{:S(2)}) async-start(f32[64,4,8,128]{3,2,1,0:T(8,128)} %shard_map.105), calls=%async_computation.1 | async-start | bytes 2097152 | tf_op jit(solution)/shard_map/all_to_all | solution.py:506
  109.5 16.8 %copy-start.10 = (f32[2,256,256]{2,1,0:T(8,128)}, f32[2,256,256]{2,1,0:T(8,128)S(1)}, u32[]{:S(2)}) copy-start(f32[2,256,256]{2,1,0:T(8,128)S(1)} %scatter-add.19) | copy-start | bytes 1572868
  119.7 7.3 %collective-permute-start.9 = (f32[64,4,8,128]{3,2,1,0:T(8,128)S(1)}, f32[64,4,8,128]{3,2,1,0:T(8,128)S(1)}, u32[]{:S(2)}, u32[]{:S(2)}) collective-permute-start(f32[64,4,8,128]{3,2,1,0:T(8,128)S(1)} %all-to-all-done.1.source_ref), channel_id=1, source_target_pairs={{0,1},{1,0},{2,3},{3,2},{4,5},{5,4},{6,7},{7,6},{8,9},{9,8},{10,11... | collective-permute-start | bytes 3145736 | tf_op jit(solution)/shard_map/ppermute | solution.py:518

commit v5 on v4

--- a/solution.py
+++ b/solution.py
@@ -14,7 +14,7 @@
 COL = ("yl", "x", "c")
 CHIPS = ("z", "yh", "yl", "x")
 ALL = CHIPS + ("c",)
-CHUNK = 16
+CHUNK = 32
 PATCH = 64
 GROUP = 64
 

time: 129 us -> 129 us (level)
  no operation moved by 1% of the time
where the time goes in v5:
time: 129 us
  starting transfers between devices  44.3 us (34%)
  Pallas kernels  30.5 us (24%)
  waiting for transfers between devices  29.7 us (23%)
  local copies, waits for them, and re-layouts  13.3 us (10%)
  other arithmetic  8.89 us (7%)
  between operations  1.77 us (1%)
    pallas_call x1, Pallas kernels, frames(): pl.pallas_call(frames_kernel, out_shape=(jax.ShapeDtypeStruct((tiles, pla...  26.2 us
    all_to_all x1, starting transfers between devices, shards(): spread = lax.all_to_all(both, CHIPS, 0, 0, tiled=True)  16.7 us
    ppermute x4, starting transfers between devices, exchange(): lax.ppermute(jnp.where(even, high, low), axes, pairs + [(j, i) for i, j i...  10.2 us
    all_to_all x1, waiting for transfers between devices, shards(): gathered = lax.all_to_all(renew(spread, old), CHIPS, 0, 0, tiled=True)  10.2 us
    all_to_all x1, waiting for transfers between devices, shards(): spread = lax.all_to_all(both, CHIPS, 0, 0, tiled=True)  9.76 us
    ppermute x4, starting transfers between devices, exchange(): lax.ppermute(jnp.where(even, low, high), axes, gaps + [(j, i) for i, j in...  7.4 us
    ppermute x4, waiting for transfers between devices, exchange(): lax.ppermute(jnp.where(even, high, low), axes, pairs + [(j, i) for i, j i...  6.4 us
    reshape x2, local copies, waits for them, and re-layouts, shards(): probe.reshape((-1, side // 2, 2, side)).swapaxes(1, 2)  5.33 us
  transfers between devices with their start and end apart: 12, of which 6 were waited for; matrix products, arithmetic and copies ran while one was open for 12% of the time, Pallas kernels for 2%

profile of v5, /device:TPU:1, one launch (start us, length us, event | category | flops | bytes accessed | tf_op | source)
XLA Modules:
  0.0 128.5 jit_solution(15291437484944634726)
XLA Ops:
  0.7 1.0 broadcast_select_fusion.13
  1.6 0.7 collective-permute-start
  2.3 6.5 %collective-permute-start.1 = (f32[2,64,256]{2,1,0:T(8,128)S(1)}, f32[2,64,256]{2,1,0:T(8,128)S(1)}, u32[]{:S(2)}, u32[]{:S(2)}) collective-permute-start(f32[2,64,256]{2,1,0:T(8,128)S(1)} %broadcast_select_fusion.12), channel_id=1, source_target_pairs={{0,16},{32,48},{64,80},{96,112},{16,0},{48,32},{80,64},{112,96},{1... | collective-permute-start | bytes 393224 | tf_op jit(solution)/shard_map/ppermute | solution.py:455
  8.9 0.1 reshape.143.starts_ref
  9.0 3.4 %reshape.145 = f32[8,128,2,256]{3,2,1,0:T(2,128)} reshape(f32[4,2,256,256]{3,2,1,0:T(8,128)} %param.19) | data formatting | bytes 4194304 | tf_op jit(solution)/shard_map/reshape | solution.py:480
  12.4 1.9 %copy.15 = f32[8,128,2,256]{3,1,2,0:T(8,128)S(1)} copy(f32[8,128,2,256]{3,2,1,0:T(2,128)} %reshape.145) | data formatting | bytes 4194304 | tf_op jit(solution)/shard_map/reshape | solution.py:480
  14.5 0.2 slice_bitcast_fusion.7
  14.7 0.9 broadcast_select_fusion.5
  15.6 1.5 %collective-permute-start.2 = (f32[384,128]{1,0:T(8,128)}, f32[384,128]{1,0:T(8,128)S(1)}, u32[]{:S(2)}, u32[]{:S(2)}) collective-permute-start(f32[384,128]{1,0:T(8,128)} %get-tuple-element.75), channel_id=1, source_target_pairs={{0,1},{2,3},{4,5},{6,7},{8,9},{10,11},{12,13},{14,15},{1,0},{3,2},... | collective-permute-start | bytes 589832 | tf_op jit(solution)/shard_map/ppermute | solution.py:455
  17.1 3.0 %collective-permute-start.3 = (f32[384,128]{1,0:T(8,128)}, f32[384,128]{1,0:T(8,128)S(1)}, u32[]{:S(2)}, u32[]{:S(2)}) collective-permute-start(f32[384,128]{1,0:T(8,128)} %get-tuple-element.76), channel_id=1, source_target_pairs={{1,2},{3,4},{5,6},{7,8},{9,10},{11,12},{13,14},{2,1},{4,3},{6,5},{... | collective-permute-start | bytes 589832 | tf_op jit(solution)/shard_map/ppermute | solution.py:458
  20.1 0.1 fusion
  20.3 0.7 reduce_max.9
  21.7 2.7 %collective-permute-done.3 = f32[384,128]{1,0:T(8,128)S(1)} collective-permute-done((f32[384,128]{1,0:T(8,128)}, f32[384,128]{1,0:T(8,128)S(1)}, u32[]{:S(2)}, u32[]{:S(2)}) %collective-permute-start.3) | collective-permute-done | bytes 196640 | tf_op jit(solution)/shard_map/ppermute | solution.py:458
  24.4 0.2 slice_bitcast_fusion.1
  24.6 0.2 maximum_maximum_fusion.ext_ref
  24.8 0.6 copy-done.3
  25.5 0.8 copy-done.1
  26.4 26.2 %shard_map.104 = (f32[64,5,8,128]{3,2,1,0:T(8,128)S(1)}, f32[64,5,8,128]{3,2,1,0:T(8,128)S(1)}, f32[2,384,384]{2,1,0:T(8,128)S(1)}) custom-call(s32[16]{0:T(128)S(1)} %reshape.143.starts_ref, s32[1]{0:T(128)} %bitcast.core_ref, f32[1]{0:T(128)} %bitcast.2.step_ref, f32[2,384,384]{2,1,0:T(8,128)S(1)} %maximum_maximum_fusion.ext_ref, ...), custom_call_target="tpu_custom_call" | custom-call | flops 17179869184 | bytes 8388608 | tf_op jit(solution)/shard_map/pallas_call | solution.py:408
  52.6 0.1 collective-permute-start.4
  52.7 0.6 collective-permute-start.6
  53.3 0.7 collective-permute-start.5
  53.9 6.3 %collective-permute-done.6 = f32[2,64,384]{2,1,0:T(8,128)S(1)} collective-permute-done((f32[2,64,384]{2,1,0:T(8,128)S(1)}, f32[2,64,384]{2,1,0:T(8,128)S(1)}, u32[]{:S(2)}, u32[]{:S(2)}) %collective-permute-start.6) | collective-permute-done | bytes 196640 | tf_op jit(solution)/shard_map/ppermute | solution.py:455
  60.3 0.8 broadcast_select_fusion
  61.0 1.2 add.83
  62.2 16.7 %all-to-all-start = ((f32[64,5,8,128]{3,2,1,0:T(8,128)}), f32[64,5,8,128]{3,2,1,0:T(8,128)S(1)}, u32[]{:S(2)}, u32[]{:S(2)}) async-start(f32[64,5,8,128]{3,2,1,0:T(8,128)} %add.83), calls=%async_computation | async-start | bytes 2621440 | tf_op jit(solution)/shard_map/all_to_all | solution.py:500
  78.9 1.2 slice.188
  80.2 1.0 add_dynamic-update-slice_fusion
  81.2 0.9 copy-done.7
  82.1 0.1 slice_bitcast_fusion.15
  82.2 0.8 broadcast_select_fusion.8
  83.1 1.6 %collective-permute-start.8 = (f32[256,128]{1,0:T(8,128)}, f32[256,128]{1,0:T(8,128)S(1)}, u32[]{:S(2)}, u32[]{:S(2)}) collective-permute-start(f32[256,128]{1,0:T(8,128)} %get-tuple-element.81), channel_id=1, source_target_pairs={{0,1},{2,3},{4,5},{6,7},{8,9},{10,11},{12,13},{14,15},{1,0},{3,2},... | collective-permute-start | bytes 393224 | tf_op jit(solution)/shard_map/ppermute | solution.py:455
  84.7 3.1 %collective-permute-start.7 = (f32[256,128]{1,0:T(8,128)}, f32[256,128]{1,0:T(8,128)}, u32[]{:S(2)}, u32[]{:S(2)}) collective-permute-start(f32[256,128]{1,0:T(8,128)} %get-tuple-element.82), channel_id=1, source_target_pairs={{1,2},{3,4},{5,6},{7,8},{9,10},{11,12},{13,14},{2,1},{4,3},{6,5},{... | collective-permute-start | bytes 393224 | tf_op jit(solution)/shard_map/ppermute | solution.py:458
  87.8 1.1 slice.211
  88.9 9.8 %all-to-all-done.spread_ref = f32[64,5,8,128]{3,2,1,0:T(8,128)S(1)} async-done(((f32[64,5,8,128]{3,2,1,0:T(8,128)}), f32[64,5,8,128]{3,2,1,0:T(8,128)S(1)}, u32[]{:S(2)}, u32[]{:S(2)}) %all-to-all-start) | async-done | bytes 1310752 | tf_op jit(solution)/shard_map/all_to_all | solution.py:500
  98.7 1.2 shard_map.105
  99.9 4.9 %all-to-all-start.1 = ((f32[64,4,8,128]{3,2,1,0:T(8,128)}), f32[64,4,8,128]{3,2,1,0:T(8,128)S(1)}, u32[]{:S(2)}, u32[]{:S(2)}) async-start(f32[64,4,8,128]{3,2,1,0:T(8,128)} %shard_map.105), calls=%async_computation.1 | async-start | bytes 2097152 | tf_op jit(solution)/shard_map/all_to_all | solution.py:506
  104.8 0.9 broadcast_select_fusion.6
  105.7 0.1 slice_bitcast_fusion.11
  105.8 1.0 slice_add_fusion.1
  106.8 1.1 scatter-add.16
  108.0 0.1 slice_bitcast_fusion.9
  108.0 0.1 slice_add_fusion
  108.2 1.2 scatter-add.19
  109.4 10.2 %all-to-all-done.1.source_ref = f32[64,4,8,128]{3,2,1,0:T(8,128)S(1)} async-done(((f32[64,4,8,128]{3,2,1,0:T(8,128)}), f32[64,4,8,128]{3,2,1,0:T(8,128)S(1)}, u32[]{:S(2)}, u32[]{:S(2)}) %all-to-all-start.1) | async-done | bytes 1048608 | tf_op jit(solution)/shard_map/all_to_all | solution.py:506
  119.6 5.0 %collective-permute-start.9 = (f32[64,4,8,128]{3,2,1,0:T(8,128)S(1)}, f32[64,4,8,128]{3,2,1,0:T(8,128)S(1)}, u32[]{:S(2)}, u32[]{:S(2)}) collective-permute-start(f32[64,4,8,128]{3,2,1,0:T(8,128)S(1)} %all-to-all-done.1.source_ref), channel_id=1, source_target_pairs={{0,1},{1,0},{2,3},{3,2},{4,5},{5,4},{6,7},{7,6},{8,9},{9,8},{10,11... | collective-permute-start | bytes 3145736 | tf_op jit(solution)/shard_map/ppermute | solution.py:518
  124.6 1.6 %shard_map.106.refs_0_ = f32[8,256,256]{2,1,0:T(8,128)} custom-call(s32[1]{0:T(128)} %bitcast.24.first_ref, f32[64,4,8,128]{3,2,1,0:T(8,128)S(1)} %all-to-all-done.1.source_ref), custom_call_target="tpu_custom_call" | custom-call | bytes 2097152 | tf_op jit(solution)/shard_map/pallas_call | solution.py:377
  126.2 0.7 collective-permute-done.9.source_ref
  126.9 1.6 %shard_map.107 = f32[8,256,256]{2,1,0:T(8,128)} custom-call(s32[1]{0:T(128)S(6)} %sub.8.first_ref, f32[64,4,8,128]{3,2,1,0:T(8,128)S(1)} %collective-permute-done.9.source_ref, f32[8,256,256]{2,1,0:T(8,128)} %shard_map.106.refs_0_), custom_call_target="tpu_custom_call", output_to_operand_aliasing={{}: (2, {})} | custom-call | bytes 2097152 | tf_op jit(solution)/shard_map/pallas_call | solution.py:377
  (40 shorter events, 0.6 us)
Async XLA Ops:
  0.6 8.2 %copy-start.13 = (s32[8,2]{0,1:T(2,128)S(1)}, s32[8,2]{0,1:T(2,128)}, u32[]{:S(2)}) copy-start(s32[8,2]{0,1:T(2,128)} %param.21) | copy-start | bytes 196
  1.6 12.7 %collective-permute-start = (f32[2,64,256]{2,1,0:T(8,128)S(1)}, f32[2,64,256]{2,1,0:T(8,128)S(1)}, u32[]{:S(2)}, u32[]{:S(2)}) collective-permute-start(f32[2,64,256]{2,1,0:T(8,128)S(1)} %get-tuple-element.66), channel_id=1, source_target_pairs={{16,32},{48,64},{80,96},{32,16},{64,48},{96,80},{17,33},{49,65},{8... | collective-permute-start | bytes 393224 | tf_op jit(solution)/shard_map/ppermute | solution.py:458
  2.3 12.1 %collective-permute-start.1 = (f32[2,64,256]{2,1,0:T(8,128)S(1)}, f32[2,64,256]{2,1,0:T(8,128)S(1)}, u32[]{:S(2)}, u32[]{:S(2)}) collective-permute-start(f32[2,64,256]{2,1,0:T(8,128)S(1)} %broadcast_select_fusion.12), channel_id=1, source_target_pairs={{0,16},{32,48},{64,80},{96,112},{16,0},{48,32},{80,64},{112,96},{1... | collective-permute-start | bytes 393224 | tf_op jit(solution)/shard_map/ppermute | solution.py:455
  12.4 2.0 %copy-start.8 = (f32[256,256]{1,0:T(8,128)S(1)}, f32[256,256]{1,0:T(8,128)}, u32[]{:S(2)}) copy-start(f32[256,256]{1,0:T(8,128)} %param.18) | copy-start | bytes 786436
  12.4 2.0 %copy-start.9 = (f32[256,256]{1,0:T(8,128)S(1)}, f32[256,256]{1,0:T(8,128)}, u32[]{:S(2)}) copy-start(f32[256,256]{1,0:T(8,128)} %param.17) | copy-start | bytes 786436
  14.5 5.6 %copy-start.6 = (f32[8,128,2,256]{3,2,1,0:T(2,128)S(1)}, f32[8,128,2,256]{3,2,1,0:T(2,128)}, u32[]{:S(2)}) copy-start(f32[8,128,2,256]{3,2,1,0:T(2,128)} %reshape.145) | copy-start | bytes 6291460
  15.6 6.1 %collective-permute-start.2 = (f32[384,128]{1,0:T(8,128)}, f32[384,128]{1,0:T(8,128)S(1)}, u32[]{:S(2)}, u32[]{:S(2)}) collective-permute-start(f32[384,128]{1,0:T(8,128)} %get-tuple-element.75), channel_id=1, source_target_pairs={{0,1},{2,3},{4,5},{6,7},{8,9},{10,11},{12,13},{14,15},{1,0},{3,2},... | collective-permute-start | bytes 589832 | tf_op jit(solution)/shard_map/ppermute | solution.py:455
  17.1 7.2 %collective-permute-start.3 = (f32[384,128]{1,0:T(8,128)}, f32[384,128]{1,0:T(8,128)S(1)}, u32[]{:S(2)}, u32[]{:S(2)}) collective-permute-start(f32[384,128]{1,0:T(8,128)} %get-tuple-element.76), channel_id=1, source_target_pairs={{1,2},{3,4},{5,6},{7,8},{9,10},{11,12},{13,14},{2,1},{4,3},{6,5},{... | collective-permute-start | bytes 589832 | tf_op jit(solution)/shard_map/ppermute | solution.py:458
  24.4 1.0 copy-start.3
  24.4 1.1 copy-start.4
  24.4 1.2 copy-start.5
  24.6 1.8 %copy-start.1 = (f32[8,256,256]{2,1,0:T(8,128)S(1)}, f32[8,256,256]{2,1,0:T(8,128)}, u32[]{:S(2)}) copy-start(f32[8,256,256]{2,1,0:T(8,128)} %amps_ref.1) | copy-start | bytes 6291460
  24.6 1.8 %copy-start.2 = (bf16[512,512]{1,0:T(8,128)(2,1)S(1)}, bf16[512,512]{1,0:T(8,128)(2,1)}, u32[]{:S(2)}) copy-start(bf16[512,512]{1,0:T(8,128)(2,1)} %constant.190.clone.col_fwd_ref) | copy-start | bytes 1572868
  52.6 9.7 %copy-start = (f32[2,384,384]{2,1,0:T(8,128)}, f32[2,384,384]{2,1,0:T(8,128)S(1)}, u32[]{:S(2)}) copy-start(f32[2,384,384]{2,1,0:T(8,128)S(1)} %get-tuple-element.60) | copy-start | bytes 3538948
  52.6 8.5 %collective-permute-start.4 = (f32[64,5,8,128]{3,2,1,0:T(8,128)S(1)}, f32[64,5,8,128]{3,2,1,0:T(8,128)S(1)}, u32[]{:S(2)}, u32[]{:S(2)}) collective-permute-start(f32[64,5,8,128]{3,2,1,0:T(8,128)S(1)} %get-tuple-element.59), channel_id=1, source_target_pairs={{0,1},{1,0},{2,3},{3,2},{4,5},{5,4},{6,7},{7,6},{8,9},{9,8},{10,11... | collective-permute-start | bytes 3932168 | tf_op jit(solution)/shard_map/ppermute | solution.py:497
  52.7 7.6 %collective-permute-start.6 = (f32[2,64,384]{2,1,0:T(8,128)S(1)}, f32[2,64,384]{2,1,0:T(8,128)S(1)}, u32[]{:S(2)}, u32[]{:S(2)}) collective-permute-start(f32[2,64,384]{2,1,0:T(8,128)S(1)} %get-tuple-element.69), channel_id=1, source_target_pairs={{0,16},{32,48},{64,80},{96,112},{16,0},{48,32},{80,64},{112,96},{1... | collective-permute-start | bytes 589832 | tf_op jit(solution)/shard_map/ppermute | solution.py:455
  53.3 7.0 %collective-permute-start.5 = (f32[2,64,384]{2,1,0:T(8,128)S(1)}, f32[2,64,384]{2,1,0:T(8,128)S(1)}, u32[]{:S(2)}, u32[]{:S(2)}) collective-permute-start(f32[2,64,384]{2,1,0:T(8,128)S(1)} %get-tuple-element.70), channel_id=1, source_target_pairs={{16,32},{48,64},{80,96},{32,16},{64,48},{96,80},{17,33},{49,65},{8... | collective-permute-start | bytes 589832 | tf_op jit(solution)/shard_map/ppermute | solution.py:458
  62.2 36.4 %all-to-all-start = ((f32[64,5,8,128]{3,2,1,0:T(8,128)}), f32[64,5,8,128]{3,2,1,0:T(8,128)S(1)}, u32[]{:S(2)}, u32[]{:S(2)}) async-start(f32[64,5,8,128]{3,2,1,0:T(8,128)} %add.83), calls=%async_computation | async-start | bytes 2621440 | tf_op jit(solution)/shard_map/all_to_all | solution.py:500
  78.9 1.3 copy-start.12
  78.9 2.2 %copy-start.11 = (f32[2,64,384]{2,1,0:T(8,128)S(1)}, f32[2,64,384]{2,1,0:T(8,128)}, u32[]{:S(2)}) copy-start(f32[2,64,384]{2,1,0:T(8,128)} %get-tuple-element.63) | copy-start | bytes 589828
  81.2 0.9 copy-start.7
  83.1 21.7 %collective-permute-start.8 = (f32[256,128]{1,0:T(8,128)}, f32[256,128]{1,0:T(8,128)S(1)}, u32[]{:S(2)}, u32[]{:S(2)}) collective-permute-start(f32[256,128]{1,0:T(8,128)} %get-tuple-element.81), channel_id=1, source_target_pairs={{0,1},{2,3},{4,5},{6,7},{8,9},{10,11},{12,13},{14,15},{1,0},{3,2},... | collective-permute-start | bytes 393224 | tf_op jit(solution)/shard_map/ppermute | solution.py:455
  84.7 20.1 %collective-permute-start.7 = (f32[256,128]{1,0:T(8,128)}, f32[256,128]{1,0:T(8,128)}, u32[]{:S(2)}, u32[]{:S(2)}) collective-permute-start(f32[256,128]{1,0:T(8,128)} %get-tuple-element.82), channel_id=1, source_target_pairs={{1,2},{3,4},{5,6},{7,8},{9,10},{11,12},{13,14},{2,1},{4,3},{6,5},{... | collective-permute-start | bytes 393224 | tf_op jit(solution)/shard_map/ppermute | solution.py:458
  99.9 19.7 %all-to-all-start.1 = ((f32[64,4,8,128]{3,2,1,0:T(8,128)}), f32[64,4,8,128]{3,2,1,0:T(8,128)S(1)}, u32[]{:S(2)}, u32[]{:S(2)}) async-start(f32[64,4,8,128]{3,2,1,0:T(8,128)} %shard_map.105), calls=%async_computation.1 | async-start | bytes 2097152 | tf_op jit(solution)/shard_map/all_to_all | solution.py:506
  109.4 16.8 %copy-start.10 = (f32[2,256,256]{2,1,0:T(8,128)}, f32[2,256,256]{2,1,0:T(8,128)S(1)}, u32[]{:S(2)}) copy-start(f32[2,256,256]{2,1,0:T(8,128)S(1)} %scatter-add.19) | copy-start | bytes 1572868
  119.6 7.3 %collective-permute-start.9 = (f32[64,4,8,128]{3,2,1,0:T(8,128)S(1)}, f32[64,4,8,128]{3,2,1,0:T(8,128)S(1)}, u32[]{:S(2)}, u32[]{:S(2)}) collective-permute-start(f32[64,4,8,128]{3,2,1,0:T(8,128)S(1)} %all-to-all-done.1.source_ref), channel_id=1, source_target_pairs={{0,1},{1,0},{2,3},{3,2},{4,5},{5,4},{6,7},{7,6},{8,9},{9,8},{10,11... | collective-permute-start | bytes 3145736 | tf_op jit(solution)/shard_map/ppermute | solution.py:518
